TPU v7x, 256 devices: a whole 4x4x8 slice. The times are simulated.
256 devices in a mesh: gx: 8 (over y, core), gy: 32 (over z, x).
Axes of the slice: x: 4, y: 4, z: 8, core: 2. Of those that a mesh axis runs over, the one named last changes fastest.
Arguments:
- tracer_adjoint: float32 [2, 50, 1280, 1024], P(None, None, 'gy', 'gx'), may hold values from -6 to 6
- surface_adjoint: float32 [1280, 1024], P('gy', 'gx'), may hold values from -6 to 6
- flow_east: float32 [50, 1280, 1024], P(None, 'gy', 'gx'), may hold values from -0.4 to 0.4, as said below
- flow_north: float32 [50, 1280, 1024], P(None, 'gy', 'gx'), may hold values from -0.4 to 0.4, as said below
- vertical_mix: float32 [49, 1280, 1024], P(None, 'gy', 'gx'), may hold values from 0.1 to 10
- land_mask: int32 [50, 1280, 1024], P(None, 'gy', 'gx'), may hold values from 0 to 1, as said below
- conduct_east: float32 [1280, 1024], P('gy', 'gx'), may hold values from 0 to 4, as said below
- conduct_north: float32 [1280, 1024], P('gy', 'gx'), may hold values from 0 to 4, as said below
- surface_diagonal: float32 [1280, 1024], P('gy', 'gx'), may hold values from 0.02 to 0.2
- pressure_load: float32 [2, 50], replicated, may hold values from -0.5 to 0.5
- surface_forcing: float32 [2, 50], replicated, may hold values from -0.1 to 0.1
- control_map: int32 [4608], replicated, may hold values from 0 to 2559
- control_weight: float32 [4608], replicated, may hold values from 0.5 to 1.5
Outputs:
- tracer_grad: float32 [2, 50, 1280, 1024], P(None, None, 'gy', 'gx')
- surface_grad: float32 [1280, 1024], P('gy', 'gx')
- control_grad: float32 [2, 50, 2560], P(None, None, ('gx', 'gy'))
Inputs may be any that keep to these rules, and one draw needn't show every extreme that they name: `land_mask`: 1 marks an ocean cell and 0 land; where a cell is ocean, the cell above it is ocean too. `flow_east`: zero on every face that touches land or lies on the grid's eastern edge. `flow_north`: zero on every face that touches land or lies on the grid's northern edge. `conduct_east`: zero on faces that touch land at the surface or lie on the eastern edge, positive elsewhere. `conduct_north`: zero on faces that touch land at the surface or lie on the northern edge, positive elsewhere.
All inputs are finite; a program needn't handle non-finite values.
Results may differ from a plain program's by a relative error of at most 0.0003.
Values sent between devices are 32-bit elements; how exact they have to be, the bound alone decides.
No kernel may reach another device: no remote copies, remote signals or barrier semaphores. Data moves between devices by JAX's collectives and lax.ppermute only.
A program may use at most 128 MiB of HBM per device.

v0:
```python
import jax
import jax.numpy as jnp
from jax import lax
from jax.sharding import PartitionSpec as P

ITERS = 3
CTRL_DEV = 10


def passed_along(value, axis, steps):
    count = lax.axis_size(axis)
    leading, last = (max(0, -steps), min(count, count - steps))
    return lax.ppermute(value, axis, [(source, source + steps) for source in range(leading, last)])


def extended(shard, sides, width):
    for axis, dim in sides:
        peers, length = (lax.axis_size(axis), shard.shape[dim])
        up = [(i, (i + 1) % peers) for i in range(peers - 1)]
        down = [(j, i) for i, j in up]
        last = lax.slice_in_dim(shard, length - width, length, axis=dim)
        leading = lax.slice_in_dim(shard, 0, width, axis=dim)
        before = lax.ppermute(last, axis, up)
        after = lax.ppermute(leading, axis, down)
        shard = jnp.concatenate([before, shard, after], axis=dim)
    return shard


def column_solve(right_side, kappa_vert):
    levels = right_side.shape[-3]
    ratios = []
    reduced = []
    for level in range(levels):
        diag_term = 1.0
        if level > 0:
            diag_term = diag_term + kappa_vert[level - 1]
        if level < levels - 1:
            diag_term = diag_term + kappa_vert[level]
        if level == 0:
            pivot_val = diag_term
            carried = right_side[..., 0, :, :]
        else:
            pivot_val = diag_term - kappa_vert[level - 1] * ratios[level - 1]
            carried = right_side[..., level, :, :] + kappa_vert[level - 1] * reduced[level - 1]
        reduced.append(carried / pivot_val)
        if level < levels - 1:
            ratios.append(kappa_vert[level] / pivot_val)
    solution = [reduced[levels - 1]]
    for level in range(levels - 2, -1, -1):
        solution.insert(0, reduced[level] + ratios[level] * solution[0])
    return jnp.stack(solution, axis=-3)


def squares(remain):
    return lax.psum(jnp.sum(remain * remain), ("gx", "gy"))


def per_device(
    tracer_adjoint,
    surface_adjoint,
    flow_east,
    flow_north,
    vertical_mix,
    land_mask,
    conduct_east,
    conduct_north,
    surface_diagonal,
    pressure_load,
    surface_forcing,
    control_map,
    control_weight,
):
    wet_cells = land_mask.astype(jnp.float32)
    tiles_lon = lax.axis_size("gx")
    tiles_lat = lax.axis_size("gy")
    tile_col = lax.axis_index("gx")
    tile_row = lax.axis_index("gy")
    levels, rows_here, cols_here = flow_east.shape
    west_rim = passed_along(
        jnp.concatenate([flow_east[:, :, -1:], conduct_east[None, :, -1:]], axis=0), "gx", 1
    )
    flow_west = jnp.concatenate([west_rim[:levels], flow_east[:, :, :-1]], axis=2)
    conduct_west = jnp.concatenate([west_rim[levels], conduct_east[:, :-1]], axis=1)
    south_rim = passed_along(
        jnp.concatenate([flow_north[:, -1:, :], conduct_north[None, -1:, :]], axis=0), "gy", 1
    )
    flow_south = jnp.concatenate([south_rim[:levels], flow_north[:, :-1, :]], axis=1)
    conduct_south = jnp.concatenate([south_rim[levels], conduct_north[:-1, :]], axis=0)
    kappa_vert = vertical_mix * wet_cells[1:]
    loads = wet_cells[None] * pressure_load[:, :, None, None]
    forcing_sum = surface_adjoint + jnp.sum(
        surface_forcing[:, :, None, None] * wet_cells[None] * tracer_adjoint, axis=(0, 1)
    )
    iterate = jnp.zeros_like(forcing_sum)
    remain = forcing_sum
    search = remain
    norm_now = squares(remain)
    for iteration in range(ITERS):
        padded = extended(search, (("gx", 1), ("gy", 0)), 1)
        surface_east_side = padded[1:-1, 2:]
        surface_west_side = padded[1:-1, :-2]
        surface_north_side = padded[2:, 1:-1]
        surface_south_side = padded[:-2, 1:-1]
        image = (
            surface_diagonal * search
            + conduct_east * (search - surface_east_side)
            + conduct_west * (search - surface_west_side)
            + conduct_north * (search - surface_north_side)
            + conduct_south * (search - surface_south_side)
        )
        step_len = norm_now / lax.psum(jnp.sum(search * image), ("gx", "gy"))
        iterate = iterate + step_len * search
        remain = remain - step_len * image
        if iteration + 1 < ITERS:
            norm_next = squares(remain)
            search = remain + norm_next / norm_now * search
            norm_now = norm_next
    lifted = tracer_adjoint + loads * iterate[None, None]
    lambda_pad = extended(
        wet_cells[None] * column_solve(lifted, kappa_vert), (("gx", 3), ("gy", 2)), 1
    )
    center = lambda_pad[..., 1:-1, 1:-1]
    east_side = lambda_pad[..., 1:-1, 2:]
    west_side = lambda_pad[..., 1:-1, :-2]
    north_side = lambda_pad[..., 2:, 1:-1]
    south_side = lambda_pad[..., :-2, 1:-1]
    tracer_grad = (
        center
        + 0.5 * flow_east * (east_side - center)
        + 0.5 * flow_west * (center - west_side)
        + 0.5 * flow_north * (north_side - center)
        + 0.5 * flow_south * (center - south_side)
    )
    lon_cells = cols_here * tiles_lon
    lat_cells = rows_here * tiles_lat
    share_len = CTRL_DEV
    control_count = share_len * tiles_lon * tiles_lat
    edge_vals = jnp.concatenate(
        [
            tracer_grad[:, :, 0, :],
            tracer_grad[:, :, -1, :],
            tracer_grad[:, :, :, 0],
            tracer_grad[:, :, :, -1],
        ],
        axis=2,
    )
    begins = [
        tile_col * cols_here,
        lon_cells + tile_col * cols_here,
        2 * lon_cells + tile_row * rows_here,
        2 * lon_cells + lat_cells + tile_row * rows_here,
    ]
    amounts = [cols_here, cols_here, rows_here, rows_here]
    actives = [tile_row == 0, tile_row == tiles_lat - 1, tile_col == 0, tile_col == tiles_lon - 1]
    point_ids = jnp.concatenate(
        [
            lax.dynamic_slice_in_dim(control_map, begin, amount)
            for begin, amount in zip(begins, amounts)
        ]
    )
    point_wts = jnp.concatenate(
        [
            lax.dynamic_slice_in_dim(control_weight, begin, amount) * active.astype(jnp.float32)
            for begin, amount, active in zip(begins, amounts, actives)
        ]
    )
    weighted = (edge_vals * point_wts).reshape(2 * levels, -1)
    onehot = (point_ids[:, None] == jnp.arange(control_count, dtype=jnp.int32)[None, :]).astype(
        jnp.float32
    )
    contribution = jnp.dot(
        weighted, onehot, precision=lax.Precision.HIGHEST, preferred_element_type=jnp.float32
    ).reshape(2, levels, control_count)
    totals = lax.psum(contribution, ("gx", "gy"))
    owner_idx = tile_col * tiles_lat + tile_row
    control_grad = lax.dynamic_slice_in_dim(totals, owner_idx * share_len, share_len, 2)
    return (tracer_grad, iterate, control_grad)


def solution(mesh):
    in_specs = (
        P(None, None, "gy", "gx"),
        P("gy", "gx"),
        P(None, "gy", "gx"),
        P(None, "gy", "gx"),
        P(None, "gy", "gx"),
        P(None, "gy", "gx"),
        P("gy", "gx"),
        P("gy", "gx"),
        P("gy", "gx"),
        P(),
        P(),
        P(),
        P(),
    )
    out_specs = (P(None, None, "gy", "gx"), P("gy", "gx"), P(None, None, ("gx", "gy")))
    return jax.shard_map(
        per_device, mesh=mesh, in_specs=in_specs, out_specs=out_specs, check_vma=False
    )
```

profile of v0, /device:TPU:1, one launch (start us, length us, event | category | flops | bytes accessed | tf_op | source)
XLA Modules:
  0.0 855.4 jit_solution(15033801169506181520)
XLA Ops:
  8.6 4.1 multiply_reduce_fusion
  13.5 5.1 collective-permute-start
  18.6 1.9 collective-permute-start.2
  22.1 1.9 collective-permute-start.1
  25.6 3.6 collective-permute-start.4
  29.3 1.3 slice_multiply_fusion
  49.4 1.5 fusion.182
  50.9 1.5 fusion.184
  52.4 1.4 dynamic-slice_multiply_fusion.3
  53.7 1.5 fusion.181
  57.3 4.0 collective-permute-start.5
  62.8 1.6 multiply_reduce_fusion.4
  64.4 82.7 %all-reduce = (f32[]{:T(128)}, f32[]{:T(128)}) all-reduce(f32[]{:T(128)} %get-tuple-element.13, f32[]{:T(128)} %get-tuple-element.12), channel_id=1, replica_groups=mesh['gx'=8,'gy'=32] {'gx','gy'}, use_global_device_ids=true, to_apply=%region_2.0 | all-reduce | flops 2 | bytes 16 | tf_op jit(solution)/shard_map/psum | solution.py:55
  149.1 74.7 %psum.51 = f32[]{:T(128)} all-reduce(f32[]{:T(128)} %get-tuple-element.159), channel_id=1, replica_groups=mesh['gx'=8,'gy'=32] {'gx','gy'}, use_global_device_ids=true, to_apply=%region_6.0 | all-reduce | flops 1 | bytes 8 | tf_op jit(solution)/shard_map/psum | solution.py:55
  225.2 2.6 collective-permute-start.6
  227.8 3.0 collective-permute-start.7
  233.1 4.0 collective-permute-start.9
  237.8 1.4 multiply_reduce_fusion.2
  239.2 79.1 %psum.52 = f32[]{:T(128)} all-reduce(f32[]{:T(128)} %get-tuple-element.157), channel_id=1, replica_groups=mesh['gx'=8,'gy'=32] {'gx','gy'}, use_global_device_ids=true, to_apply=%region_8.0 | all-reduce | flops 1 | bytes 8 | tf_op jit(solution)/shard_map/psum | solution.py:111
  321.1 74.3 %psum.53 = f32[]{:T(128)} all-reduce(f32[]{:T(128)} %multiply_reduce_fusion.1), channel_id=1, replica_groups=mesh['gx'=8,'gy'=32] {'gx','gy'}, use_global_device_ids=true, to_apply=%region_10.0 | all-reduce | flops 1 | bytes 8 | tf_op jit(solution)/shard_map/psum | solution.py:55
  396.8 2.6 collective-permute-start.10
  399.4 3.0 collective-permute-start.11
  405.2 4.6 collective-permute-start.13
  411.1 1.4 copy.141
  412.4 2.5 copy.200
  416.2 1.4 fusion.102
  417.6 2.3 copy.203
  419.8 76.1 %psum.54 = f32[]{:T(128)} all-reduce(f32[]{:T(128)} %fusion.102), channel_id=1, replica_groups=mesh['gx'=8,'gy'=32] {'gx','gy'}, use_global_device_ids=true, to_apply=%region_12.0 | all-reduce | flops 1 | bytes 8 | tf_op jit(solution)/shard_map/psum | solution.py:111
  497.7 4.0 multiply_add_fusion
  502.2 5.7 add_divide_fusion.3
  508.3 4.7 fusion.21
  513.3 5.0 constant_dynamic-update-slice_fusion.49
  521.8 4.2 fusion.199
  526.0 3.7 copy.201
  529.6 2.6 collective-permute-start.14
  532.2 3.7 copy.205
  535.9 3.0 collective-permute-start.15
  538.9 1.5 maximum_multiply_fusion
  542.5 3.0 copy.202
  545.5 3.1 copy.206
  548.6 1.4 pad_maximum_fusion.10
  551.4 4.0 collective-permute-start.17
  557.9 12.9 %fusion.5 = f32[2,50,40,128]{3,0,1,2:T(2,128)S(1)} fusion(f32[2,50,40,128]{3,0,1,2:T(2,128)S(1)} %broadcast_multiply_fusion, f32[2,50,1,130]{3,0,1,2:T(2,128)S(1)} %collective-permute-done.17, f32[2,50,40,1]{3,0,1,2:T(2,128)S(1)} %copy-done.2, f32[2,50,40,1]{3,0,1,2:T(2,128)S(1)} %copy-done.3, f32[2,50,1,130]{3,0,1,2:T(2,128)S(1)} %collective-permute-done.16, ...), kind=kLoop, calls=%fused_computation.6 | loop fusion | flops 10240000 | bytes 8328000 | tf_op jit(solution)/shard_map/add | solution.py:128
  570.8 3.5 fusion.198
  574.3 3.7 copy.212
  579.7 4.8 fusion.1
  584.5 1.4 copy.217
  586.0 261.0 %all-reduce.3.cloned.1.call-done = f32[2,50,2560]{1,2,0:T(8,128)} async-done(((f32[2,50,2560]{1,2,0:T(8,128)}), f32[2,50,2560]{1,2,0:T(8,128)}) %all-reduce.3.cloned.1.call-update) | async-done | bytes 1024016 | tf_op jit(solution)/shard_map/psum | solution.py:174
  (405 shorter events, 50.2 us)
Async XLA Ops:
  7.2 839.8 %all-reduce.3.cloned.1.call-start = ((), (), s32[]{:S(2)}) async-start(), calls=%async_computation | async-start | bytes 5242880 | tf_op jit(solution)/shard_map/psum | solution.py:174
  8.5 12.0 %copy-start.4 = (f32[50,40,128]{2,1,0:T(8,128)S(1)}, f32[50,40,128]{2,1,0:T(8,128)}, u32[]{:S(2)}) copy-start(f32[50,40,128]{2,1,0:T(8,128)} %param.15) | copy-start | bytes 3072004
  12.7 8.6 %copy-start.12 = (f32[40,128]{1,0:T(8,128)S(1)}, f32[40,128]{1,0:T(8,128)}, u32[]{:S(2)}) copy-start(f32[40,128]{1,0:T(8,128)} %param.19) | copy-start | bytes 61444
  12.7 12.3 %copy-start.13 = (f32[40,128]{1,0:T(8,128)S(1)}, f32[40,128]{1,0:T(8,128)}, u32[]{:S(2)}) copy-start(f32[40,128]{1,0:T(8,128)} %param.20) | copy-start | bytes 61444
  13.5 41.8 %collective-permute-start = (f32[40,1]{1,0:T(8,128)}, f32[40,1]{1,0:T(8,128)}, u32[]{:S(2)}, u32[]{:S(2)}) collective-permute-start(f32[40,1]{1,0:T(8,128)} %get-tuple-element.264), channel_id=1, source_target_pairs={{32,0},{64,32},{96,64},{128,96},{160,128},{192,160},{224,192},{33,... | collective-permute-start | bytes 488 | tf_op jit(solution)/shard_map/ppermute | solution.py:24
  18.6 36.6 %collective-permute-start.2 = (f32[40,1]{1,0:T(8,128)}, f32[40,1]{1,0:T(8,128)}, u32[]{:S(2)}, u32[]{:S(2)}) collective-permute-start(f32[40,1]{1,0:T(8,128)} %get-tuple-element.263), channel_id=1, source_target_pairs={{0,32},{32,64},{64,96},{96,128},{128,160},{160,192},{192,224},{1,3... | collective-permute-start | bytes 488 | tf_op jit(solution)/shard_map/ppermute | solution.py:23
  22.1 39.2 %collective-permute-start.1 = (f32[51,40,1]{0,1,2:T(8,128)}, f32[51,40,1]{0,1,2:T(8,128)}, u32[]{:S(2)}, u32[]{:S(2)}) collective-permute-start(f32[51,40,1]{0,1,2:T(8,128)} %pad_maximum_fusion.36), channel_id=1, source_target_pairs={{0,32},{32,64},{64,96},{96,128},{128,160},{160,192},{192,224},{1,3... | collective-permute-start | bytes 24488 | tf_op jit(solution)/shard_map/ppermute | solution.py:13
  25.6 36.5 %collective-permute-start.4 = (f32[51,1,128]{2,0,1:T(8,128)}, f32[51,1,128]{2,0,1:T(8,128)}, u32[]{:S(2)}, u32[]{:S(2)}) collective-permute-start(f32[51,1,128]{2,0,1:T(8,128)} %pad_maximum_fusion.11), channel_id=1, source_target_pairs={{0,1},{1,2},{2,3},{3,4},{4,5},{5,6},{6,7},{7,8},{8,9},{9,10},{10,1... | collective-permute-start | bytes 78344 | tf_op jit(solution)/shard_map/ppermute | solution.py:13
  31.3 7.7 copy-start.18
  32.3 14.0 %copy-start.81 = (f32[40,128]{1,0:T(8,128)}, f32[40,128]{1,0:T(8,128)S(1)}, u32[]{:S(2)}) copy-start(f32[40,128]{1,0:T(8,128)S(1)} %get-tuple-element.107) | copy-start | bytes 61444
  35.1 11.2 %copy-start.20 = (f32[1,40,128]{2,1,0:T(8,128)}, f32[1,40,128]{2,1,0:T(8,128)S(1)}, u32[]{:S(2)}) copy-start(f32[1,40,128]{2,1,0:T(8,128)S(1)} %get-tuple-element.51) | copy-start | bytes 61444
  35.1 11.2 %copy-start.46 = (f32[1,40,128]{2,1,0:T(8,128)}, f32[1,40,128]{2,1,0:T(8,128)S(1)}, u32[]{:S(2)}) copy-start(f32[1,40,128]{2,1,0:T(8,128)S(1)} %get-tuple-element.50) | copy-start | bytes 61444
  35.7 11.2 %copy-start.22 = (f32[1,40,128]{2,1,0:T(8,128)}, f32[1,40,128]{2,1,0:T(8,128)S(1)}, u32[]{:S(2)}) copy-start(f32[1,40,128]{2,1,0:T(8,128)S(1)} %get-tuple-element.54) | copy-start | bytes 61444
  36.3 11.1 %copy-start.24 = (f32[1,40,128]{2,1,0:T(8,128)}, f32[1,40,128]{2,1,0:T(8,128)S(1)}, u32[]{:S(2)}) copy-start(f32[1,40,128]{2,1,0:T(8,128)S(1)} %get-tuple-element.57) | copy-start | bytes 61444
  36.4 11.1 %copy-start.50 = (f32[1,40,128]{2,1,0:T(8,128)}, f32[1,40,128]{2,1,0:T(8,128)S(1)}, u32[]{:S(2)}) copy-start(f32[1,40,128]{2,1,0:T(8,128)S(1)} %get-tuple-element.56) | copy-start | bytes 61444
  37.0 11.1 %copy-start.26 = (f32[1,40,128]{2,1,0:T(8,128)}, f32[1,40,128]{2,1,0:T(8,128)S(1)}, u32[]{:S(2)}) copy-start(f32[1,40,128]{2,1,0:T(8,128)S(1)} %get-tuple-element.60) | copy-start | bytes 61444
  37.0 11.1 %copy-start.52 = (f32[1,40,128]{2,1,0:T(8,128)}, f32[1,40,128]{2,1,0:T(8,128)S(1)}, u32[]{:S(2)}) copy-start(f32[1,40,128]{2,1,0:T(8,128)S(1)} %get-tuple-element.59) | copy-start | bytes 61444
  38.2 9.2 %copy-start.32 = (f32[1,40,128]{2,1,0:T(8,128)}, f32[1,40,128]{2,1,0:T(8,128)S(1)}, u32[]{:S(2)}) copy-start(f32[1,40,128]{2,1,0:T(8,128)S(1)} %get-tuple-element.66) | copy-start | bytes 61444
  38.3 9.9 %copy-start.30 = (f32[1,40,128]{2,1,0:T(8,128)}, f32[1,40,128]{2,1,0:T(8,128)S(1)}, u32[]{:S(2)}) copy-start(f32[1,40,128]{2,1,0:T(8,128)S(1)} %get-tuple-element.65) | copy-start | bytes 61444
  39.7 15.5 %copy-start.14 = (f32[1,40,128]{2,1,0:T(8,128)}, f32[1,40,128]{2,1,0:T(8,128)S(1)}, u32[]{:S(2)}) copy-start(f32[1,40,128]{2,1,0:T(8,128)S(1)} %get-tuple-element.72) | copy-start | bytes 61444
  40.5 7.1 copy-start.56
  40.5 23.9 %copy-start.16 = (f32[1,40,128]{2,1,0:T(8,128)}, f32[1,40,128]{2,1,0:T(8,128)S(1)}, u32[]{:S(2)}) copy-start(f32[1,40,128]{2,1,0:T(8,128)S(1)} %get-tuple-element.75) | copy-start | bytes 61444
  41.8 5.7 copy-start.59
  41.8 19.5 %copy-start.34 = (f32[1,40,128]{2,1,0:T(8,128)}, f32[1,40,128]{2,1,0:T(8,128)S(1)}, u32[]{:S(2)}) copy-start(f32[1,40,128]{2,1,0:T(8,128)S(1)} %get-tuple-element.81) | copy-start | bytes 61444
  42.4 195.4 %copy-start.36 = (f32[1,40,128]{2,1,0:T(8,128)}, f32[1,40,128]{2,1,0:T(8,128)S(1)}, u32[]{:S(2)}) copy-start(f32[1,40,128]{2,1,0:T(8,128)S(1)} %get-tuple-element.84) | copy-start | bytes 61444
  43.0 5.1 copy-start.63
  56.0 6.8 collective-permute-start.3
  57.3 5.5 collective-permute-start.5
  225.2 6.4 collective-permute-start.6
  227.8 3.9 collective-permute-start.7
  231.8 6.0 collective-permute-start.8
  233.1 4.7 collective-permute-start.9
  396.8 6.4 collective-permute-start.10
  399.4 3.9 collective-permute-start.11
  403.3 6.5 copy-start.122
  403.3 6.5 copy-start.124
  403.9 12.2 %collective-permute-start.12 = (f32[1,130]{1,0:T(1,128)}, f32[1,130]{1,0:T(1,128)}, u32[]{:S(2)}, u32[]{:S(2)}) collective-permute-start(f32[1,130]{1,0:T(1,128)} %get-tuple-element.245), channel_id=1, source_target_pairs={{1,0},{2,1},{3,2},{4,3},{5,4},{6,5},{7,6},{8,7},{9,8},{10,9},{11,1... | collective-permute-start | bytes 1568 | tf_op jit(solution)/shard_map/ppermute | solution.py:24
  405.2 10.9 %collective-permute-start.13 = (f32[1,130]{1,0:T(1,128)}, f32[1,130]{1,0:T(1,128)}, u32[]{:S(2)}, u32[]{:S(2)}) collective-permute-start(f32[1,130]{1,0:T(1,128)} %get-tuple-element.246), channel_id=1, source_target_pairs={{0,1},{1,2},{2,3},{3,4},{4,5},{5,6},{6,7},{7,8},{8,9},{9,10},{10,1... | collective-permute-start | bytes 1568 | tf_op jit(solution)/shard_map/ppermute | solution.py:23
  409.9 5.1 copy-start.11
  502.2 6.1 copy-start.43
  529.6 12.8 %collective-permute-start.14 = (f32[2,50,40,1]{1,2,3,0:T(8,128)S(1)}, f32[2,50,40,1]{1,2,3,0:T(8,128)S(1)}, u32[]{:S(2)}, u32[]{:S(2)}) collective-permute-start(f32[2,50,40,1]{1,2,3,0:T(8,128)S(1)} %copy.201), channel_id=1, source_target_pairs={{32,0},{64,32},{96,64},{128,96},{160,128},{192,160},{224,192},{33,... | collective-permute-start | bytes 48008 | tf_op jit(solution)/shard_map/ppermute | solution.py:24
  535.9 9.6 %collective-permute-start.15 = (f32[2,50,40,1]{1,2,3,0:T(8,128)S(1)}, f32[2,50,40,1]{1,2,3,0:T(8,128)S(1)}, u32[]{:S(2)}, u32[]{:S(2)}) collective-permute-start(f32[2,50,40,1]{1,2,3,0:T(8,128)S(1)} %copy.205), channel_id=1, source_target_pairs={{0,32},{32,64},{64,96},{96,128},{128,160},{160,192},{192,224},{1,3... | collective-permute-start | bytes 48008 | tf_op jit(solution)/shard_map/ppermute | solution.py:23
  548.6 6.7 copy-start.10
  548.6 9.2 %copy-start.6 = (f32[50,40,128]{2,0,1:T(8,128)S(1)}, f32[50,40,128]{2,0,1:T(8,128)}, u32[]{:S(2)}) copy-start(f32[50,40,128]{2,0,1:T(8,128)} %copy.200) | copy-start | bytes 3072004
  548.6 9.2 %copy-start.7 = (f32[50,40,128]{2,0,1:T(8,128)S(1)}, f32[50,40,128]{2,0,1:T(8,128)}, u32[]{:S(2)}) copy-start(f32[50,40,128]{2,0,1:T(8,128)} %copy.207) | copy-start | bytes 3072004
  548.6 9.2 %copy-start.8 = (f32[50,40,128]{2,0,1:T(8,128)S(1)}, f32[50,40,128]{2,0,1:T(8,128)}, u32[]{:S(2)}) copy-start(f32[50,40,128]{2,0,1:T(8,128)} %copy.204) | copy-start | bytes 3072004
  550.1 6.6 collective-permute-start.16
  551.4 6.5 collective-permute-start.17
  (102 other events, 436.0 us)
Sparse Core Ops, SparseCore 0:
  584.6 262.3 all-reduce.2
where the time goes:
time: 866 us; the launch traced here: 855 us
  blocking collectives  387 us (45%)
  waiting for transfers between devices  263 us (30%)
  other arithmetic  78.1 us (9%)
  starting transfers between devices  51 us (6%)
  local copies, waits for them, and re-layouts  48 us (6%)
  between operations  23.2 us (3%)
    psum x1, waiting for transfers between devices, per_device(): totals = lax.psum(contribution, ('gx', 'gy'))  261 us
    psum x3, blocking collectives, squares(): return lax.psum(jnp.sum(remain * remain), ('gx', 'gy'))  232 us
    psum x2, blocking collectives, per_device(): step_len = norm_now / lax.psum(jnp.sum(search * image), ('gx', 'gy'))  155 us
    ppermute x8, starting transfers between devices, extended(): before = lax.ppermute(last, axis, up)  27.4 us
    ppermute x8, starting transfers between devices, extended(): after = lax.ppermute(leading, axis, down)  18 us
  transfers between devices with their start and end apart: 19, of which 3 were waited for; matrix products, arithmetic and copies ran while one was open for 6% of the time, Pallas kernels for 0%

commit v1 on v0

v1 whole, which is shorter than its diff:
```python
import functools

import jax
import jax.numpy as jnp
from jax import lax
from jax.experimental import pallas as pl
from jax.experimental.pallas import tpu as pltpu
from jax.sharding import PartitionSpec as P

SLOTS = 10
LANES = 128
BLOCK = 8
GRAM = ((0, 0), (0, 1), (0, 2), (0, 3), (1, 1), (1, 2), (1, 3), (2, 2), (2, 3))
VMEM = pl.BlockSpec(memory_space=pltpu.VMEM)
SMEM = pl.BlockSpec(memory_space=pltpu.SMEM)
HBM = pl.BlockSpec(memory_space=pltpu.HBM)
MIB = 1024 * 1024
BIG = pltpu.CompilerParams(vmem_limit_bytes=16 * MIB)
MIDDLE = pltpu.CompilerParams(vmem_limit_bytes=8 * MIB)
SMALL = pltpu.CompilerParams(vmem_limit_bytes=3 * MIB)


def lanes_of(shape):
    return lax.broadcasted_iota(jnp.int32, shape, len(shape) - 1)


def moved(value, source, target):
    shift = target - source
    shift = shift % LANES if isinstance(shift, int) else lax.rem(shift + 4 * LANES, LANES)
    return pltpu.roll(value, shift, 1)


def columns_kernel(
    forcing_in, loads_in, tracer_in, surface_in, east_flow, north_flow, mix_in, mask_in, c_east_in,
    c_north_in, diag_in,
    b_out, u_out, v_out, west_pack, east_pack, south_rows, north_rows,
    ratios, forcing, loads, tracer, surface, flow_east, flow_north, mix, mask, c_east, c_north, diag,
    sems,
):
    levels, rows, cols = mask.shape
    shape = (rows, cols)
    zero = jnp.zeros(shape, jnp.float32)
    last = levels - 1
    chunk = 7
    started = []

    def fetch(source, target):
        copy = pltpu.make_async_copy(source, target, sems.at[len(started)])
        copy.start()
        started.append(copy)
        return copy

    scalars = [fetch(forcing_in, forcing), fetch(loads_in, loads)]
    chunks = []
    for at in range(0, last, chunk):
        here = pl.ds(at, chunk if at + chunk < last else chunk + 1)
        below = pl.ds(at + 1, chunk) if at else pl.ds(0, chunk + 1)
        chunks.append([
            fetch(mask_in.at[below], mask.at[below]),
            fetch(mix_in.at[pl.ds(at, chunk)], mix.at[pl.ds(at, chunk)]),
            fetch(tracer_in.at[:, here], tracer.at[:, here]),
        ])
    flats = [
        fetch(source, target)
        for source, target in (
            (surface_in, surface), (c_east_in, c_east), (c_north_in, c_north), (diag_in, diag),
            (north_flow.at[:, pl.ds(rows - BLOCK, BLOCK)], flow_north), (east_flow, flow_east),
        )
    ]
    for copy in scalars:
        copy.wait()

    def level_step(k, carry, kappa):
        before, ratio, r0, r1, r2, r3, total = carry
        wet = mask[k].astype(jnp.float32)
        t0, t1 = tracer[0, k], tracer[1, k]
        total = total + wet * (forcing[0, k] * t0 + forcing[1, k] * t1)
        inverse = 1.0 / (1.0 + before + kappa - before * ratio)
        r0 = (t0 + before * r0) * inverse
        r1 = (t1 + before * r1) * inverse
        r2 = (wet * loads[0, k] + before * r2) * inverse
        r3 = (wet * loads[1, k] + before * r3) * inverse
        return kappa * inverse, r0, r1, r2, r3, total

    carry = (zero,) * 7
    for k in range(last):
        if k % chunk == 0:
            for copy in chunks[k // chunk]:
                copy.wait()
        kappa = mix[k] * mask[k + 1].astype(jnp.float32)
        ratio, *reds, total = level_step(k, carry, kappa)
        ratios[k] = ratio
        u_out[0, k], u_out[1, k], v_out[0, k], v_out[1, k] = reds
        carry = (kappa, ratio, *reds, total)
    _, *sols, total = level_step(last, carry, zero)
    for copy in flats:
        copy.wait()
    total = total + surface[...]
    b_out[...] = total

    for k in range(last, -1, -1):
        if k < last:
            ratio = ratios[k]
            reds = (u_out[0, k], u_out[1, k], v_out[0, k], v_out[1, k])
            sols = [red + ratio * sol for red, sol in zip(reds, sols)]
        wet = mask[k].astype(jnp.float32)
        fields = [wet * sol for sol in sols]
        u_out[0, k], u_out[1, k], v_out[0, k], v_out[1, k] = fields
        for q, field in enumerate(fields):
            south_rows[q * levels + k : q * levels + k + 1, :] = field[0:1]
            north_rows[q * levels + k : q * levels + k + 1, :] = field[rows - 1 : rows]
    lane = lanes_of(shape)
    side = slice(LANES, 2 * LANES)
    west_pack[:, side] = zero
    east_pack[:, side] = zero
    for tile in range(2):
        west, east = zero, zero
        for spot in range(4 * min(32, levels - 32 * tile)):
            k, q = 32 * tile + spot // 4, spot % 4
            field = u_out[q, k] if q < 2 else v_out[q - 2, k]
            west = jnp.where(lane == spot, moved(field, 0, spot), west)
            east = jnp.where(lane == spot, moved(field, cols - 1, spot), east)
        west_pack[:, tile * LANES : (tile + 1) * LANES] = west
        east_pack[:, tile * LANES : (tile + 1) * LANES] = east
    value = east_pack[:, side]
    for k in range(levels):
        value = jnp.where(lane == 72 + k, moved(flow_east[k], cols - 1, 72 + k), value)
        north_rows[240 + k : 241 + k, :] = flow_north[k, BLOCK - 1 : BLOCK, :]
    east_pack[:, side] = value
    west, east = zero, zero
    for a, field in enumerate((total, c_east[...], c_north[...], diag[...])):
        here = (lane >= 4 * a) & (lane < 4 * a + 3)
        west = jnp.where(here, moved(field, 0, 4 * a), west)
        east = jnp.where(here, moved(field, cols - 3, 4 * a), east)
    west_pack[:, 2 * LANES :], east_pack[:, 2 * LANES :] = west, east


def rows_kernel(b, c_east, c_north, diag, west_in, east_in, _s, _n, south_rows, north_rows, side):
    shape = b.shape
    rows = shape[0]
    lane = lanes_of(shape)
    both = jnp.where(
        lane < 64, west_in[:, 2 * LANES :], moved(east_in[:, 2 * LANES :], 0, 64)
    )
    side[...] = both
    for a, field in enumerate((b, c_east, c_north, diag, side)):
        south_rows[8 * a : 8 * a + 8, :] = field[0:BLOCK, :]
        north_rows[8 * a : 8 * a + 8, :] = field[rows - BLOCK :, :]


def krylov_kernel(b, c_east, c_north, diag, side, south_in, north_in, v0_out, v1_out, v2_out, sums):
    rows = b.shape[0]
    sides = jnp.concatenate([south_in[232:240, :], side[...], north_in[232:240, :]], axis=0)
    lane = lanes_of(sides.shape)
    full = []
    for a, field in enumerate((b, c_east, c_north, diag)):
        at = slice(200 + 8 * a, 208 + 8 * a)
        main = jnp.concatenate([south_in[at, :], field[...], north_in[at, :]], axis=0)
        beside = jnp.where(
            lane >= LANES - 3,
            moved(sides, 4 * a, LANES - 3),
            jnp.where(lane < 3, moved(sides, 64 + 4 * a, 0), 0.0),
        )
        full.append(jnp.concatenate([main, beside], axis=1))
    vec, ce, cn, dg = full
    tall, wide = vec.shape
    cw = pltpu.roll(ce, 1, 1)
    cs = pltpu.roll(cn, 1, 0)
    vecs = [vec]
    for _ in range(3):
        vec = (
            dg * vec
            + ce * (vec - pltpu.roll(vec, wide - 1, 1))
            + cw * (vec - pltpu.roll(vec, 1, 1))
            + cn * (vec - pltpu.roll(vec, tall - 1, 0))
            + cs * (vec - pltpu.roll(vec, 1, 0))
        )
        vecs.append(vec)
    v0_out[...], v1_out[...], v2_out[...] = vecs[:3]
    inner = [value[BLOCK : BLOCK + rows, :LANES] for value in vecs]
    spot = lanes_of((1, LANES))
    row = jnp.zeros((1, LANES), jnp.float32)
    for n, (i, j) in enumerate(GRAM):
        part = jnp.sum(inner[i] * inner[j], axis=0, keepdims=True)
        row = jnp.where(spot == n, jnp.sum(part, axis=1, keepdims=True), row)
    sums[...] = row


def krylov_weights(gram):
    def form(left, right):
        total = 0.0
        for i, x in left.items():
            for j, y in right.items():
                total = total + x * y * gram[min(i, j), max(i, j)]
        return total

    one = jnp.ones_like(gram[0, 0])
    remain, search = {0: one}, {0: one}
    weights = {}
    norm = gram[0, 0]
    for iteration in range(3):
        image = {i + 1: x for i, x in search.items()}
        step = norm / form(search, image)
        for i, x in search.items():
            weights[i] = weights.get(i, 0.0) + step * x
        if iteration < 2:
            remain = {
                i: remain.get(i, 0.0) - step * image.get(i, 0.0) for i in range(iteration + 2)
            }
            renewed = form(remain, remain)
            ratio = renewed / norm
            search = {i: x + ratio * search.get(i, 0.0) for i, x in remain.items()}
            norm = renewed
    return weights


def fields_kernel(
    place, sums_in, v0, v1, v2, u, v, flow_east, flow_north, west_in, east_in, south_in, north_in,
    grad_out, x_out, rim, grad, x_full, south_lam, north_lam, lam_buf, flux_buf, sems,
):
    levels, rows, cols = flow_east.shape
    shape = (rows, cols)
    lane = lanes_of(shape)
    totals = jnp.sum(sums_in[...], axis=0, keepdims=True)
    gram = {pair: totals[:, n : n + 1] for n, pair in enumerate(GRAM)}
    weights = krylov_weights(gram)
    x_full[...] = weights[0] * v0[...] + weights[1] * v1[...] + weights[2] * v2[...]
    x = x_full[BLOCK : BLOCK + rows, :cols]
    x_out[...] = x
    count = 2 * levels
    south_lam[...] = (
        south_in[0:count, :] + south_in[count : 2 * count, :] * x_full[BLOCK - 1 : BLOCK, :cols]
    )
    north_lam[...] = (
        north_in[0:count, :]
        + north_in[count : 2 * count, :] * x_full[BLOCK + rows : BLOCK + rows + 1, :cols]
    )
    x_west = x_full[BLOCK : BLOCK + rows, 2 * LANES - 1 :]
    x_east = x_full[BLOCK : BLOCK + rows, LANES : LANES + 1]
    part = lane & 3
    halos = []
    for tile in range(2):
        at = slice(tile * LANES, (tile + 1) * LANES)
        west, east = west_in[:, at], east_in[:, at]
        west = west + pltpu.roll(west, LANES - 2, 1) * x_west
        east = east + pltpu.roll(east, LANES - 2, 1) * x_east
        later = jnp.where(part == 2, pltpu.roll(west, 1, 1), pltpu.roll(east, LANES - 1, 1))
        halos.append(jnp.where(part == 0, west, jnp.where(part == 1, east, later)))
    rim_row = jnp.where(place[1] == 0, 0, rows - 1)
    rim_shift = jnp.where(place[0] == 0, 0, 1)
    rim_base = 104
    rim[2 * levels : rim_base, :] = jnp.zeros((rim_base - 2 * levels, LANES), jnp.float32)
    copies = []
    for k in range(levels):
        fe, fn = 0.5 * flow_east[k], 0.5 * flow_north[k]
        fw = jnp.where(
            lane == 0, 0.5 * moved(west_in[:, LANES : 2 * LANES], 72 + k, 0), pltpu.roll(fe, 1, 1)
        )
        fs = 0.5 * south_in[240 + k : 241 + k, :]
        for s in range(2):
            n = s * levels + k
            slot = n % 10
            lam = u[s, k] + v[s, k] * x
            lam_buf[slot, 0:rows, :] = lam
            lam_buf[slot, rows : rows + 1, :] = north_lam[n : n + 1, :]
            halo = moved(halos[k // 32], 4 * (k % 32) + 2 * s, 0)
            east = jnp.where(lane == cols - 1, halo, pltpu.roll(lam, cols - 1, 1))
            west = jnp.where(lane == 0, halo, pltpu.roll(lam, 1, 1))
            flux = fn * (lam_buf[slot, 1 : rows + 1, :] - lam)
            flux_buf[slot, BLOCK : BLOCK + rows, :] = flux
            flux_buf[slot, BLOCK - 1 : BLOCK, :] = fs * (lam[0:1] - south_lam[n : n + 1, :])
            out = (
                lam
                + fe * (east - lam)
                + fw * (lam - west)
                + flux
                + flux_buf[slot, BLOCK - 1 : BLOCK - 1 + rows, :]
            )
            grad[s, k] = out
            rim[n : n + 1, :] = grad[s, k, pl.ds(rim_row, 1), :]
        if k % 10 == 9:
            at = pl.ds(k - 9, 10)
            copies.append(
                pltpu.make_async_copy(grad.at[:, at], grad_out.at[:, at], sems.at[k // 10])
            )
            copies[-1].start()
    rim_side = jnp.zeros(shape, jnp.float32)
    for n in range(2 * levels):
        rolled = moved(grad[n // levels, n % levels], 0, n)
        rim_side = jnp.where(lane == ((n - rim_shift) & (LANES - 1)), rolled, rim_side)
    rim[rim_base:, :] = pltpu.roll(rim_side, rim_shift, 1)
    for copy in copies:
        copy.wait()


def controls_kernel(place, rims, point_map, point_weight, out, beside):
    peers, rim_rows, _ = rims.shape
    depth = 104
    wide = rim_rows - depth
    share = 32 * SLOTS
    row_of = lax.broadcasted_iota(jnp.int32, (share, LANES), 0)

    def spread(ids, weights):
        return jnp.where(row_of == ids - place[0] * share, weights, 0.0)

    def window(ref, start):
        first = start // LANES
        second = jnp.minimum(first + 1, ref.shape[0] - 1)
        pair = jnp.concatenate([ref[pl.ds(first, 1), :], ref[pl.ds(second, 1), :]], axis=1)
        pair = pltpu.roll(pair, lax.rem(2 * LANES - lax.rem(start, LANES), 2 * LANES), 1)
        return pair[:, :LANES]

    lane = lanes_of((1, LANES))
    west_at = 2048 + place[1] * wide
    east_at = 3328 + place[1] * wide

    def joined(ref, fill):
        west, east = window(ref, west_at), window(ref, east_at)
        east = pltpu.roll(east, wide, 1)
        return jnp.where(lane < wide, west, jnp.where(lane < 2 * wide, east, fill))

    beside[...] = jnp.zeros_like(beside)
    beside[0:wide, :] = rims[0, depth:, :]
    beside[wide : 2 * wide, :] = rims[peers - 1, depth:, :]
    out[...] = lax.dot_general(
        spread(joined(point_map, -1), joined(point_weight, 0.0)),
        beside[...],
        (((1,), (0,)), ((), ())),
        precision=lax.Precision.HIGHEST,
        preferred_element_type=jnp.float32,
    )
    first = jnp.where(place[1] == 0, 0, peers)

    @pl.when((place[1] == 0) | (place[1] == 31))
    def _():
        total = jnp.zeros((share, depth), jnp.float32)
        for peer in range(peers):
            ids = point_map[pl.ds(first + peer, 1), :]
            weights = point_weight[pl.ds(first + peer, 1), :]
            total = total + lax.dot_general(
                spread(ids, weights),
                rims[peer, 0:depth, :],
                (((1,), (1,)), ((), ())),
                precision=lax.Precision.HIGHEST,
                preferred_element_type=jnp.float32,
            )
        out[:, 0:depth] = out[:, 0:depth] + total


def gather_kernel(parts, out):
    total = parts[0:SLOTS, :]
    for at in range(SLOTS, parts.shape[0], SLOTS):
        total = total + parts[at : at + SLOTS, :]
    levels = out.shape[2]
    out[:, 0, :] = total[0:SLOTS, 0:levels]
    out[:, 1, :] = total[0:SLOTS, levels : 2 * levels]


def shifted(value, axis, step):
    count = lax.axis_size(axis)
    pairs = [(i, i + step) for i in range(count) if 0 <= i + step < count]
    return lax.ppermute(value, axis, pairs)


def shape_of(*shape):
    return jax.ShapeDtypeStruct(shape, jnp.float32)


def per_device(
    tracer_adjoint,
    surface_adjoint,
    flow_east,
    flow_north,
    vertical_mix,
    land_mask,
    conduct_east,
    conduct_north,
    surface_diagonal,
    pressure_load,
    surface_forcing,
    control_map,
    control_weight,
):
    levels, rows, cols = flow_east.shape
    across, along = lax.axis_size("gx"), lax.axis_size("gy")
    place = jnp.stack([lax.axis_index("gx"), lax.axis_index("gy")]).astype(jnp.int32)
    point_map = control_map.reshape(-1, LANES)
    point_weight = control_weight.reshape(-1, LANES)

    tile = shape_of(rows, cols)
    field = shape_of(2, levels, rows, cols)
    pack = shape_of(rows, 3 * LANES)
    kept = pltpu.VMEM(field.shape, jnp.float32)
    south_shape, north_shape = shape_of(240, cols), shape_of(296, cols)
    b, u, v, west_pack, east_pack, south_rows, north_rows = pl.pallas_call(
        columns_kernel,
        out_shape=(tile, kept, kept, pack, pack, south_shape, north_shape),
        in_specs=[HBM] * 11,
        out_specs=(VMEM,) * 7,
        scratch_shapes=[
            pltpu.VMEM((levels, rows, cols), jnp.float32),
            pltpu.SMEM((2, levels), jnp.float32),
            pltpu.SMEM((2, levels), jnp.float32),
            pltpu.VMEM((2, levels, rows, cols), jnp.float32),
            pltpu.VMEM((rows, cols), jnp.float32),
            pltpu.VMEM((levels, rows, cols), jnp.float32),
            pltpu.VMEM((levels, BLOCK, cols), jnp.float32),
            pltpu.VMEM((levels - 1, rows, cols), jnp.float32),
            pltpu.VMEM((levels, rows, cols), jnp.int32),
            pltpu.VMEM((rows, cols), jnp.float32),
            pltpu.VMEM((rows, cols), jnp.float32),
            pltpu.VMEM((rows, cols), jnp.float32),
            pltpu.SemaphoreType.DMA((48,)),
        ],
        compiler_params=BIG,
        name="columns",
    )(
        *(
            pltpu.with_memory_space_constraint(value, pltpu.HBM)
            for value in (
                surface_forcing, pressure_load, tracer_adjoint, surface_adjoint, flow_east, flow_north,
                vertical_mix, land_mask, conduct_east, conduct_north, surface_diagonal,
            )
        )
    )
    stay = [pltpu.with_memory_space_constraint(value, pltpu.VMEM) for value in (u, v)]
    west_pack, place = lax.optimization_barrier((west_pack, place))
    west_in = shifted(east_pack, "gx", 1)
    east_in = shifted(west_pack, "gx", -1)
    outer = pl.BlockSpec((5 * BLOCK, cols), lambda i: (5, 0))
    south_rows, north_rows, side = pl.pallas_call(
        rows_kernel,
        out_shape=(south_shape, north_shape, tile),
        grid=(1,),
        in_specs=[VMEM] * 6 + [pl.BlockSpec(memory_space=pl.ANY)] * 2,
        out_specs=(outer, outer, VMEM),
        input_output_aliases={6: 0, 7: 1},
        compiler_params=SMALL,
        name="rows",
    )(b, conduct_east, conduct_north, surface_diagonal, west_in, east_in, south_rows, north_rows)
    south_in = shifted(north_rows, "gy", 1)
    north_in = shifted(south_rows, "gy", -1)
    full = shape_of(rows + 2 * BLOCK, 2 * LANES)
    v0, v1, v2, sums = pl.pallas_call(
        krylov_kernel,
        out_shape=(full, full, full, shape_of(1, LANES)),
        in_specs=[VMEM] * 7,
        out_specs=(VMEM,) * 4,
        compiler_params=SMALL,
        name="krylov",
    )(b, conduct_east, conduct_north, surface_diagonal, side, south_in, north_in)
    everyone = across * along
    sums = jnp.broadcast_to(sums[None], (everyone, 1, LANES))
    sums = lax.all_to_all(sums, ("gx", "gy"), 0, 0).reshape(everyone, LANES)
    rim_rows = 104 + rows
    tracer_grad, x, rim = pl.pallas_call(
        fields_kernel,
        out_shape=(field, tile, shape_of(rim_rows, LANES)),
        in_specs=[SMEM] + [VMEM] * 12,
        out_specs=(HBM, VMEM, VMEM),
        scratch_shapes=[
            pltpu.VMEM((2, levels, rows, cols), jnp.float32),
            pltpu.VMEM(full.shape, jnp.float32),
            pltpu.VMEM((2 * levels, cols), jnp.float32),
            pltpu.VMEM((2 * levels, cols), jnp.float32),
            pltpu.VMEM((10, rows + BLOCK, cols), jnp.float32),
            pltpu.VMEM((10, rows + BLOCK, cols), jnp.float32),
            pltpu.SemaphoreType.DMA((levels // 10,)),
        ],
        compiler_params=MIDDLE,
        name="fields",
    )(place, sums, v0, v1, v2, *stay, flow_east, flow_north, west_in, east_in, south_in, north_in)
    rims = lax.all_to_all(jnp.broadcast_to(rim[None], (across, rim_rows, LANES)), "gx", 0, 0)
    parts = pl.pallas_call(
        controls_kernel,
        out_shape=shape_of(along * SLOTS, LANES),
        in_specs=[SMEM] + [VMEM] * 3,
        out_specs=VMEM,
        scratch_shapes=[pltpu.VMEM((LANES, LANES), jnp.float32)],
        compiler_params=SMALL,
        name="controls",
    )(place, rims, point_map, point_weight)
    parts = lax.all_to_all(parts.reshape(along, 1, SLOTS * LANES), "gy", 0, 0)
    parts = parts.reshape(along * SLOTS, LANES)
    control_grad = pl.pallas_call(
        gather_kernel,
        out_shape=shape_of(SLOTS, 2, levels),
        in_specs=[VMEM],
        out_specs=VMEM,
        compiler_params=SMALL,
        name="gather",
    )(parts)
    return tracer_grad, x, jnp.transpose(control_grad, (1, 2, 0))


def solution(mesh):
    in_specs = (
        P(None, None, "gy", "gx"),
        P("gy", "gx"),
        P(None, "gy", "gx"),
        P(None, "gy", "gx"),
        P(None, "gy", "gx"),
        P(None, "gy", "gx"),
        P("gy", "gx"),
        P("gy", "gx"),
        P("gy", "gx"),
        P(),
        P(),
        P(),
        P(),
    )
    out_specs = (P(None, None, "gy", "gx"), P("gy", "gx"), P(None, None, ("gx", "gy")))
    return jax.shard_map(
        per_device, mesh=mesh, in_specs=in_specs, out_specs=out_specs, check_vma=False
    )
```

time: 866 us -> 90.7 us (0.10); the launches traced: 855 us -> 90.4 us
  blocking collectives: 387 us -> 56.6 us
  waiting for transfers between devices: 263 us -> 6.57 us
  other arithmetic: 78.1 us -> 0.08 us
  local copies, waits for them, and re-layouts: 48 us -> 0.14 us
  starting transfers between devices: 51 us -> 10.9 us
  between operations: 23.2 us -> 0.74 us
  Pallas kernels: 0 us -> 15.3 us
    psum x5 -> x0, blocking collectives: 387 us -> none  [the longest x3 232 us: squares(): return lax.psum(jnp.sum(remain * remain), ('gx', 'gy'))]
    psum x1 -> x0, waiting for transfers between devices: 261 us -> none  [per_device(): totals = lax.psum(contribution, ('gx', 'gy'))]
    all_to_all x0 -> x3, blocking collectives: none -> 56.6 us  [the longest x1 30.3 us: per_device(): sums = lax.all_to_all(sums, ('gx', 'gy'), 0, 0).reshape(everyone, LANES)]
    ppermute x18 -> x4, starting transfers between devices: 50.9 us -> 10.9 us  [shifted(): return lax.ppermute(value, axis, pairs)]
    slice x13 -> x0, local copies, waits for them, and re-layouts: 25.2 us -> none  [the longest x5 8.71 us: extended(): last = lax.slice_in_dim(shard, length - width, length, axis=dim)]
    mul x30 -> x0, other arithmetic: 23.9 us -> none  [the longest x21 15.3 us: column_solve(): solution.insert(0, reduced[level] + ratios[level] * solution[0])]
    add x6 -> x0, other arithmetic: 16.9 us -> none  [the longest x1 12.9 us: per_device(): center + 0.5 * flow_east * (east_side - center)]
    pallas_call x0 -> x6, Pallas kernels: none -> 15.3 us  [the longest x1 6.37 us: per_device(): pl.pallas_call(columns_kernel, out_shape=(tile, kept, kept, pack, pack, s...]
  transfers between devices with their start and end apart: 19 -> 4, of which waited for: 3 -> 2; matrix products, arithmetic and copies ran while one was open for 6% -> 0% of each run, Pallas kernels for 0% -> 0%
where the time goes in v1:
time: 90.7 us; the launch traced here: 90.4 us
  blocking collectives  56.6 us (62%)
  Pallas kernels  15.3 us (17%)
  starting transfers between devices  10.9 us (12%)
  waiting for transfers between devices  6.57 us (7%)
    all_to_all x1, blocking collectives, per_device(): sums = lax.all_to_all(sums, ('gx', 'gy'), 0, 0).reshape(everyone, LANES)  30.3 us
    all_to_all x1, blocking collectives, per_device(): lax.all_to_all(jnp.broadcast_to(rim[None], (across, rim_rows, LANES)), 'g...  13.8 us
    all_to_all x1, blocking collectives, per_device(): parts = lax.all_to_all(parts.reshape(along, 1, SLOTS * LANES), 'gy', 0, 0)  12.5 us
    ppermute x4, starting transfers between devices, shifted(): return lax.ppermute(value, axis, pairs)  10.9 us
    ppermute x4, waiting for transfers between devices, shifted(): return lax.ppermute(value, axis, pairs)  6.57 us
    pallas_call x1, Pallas kernels, per_device(): pl.pallas_call(columns_kernel, out_shape=(tile, kept, kept, pack, pack, s...  6.37 us
    pallas_call x1, Pallas kernels, per_device(): pl.pallas_call(fields_kernel, out_shape=(field, tile, shape_of(rim_rows,...  5.52 us
    pallas_call x1, Pallas kernels, per_device(): pl.pallas_call(controls_kernel, out_shape=shape_of(along * SLOTS, LANES),...  2.23 us
  transfers between devices with their start and end apart: 4, of which 2 were waited for; matrix products, arithmetic and copies ran while one was open for 0% of the time, Pallas kernels for 0%

profile of v1, /device:TPU:1, one launch (start us, length us, event | category | flops | bytes accessed | tf_op | source)
XLA Modules:
  0.0 90.4 jit_solution(15401905129637254447)
XLA Ops:
  0.6 0.1 pad_add_fusion.place
  0.7 0.0 copy-start.2
  0.7 0.0 copy-start.3
  0.7 0.0 copy-start.4
  0.7 0.0 copy-start
  0.7 0.0 copy-start.1
  0.7 6.4 %columns.1 = (f32[40,128]{1,0:T(8,128)S(1)}, f32[2,50,40,128]{3,2,1,0:T(8,128)S(1)}, f32[2,50,40,128]{3,2,1,0:T(8,128)S(1)}, f32[40,384]{1,0:T(8,128)S(1)}, f32[...) custom-call(f32[2,50]{1,0:T(2,128)} %forcing_in.1, f32[2,50]{1,0:T(2,128)} %loads_in.1, ...), custom_call_target="tpu_custom_call" | custom-call | tf_op jit(solution)/shard_map/columns/pallas_call | solution.py:395
  7.1 5.1 %collective-permute-start.1 = (f32[40,384]{1,0:T(8,128)S(1)}, f32[40,384]{1,0:T(8,128)S(1)}, u32[]{:S(2)}, u32[]{:S(2)}) collective-permute-start(f32[40,384]{1,0:T(8,128)S(1)} %get-tuple-element.26), channel_id=1, source_target_pairs={{32,0},{64,32},{96,64},{128,96},{160,128},{192,160},{224,192},{33,... | collective-permute-start | bytes 184328 | tf_op jit(solution)/shard_map/ppermute | solution.py:362
  12.3 1.9 %collective-permute-start = (f32[40,384]{1,0:T(8,128)S(1)}, f32[40,384]{1,0:T(8,128)S(1)}, u32[]{:S(2)}, u32[]{:S(2)}) collective-permute-start(f32[40,384]{1,0:T(8,128)S(1)} %get-tuple-element.25), channel_id=1, source_target_pairs={{0,32},{32,64},{64,96},{96,128},{128,160},{160,192},{192,224},{1,3... | collective-permute-start | bytes 184328 | tf_op jit(solution)/shard_map/ppermute | solution.py:362
  14.2 0.0 collective-permute-done.1.east_in
  14.2 1.3 %collective-permute-done.west_in = f32[40,384]{1,0:T(8,128)S(1)} collective-permute-done((f32[40,384]{1,0:T(8,128)S(1)}, f32[40,384]{1,0:T(8,128)S(1)}, u32[]{:S(2)}, u32[]{:S(2)}) %collective-permute-start) | collective-permute-done | bytes 61472 | tf_op jit(solution)/shard_map/ppermute | solution.py:362
  15.5 0.0 copy-done.2
  15.5 0.0 copy-done.3
  15.5 0.0 copy-done.4
  15.5 0.1 rows.1
  15.6 2.6 %collective-permute-start.2 = (f32[296,128]{1,0:T(8,128)S(1)}, f32[296,128]{1,0:T(8,128)S(1)}, u32[]{:S(2)}, u32[]{:S(2)}) collective-permute-start(f32[296,128]{1,0:T(8,128)S(1)} %get-tuple-element.30), channel_id=1, source_target_pairs={{0,1},{1,2},{2,3},{3,4},{4,5},{5,6},{6,7},{7,8},{8,9},{9,10},{10,1... | collective-permute-start | bytes 454664 | tf_op jit(solution)/shard_map/ppermute | solution.py:362
  18.1 1.3 %collective-permute-start.3 = (f32[240,128]{1,0:T(8,128)S(1)}, f32[240,128]{1,0:T(8,128)S(1)}, u32[]{:S(2)}, u32[]{:S(2)}) collective-permute-start(f32[240,128]{1,0:T(8,128)S(1)} %get-tuple-element.31), channel_id=1, source_target_pairs={{1,0},{2,1},{3,2},{4,3},{5,4},{6,5},{7,6},{8,7},{9,8},{10,9},{11,1... | collective-permute-start | bytes 368648 | tf_op jit(solution)/shard_map/ppermute | solution.py:362
  19.4 5.3 %collective-permute-done.3.north_in = f32[240,128]{1,0:T(8,128)S(1)} collective-permute-done((f32[240,128]{1,0:T(8,128)S(1)}, f32[240,128]{1,0:T(8,128)S(1)}, u32[]{:S(2)}, u32[]{:S(2)}) %collective-permute-start.3) | collective-permute-done | bytes 122912 | tf_op jit(solution)/shard_map/ppermute | solution.py:362
  24.7 0.0 collective-permute-done.2.south_in
  24.7 0.4 krylov.1
  25.2 0.1 broadcast_in_dim.7
  25.2 30.3 %all_to_all.15 = f32[256,1,128]{2,1,0:T(1,128)S(1)} all-to-all(f32[256,1,128]{2,1,0:T(1,128)S(1)} %broadcast_in_dim.7), channel_id=1, replica_groups=mesh['gx'=8,'gy'=32] {'gx','gy'}, dimensions={0} | all-to-all | bytes 262144 | tf_op jit(solution)/shard_map/all_to_all | solution.py:454
  55.5 0.0 copy-done
  55.5 0.0 copy-done.1
  55.5 0.0 copy-start.5
  55.5 0.0 copy-start.6
  55.5 5.5 %fields.1 = (f32[2,50,40,128]{3,2,1,0:T(8,128)}, f32[40,128]{1,0:T(8,128)}, f32[144,128]{1,0:T(8,128)S(1)}) custom-call(s32[2]{0:T(128)S(1)} %pad_add_fusion.place, f32[256,128]{1,0:T(8,128)S(1)} %bitcast.11, f32[56,256]{1,0:T(8,128)S(1)} %get-tuple-element.33.v0, f32[56,256]{1,0:T(8,128)S(1)} %get-tuple-element.34.v1, f32[56,256]{1,0:T(8,128)S(1)} %get-tuple-element.35.v2, ...), custom_call_target="tpu_custom_call" | custom-call | tf_op jit(solution)/shard_map/fields/pallas_call | solution.py:456
  61.1 13.8 %all_to_all.16.rims = f32[8,144,128]{2,1,0:T(8,128)S(1)} all-to-all(f32[8,144,128]{2,1,0:T(8,128)S(1)} %broadcast_in_dim.16), channel_id=1, replica_groups=mesh['gx'=8,'gy'=32] {'gx'}, dimensions={0} | all-to-all | bytes 1179648 | tf_op jit(solution)/shard_map/all_to_all | solution.py:473
  74.9 0.0 copy-done.5
  74.9 0.0 copy-done.6
  74.9 2.2 %controls.1 = f32[320,128]{1,0:T(8,128)S(1)} custom-call(s32[2]{0:T(128)S(1)} %pad_add_fusion.place, f32[8,144,128]{2,1,0:T(8,128)S(1)} %all_to_all.16.rims, s32[36,128]{1,0:T(8,128)S(1)} %bitcast.12, f32[36,128]{1,0:T(8,128)S(1)} %bitcast.13), custom_call_target="tpu_custom_call" | custom-call | tf_op jit(solution)/shard_map/controls/pallas_call | solution.py:474
  77.1 12.5 %all_to_all.17 = f32[32,1,1280]{2,1,0:T(1,128)S(1)} all-to-all(f32[32,1,1280]{2,1,0:T(1,128)S(1)} %bitcast.10), channel_id=1, replica_groups=mesh['gx'=8,'gy'=32] {'gy'}, dimensions={0} | all-to-all | bytes 327680 | tf_op jit(solution)/shard_map/all_to_all | solution.py:483
  89.7 0.7 gather.1
  (1 shorter events, 0.0 us)
Async XLA Ops:
  0.7 14.8 %copy-start.2 = (f32[40,128]{1,0:T(8,128)S(1)}, f32[40,128]{1,0:T(8,128)}, u32[]{:S(2)}) copy-start(f32[40,128]{1,0:T(8,128)} %c_east.3) | copy-start | bytes 61444
  0.7 14.8 %copy-start.3 = (f32[40,128]{1,0:T(8,128)S(1)}, f32[40,128]{1,0:T(8,128)}, u32[]{:S(2)}) copy-start(f32[40,128]{1,0:T(8,128)} %c_north.3) | copy-start | bytes 61444
  0.7 14.8 %copy-start.4 = (f32[40,128]{1,0:T(8,128)S(1)}, f32[40,128]{1,0:T(8,128)}, u32[]{:S(2)}) copy-start(f32[40,128]{1,0:T(8,128)} %diag.3) | copy-start | bytes 61444
  0.7 54.8 %copy-start = (f32[50,40,128]{2,1,0:T(8,128)S(1)}, f32[50,40,128]{2,1,0:T(8,128)}, u32[]{:S(2)}) copy-start(f32[50,40,128]{2,1,0:T(8,128)} %flow_east.1) | copy-start | bytes 3072004
  0.7 54.8 %copy-start.1 = (f32[50,40,128]{2,1,0:T(8,128)S(1)}, f32[50,40,128]{2,1,0:T(8,128)}, u32[]{:S(2)}) copy-start(f32[50,40,128]{2,1,0:T(8,128)} %flow_north.1) | copy-start | bytes 3072004
  7.1 7.1 %collective-permute-start.1 = (f32[40,384]{1,0:T(8,128)S(1)}, f32[40,384]{1,0:T(8,128)S(1)}, u32[]{:S(2)}, u32[]{:S(2)}) collective-permute-start(f32[40,384]{1,0:T(8,128)S(1)} %get-tuple-element.26), channel_id=1, source_target_pairs={{32,0},{64,32},{96,64},{128,96},{160,128},{192,160},{224,192},{33,... | collective-permute-start | bytes 184328 | tf_op jit(solution)/shard_map/ppermute | solution.py:362
  12.3 3.2 %collective-permute-start = (f32[40,384]{1,0:T(8,128)S(1)}, f32[40,384]{1,0:T(8,128)S(1)}, u32[]{:S(2)}, u32[]{:S(2)}) collective-permute-start(f32[40,384]{1,0:T(8,128)S(1)} %get-tuple-element.25), channel_id=1, source_target_pairs={{0,32},{32,64},{64,96},{96,128},{128,160},{160,192},{192,224},{1,3... | collective-permute-start | bytes 184328 | tf_op jit(solution)/shard_map/ppermute | solution.py:362
  15.6 9.2 %collective-permute-start.2 = (f32[296,128]{1,0:T(8,128)S(1)}, f32[296,128]{1,0:T(8,128)S(1)}, u32[]{:S(2)}, u32[]{:S(2)}) collective-permute-start(f32[296,128]{1,0:T(8,128)S(1)} %get-tuple-element.30), channel_id=1, source_target_pairs={{0,1},{1,2},{2,3},{3,4},{4,5},{5,6},{6,7},{7,8},{8,9},{9,10},{10,1... | collective-permute-start | bytes 454664 | tf_op jit(solution)/shard_map/ppermute | solution.py:362
  18.1 6.6 %collective-permute-start.3 = (f32[240,128]{1,0:T(8,128)S(1)}, f32[240,128]{1,0:T(8,128)S(1)}, u32[]{:S(2)}, u32[]{:S(2)}) collective-permute-start(f32[240,128]{1,0:T(8,128)S(1)} %get-tuple-element.31), channel_id=1, source_target_pairs={{1,0},{2,1},{3,2},{4,3},{5,4},{6,5},{7,6},{8,7},{9,8},{10,9},{11,1... | collective-permute-start | bytes 368648 | tf_op jit(solution)/shard_map/ppermute | solution.py:362
  55.5 19.4 %copy-start.5 = (s32[4608]{0:T(1024)S(1)}, s32[4608]{0:T(1024)}, u32[]{:S(2)}) copy-start(s32[4608]{0:T(1024)} %param.24) | copy-start | bytes 55300
  55.5 19.4 %copy-start.6 = (f32[4608]{0:T(1024)S(1)}, f32[4608]{0:T(1024)}, u32[]{:S(2)}) copy-start(f32[4608]{0:T(1024)} %param.25) | copy-start | bytes 55300

commit v2 on v1

--- a/solution.py
+++ b/solution.py
@@ -16,7 +16,7 @@
 HBM = pl.BlockSpec(memory_space=pltpu.HBM)
 MIB = 1024 * 1024
 BIG = pltpu.CompilerParams(vmem_limit_bytes=16 * MIB)
-MIDDLE = pltpu.CompilerParams(vmem_limit_bytes=8 * MIB)
+MIDDLE = pltpu.CompilerParams(vmem_limit_bytes=12 * MIB)
 SMALL = pltpu.CompilerParams(vmem_limit_bytes=3 * MIB)
 
 
@@ -31,10 +31,10 @@
 
 
 def columns_kernel(
-    forcing_in, loads_in, tracer_in, surface_in, east_flow, north_flow, mix_in, mask_in, c_east_in,
+    place, forcing_in, loads_in, tracer_in, surface_in, east_flow, north_flow, mix_in, mask_in, c_east_in,
     c_north_in, diag_in,
-    b_out, u_out, v_out, west_pack, east_pack, south_rows, north_rows,
-    ratios, forcing, loads, tracer, surface, flow_east, flow_north, mix, mask, c_east, c_north, diag,
+    b_out, u_hbm, v_hbm, west_pack, east_pack, west_inner, east_inner, south_rows, north_rows, inner_rows,
+    u_out, v_out, ratios, forcing, loads, tracer, surface, flow_east, flow_north, mix, mask, c_east, c_north, diag,
     sems,
 ):
     levels, rows, cols = mask.shape
@@ -98,6 +98,8 @@
     total = total + surface[...]
     b_out[...] = total
 
+    southern = place[1] == 0
+    leaving = []
     for k in range(last, -1, -1):
         if k < last:
             ratio = ratios[k]
@@ -107,21 +109,33 @@
         fields = [wet * sol for sol in sols]
         u_out[0, k], u_out[1, k], v_out[0, k], v_out[1, k] = fields
         for q, field in enumerate(fields):
-            south_rows[q * levels + k : q * levels + k + 1, :] = field[0:1]
-            north_rows[q * levels + k : q * levels + k + 1, :] = field[rows - 1 : rows]
-    lane = lanes_of(shape)
+            line = slice(4 * k + q, 4 * k + q + 1)
+            south_rows[line, :] = field[0:1]
+            north_rows[line, :] = field[rows - 1 : rows]
+            inner_rows[line, :] = jnp.where(southern, field[1:2], field[rows - 2 : rows - 1])
+        if k % 10 == 0:
+            at = pl.ds(k, 10)
+            leaving += [
+                fetch(buffer.at[:, at], target.at[:, at])
+                for buffer, target in ((u_out, u_hbm), (v_out, v_hbm))
+            ]
+    lane = lanes_of((1, cols))
     side = slice(LANES, 2 * LANES)
     west_pack[:, side] = zero
     east_pack[:, side] = zero
     for tile in range(2):
-        west, east = zero, zero
+        west, east, west_in, east_in = zero, zero, zero, zero
         for spot in range(4 * min(32, levels - 32 * tile)):
             k, q = 32 * tile + spot // 4, spot % 4
             field = u_out[q, k] if q < 2 else v_out[q - 2, k]
-            west = jnp.where(lane == spot, moved(field, 0, spot), west)
-            east = jnp.where(lane == spot, moved(field, cols - 1, spot), east)
-        west_pack[:, tile * LANES : (tile + 1) * LANES] = west
-        east_pack[:, tile * LANES : (tile + 1) * LANES] = east
+            turned = moved(field, 0, spot)
+            west = jnp.where(lane == spot, turned, west)
+            west_in = jnp.where(lane == (spot + 1) % LANES, turned, west_in)
+            east = jnp.where(lane == (spot - 1) % LANES, turned, east)
+            east_in = jnp.where(lane == (spot - 2) % LANES, turned, east_in)
+        at = slice(tile * LANES, (tile + 1) * LANES)
+        west_pack[:, at], east_pack[:, at] = west, moved(east, 0, 1)
+        west_inner[:, at], east_inner[:, at] = moved(west_in, 1, 0), moved(east_in, 0, 2)
     value = east_pack[:, side]
     for k in range(levels):
         value = jnp.where(lane == 72 + k, moved(flow_east[k], cols - 1, 72 + k), value)
@@ -133,6 +147,8 @@
         west = jnp.where(here, moved(field, 0, 4 * a), west)
         east = jnp.where(here, moved(field, cols - 3, 4 * a), east)
     west_pack[:, 2 * LANES :], east_pack[:, 2 * LANES :] = west, east
+    for copy in leaving:
+        copy.wait()
 
 
 def rows_kernel(b, c_east, c_north, diag, west_in, east_in, _s, _n, south_rows, north_rows, side):
@@ -148,8 +164,44 @@
         north_rows[8 * a : 8 * a + 8, :] = field[rows - BLOCK :, :]
 
 
-def krylov_kernel(b, c_east, c_north, diag, side, south_in, north_in, v0_out, v1_out, v2_out, sums):
-    rows = b.shape[0]
+def tall_transpose(value):
+    rows, wide = value.shape
+    if rows < LANES:
+        value = jnp.concatenate([value, jnp.zeros((LANES - rows, wide), jnp.float32)], axis=0)
+    tiles = [jnp.transpose(value[:, at : at + LANES]) for at in range(0, wide, LANES)]
+    return jnp.concatenate(tiles, axis=0)
+
+
+def rim_parts(center, inner, low, high, face_high, face_low, face_inner, last, factors):
+    lane = lanes_of(center.shape)
+    which = lax.broadcasted_iota(jnp.int32, center.shape, 0) & 3
+    low = jnp.where(lane == 0, low, pltpu.roll(center, 1, 1))
+    high = jnp.where(lane == last, high, pltpu.roll(center, LANES - 1, 1))
+    face_low = jnp.where(lane == 0, face_low, pltpu.roll(face_high, 1, 1))
+    parts = []
+    for n, (f_center, f_inner, f_low, f_high) in enumerate(factors):
+        if n == 0:
+            f_center, f_inner, f_low, f_high = (
+                jnp.where(which < 2, 1.0, f) for f in (f_center, f_inner, f_low, f_high)
+            )
+        here = center * f_center
+        parts.append(
+            here
+            + 0.5 * face_high * (high * f_high - here)
+            + 0.5 * face_low * (here - low * f_low)
+            + 0.5 * face_inner * (inner * f_inner - here)
+        )
+    rows = center.shape[0]
+    return parts[0], jnp.where(which >= 2, parts[1], pltpu.roll(parts[2], rows - 2, 0))
+
+
+def krylov_kernel(
+    place, b, c_east, c_north, diag, side, south_in, north_in, west_in, east_in,
+    flow_east, flow_north, west_pack, east_pack, west_inner, east_inner, south_rows, north_rows, inner_rows,
+    v0_out, v1_out, v2_out, out,
+    high_buf, low_buf, face_buf, turned,
+):
+    levels, rows, cols = flow_east.shape
     sides = jnp.concatenate([south_in[232:240, :], side[...], north_in[232:240, :]], axis=0)
     lane = lanes_of(sides.shape)
     full = []
@@ -176,17 +228,112 @@
             + cs * (vec - pltpu.roll(vec, 1, 0))
         )
         vecs.append(vec)
-    v0_out[...], v1_out[...], v2_out[...] = vecs[:3]
-    inner = [value[BLOCK : BLOCK + rows, :LANES] for value in vecs]
+    outs = (v0_out, v1_out, v2_out)
+    for target, value in zip(outs, vecs):
+        target[...] = value
+    tiles = [value[BLOCK : BLOCK + rows, :LANES] for value in vecs]
     spot = lanes_of((1, LANES))
     row = jnp.zeros((1, LANES), jnp.float32)
     for n, (i, j) in enumerate(GRAM):
-        part = jnp.sum(inner[i] * inner[j], axis=0, keepdims=True)
+        part = jnp.sum(tiles[i] * tiles[j], axis=0, keepdims=True)
         row = jnp.where(spot == n, jnp.sum(part, axis=1, keepdims=True), row)
-    sums[...] = row
-
-
-def krylov_weights(gram):
+    groups = out.shape[0]
+    out[...] = jnp.zeros_like(out)
+    for group in range(groups):
+        out[group, 96:97, :] = row
+    count = 4 * levels
+    used = -(-count // 32)
+
+    def emit(parts, first, step):
+        for group in range(used):
+            length = min(32, count - 32 * group)
+            for n, part in enumerate(parts):
+                out[group, first + n * step : first + n * step + length, :] = part[
+                    32 * group : 32 * group + length
+                ]
+
+    @pl.when((place[1] == 0) | (place[1] == place[3] - 1))
+    def _():
+        south = place[1] == 0
+        at = jnp.where(south, 0, rows - 1)
+        at_in = jnp.where(south, 1, rows - 2)
+        sign = jnp.where(south, 1.0, -1.0)
+        west_turned = tall_transpose(west_in[:, : 2 * LANES])
+        west_turned = jnp.where(south, west_turned, moved(west_turned, rows - 1, 0))
+        turned[...] = west_turned
+        east_turned = tall_transpose(east_in[:, : 2 * LANES])
+        high = jnp.where(
+            south, moved(east_turned, 0, cols - 1), moved(east_turned, rows - 1, cols - 1)
+        )
+        for k in range(levels):
+            four = slice(4 * k, 4 * k + 4)
+            high_buf[four, :] = jnp.broadcast_to(flow_east[k, pl.ds(at, 1), :], (4, cols))
+            low_buf[four, :] = jnp.broadcast_to(turned[count + k : count + k + 1, :], (4, cols))
+            face_buf[four, :] = jnp.broadcast_to(
+                sign * flow_north[k, pl.ds(jnp.where(south, 0, rows - 2), 1), :], (4, cols)
+            )
+        factors = []
+        for value in outs:
+            line = value[pl.ds(BLOCK + at, 1), :]
+            factors.append((
+                line[:, :cols], value[pl.ds(BLOCK + at_in, 1), :][:, :cols],
+                pltpu.roll(line, 1, 1)[:, :cols], pltpu.roll(line, wide - 1, 1)[:, :cols],
+            ))
+        parts = rim_parts(
+            jnp.where(south, south_rows[0:count, :], north_rows[0:count, :]),
+            inner_rows[...], west_turned[0:count], high[0:count],
+            high_buf[...], low_buf[...], face_buf[...], cols - 1, factors,
+        )
+        emit(parts, 0, 32)
+
+    @pl.when((place[0] == 0) | (place[0] == place[2] - 1))
+    def _():
+        western = place[0] == 0
+        at = jnp.where(western, 0, cols - 1)
+        at_in = jnp.where(western, 1, cols - 2)
+        sign = jnp.where(western, 1.0, -1.0)
+        flat = lanes_of((rows, cols))
+        norths = jnp.zeros((rows, cols), jnp.float32)
+        easts = norths
+        for k in range(levels):
+            mark = jnp.where(western, k, (k - 1) % LANES)
+            norths = jnp.where(flat == mark, moved(flow_north[k], 0, k), norths)
+            mark = jnp.where(western, k, (k - 2) % LANES)
+            easts = jnp.where(flat == mark, moved(flow_east[k], 0, k), easts)
+        norths = jnp.where(western, norths, pltpu.roll(norths, 1, 1))
+        easts = jnp.where(western, moved(easts, 0, 64), moved(easts, 0, 66))
+        turned[0:LANES, :] = tall_transpose(jnp.where(flat < 64, norths, easts))
+        for k in range(levels):
+            four = slice(4 * k, 4 * k + 4)
+            high_buf[four, :] = jnp.broadcast_to(turned[k : k + 1, :], (4, cols))
+            face_buf[four, :] = jnp.broadcast_to(sign * turned[64 + k : 65 + k, :], (4, cols))
+            low_buf[four, :] = jnp.broadcast_to(south_in[240 + k : 241 + k, :], (4, cols))
+
+        def line_up(value, target):
+            return jnp.where(western, moved(value, 0, target), moved(value, cols - 1, target))
+
+        factors = []
+        for value in outs:
+            turned[0:LANES, :] = tall_transpose(value[:, :cols])
+            line = pltpu.roll(turned[pl.ds(at, 1), :], LANES - BLOCK, 1)
+            factors.append((
+                line, pltpu.roll(turned[pl.ds(at_in, 1), :], LANES - BLOCK, 1),
+                pltpu.roll(line, 1, 1), pltpu.roll(line, LANES - 1, 1),
+            ))
+        center = jnp.where(western, west_pack[:, : 2 * LANES], east_pack[:, : 2 * LANES])
+        inside = jnp.where(western, west_inner[...], east_inner[...])
+        first, second = rim_parts(
+            tall_transpose(center)[0:count], tall_transpose(inside)[0:count],
+            line_up(south_in[0:count, :], 0), line_up(north_in[0:count, :], rows - 1),
+            high_buf[...], line_up(low_buf[...], 0), face_buf[...], rows - 1, factors,
+        )
+        half = lanes_of(first.shape) < 64
+        emit((jnp.where(half, first, moved(second, 0, 64)),), 64, 0)
+
+
+def krylov_weights(sums):
+    gram = {pair: sums[0:1, n : n + 1] for n, pair in enumerate(GRAM)}
+
     def form(left, right):
         total = 0.0
         for i, x in left.items():
@@ -215,26 +362,28 @@
 
 
 def fields_kernel(
-    place, sums_in, v0, v1, v2, u, v, flow_east, flow_north, west_in, east_in, south_in, north_in,
-    grad_out, x_out, rim, grad, x_full, south_lam, north_lam, lam_buf, flux_buf, sems,
+    sums_in, v0, v1, v2, u_hbm, v_hbm, flow_east, flow_north, west_in, east_in, south_in, north_in,
+    grad_out, x_out, u, v, grad, x_full, south_lam, north_lam, lam_buf, flux_buf, sems,
 ):
     levels, rows, cols = flow_east.shape
     shape = (rows, cols)
+    arrivals = []
+    for n, at in enumerate(range(0, levels, 10)):
+        at = pl.ds(at, 10)
+        arrivals.append([
+            pltpu.make_async_copy(source.at[:, at], target.at[:, at], sems.at[5 + 2 * n + m])
+            for m, (source, target) in enumerate(((u_hbm, u), (v_hbm, v)))
+        ])
+        for copy in arrivals[-1]:
+            copy.start()
     lane = lanes_of(shape)
-    totals = jnp.sum(sums_in[...], axis=0, keepdims=True)
-    gram = {pair: totals[:, n : n + 1] for n, pair in enumerate(GRAM)}
-    weights = krylov_weights(gram)
+    weights = krylov_weights(sums_in)
     x_full[...] = weights[0] * v0[...] + weights[1] * v1[...] + weights[2] * v2[...]
     x = x_full[BLOCK : BLOCK + rows, :cols]
     x_out[...] = x
-    count = 2 * levels
-    south_lam[...] = (
-        south_in[0:count, :] + south_in[count : 2 * count, :] * x_full[BLOCK - 1 : BLOCK, :cols]
-    )
-    north_lam[...] = (
-        north_in[0:count, :]
-        + north_in[count : 2 * count, :] * x_full[BLOCK + rows : BLOCK + rows + 1, :cols]
-    )
+    count = 4 * levels
+    for source, target, at in ((south_in, south_lam, BLOCK - 1), (north_in, north_lam, BLOCK + rows)):
+        target[...] = source[0:count, :] + source[2 : count + 2, :] * x_full[at : at + 1, :cols]
     x_west = x_full[BLOCK : BLOCK + rows, 2 * LANES - 1 :]
     x_east = x_full[BLOCK : BLOCK + rows, LANES : LANES + 1]
     part = lane & 3
@@ -246,12 +395,11 @@
         east = east + pltpu.roll(east, LANES - 2, 1) * x_east
         later = jnp.where(part == 2, pltpu.roll(west, 1, 1), pltpu.roll(east, LANES - 1, 1))
         halos.append(jnp.where(part == 0, west, jnp.where(part == 1, east, later)))
-    rim_row = jnp.where(place[1] == 0, 0, rows - 1)
-    rim_shift = jnp.where(place[0] == 0, 0, 1)
-    rim_base = 104
-    rim[2 * levels : rim_base, :] = jnp.zeros((rim_base - 2 * levels, LANES), jnp.float32)
     copies = []
     for k in range(levels):
+        if k % 10 == 0:
+            for copy in arrivals[k // 10]:
+                copy.wait()
         fe, fn = 0.5 * flow_east[k], 0.5 * flow_north[k]
         fw = jnp.where(
             lane == 0, 0.5 * moved(west_in[:, LANES : 2 * LANES], 72 + k, 0), pltpu.roll(fe, 1, 1)
@@ -260,15 +408,16 @@
         for s in range(2):
             n = s * levels + k
             slot = n % 10
+            line = slice(4 * k + s, 4 * k + s + 1)
             lam = u[s, k] + v[s, k] * x
             lam_buf[slot, 0:rows, :] = lam
-            lam_buf[slot, rows : rows + 1, :] = north_lam[n : n + 1, :]
+            lam_buf[slot, rows : rows + 1, :] = north_lam[line, :]
             halo = moved(halos[k // 32], 4 * (k % 32) + 2 * s, 0)
             east = jnp.where(lane == cols - 1, halo, pltpu.roll(lam, cols - 1, 1))
             west = jnp.where(lane == 0, halo, pltpu.roll(lam, 1, 1))
             flux = fn * (lam_buf[slot, 1 : rows + 1, :] - lam)
             flux_buf[slot, BLOCK : BLOCK + rows, :] = flux
-            flux_buf[slot, BLOCK - 1 : BLOCK, :] = fs * (lam[0:1] - south_lam[n : n + 1, :])
+            flux_buf[slot, BLOCK - 1 : BLOCK, :] = fs * (lam[0:1] - south_lam[line, :])
             out = (
                 lam
                 + fe * (east - lam)
@@ -277,31 +426,26 @@
                 + flux_buf[slot, BLOCK - 1 : BLOCK - 1 + rows, :]
             )
             grad[s, k] = out
-            rim[n : n + 1, :] = grad[s, k, pl.ds(rim_row, 1), :]
         if k % 10 == 9:
             at = pl.ds(k - 9, 10)
             copies.append(
                 pltpu.make_async_copy(grad.at[:, at], grad_out.at[:, at], sems.at[k // 10])
             )
             copies[-1].start()
-    rim_side = jnp.zeros(shape, jnp.float32)
-    for n in range(2 * levels):
-        rolled = moved(grad[n // levels, n % levels], 0, n)
-        rim_side = jnp.where(lane == ((n - rim_shift) & (LANES - 1)), rolled, rim_side)
-    rim[rim_base:, :] = pltpu.roll(rim_side, rim_shift, 1)
     for copy in copies:
         copy.wait()
 
 
-def controls_kernel(place, rims, point_map, point_weight, out, beside):
-    peers, rim_rows, _ = rims.shape
-    depth = 104
-    wide = rim_rows - depth
-    share = 32 * SLOTS
-    row_of = lax.broadcasted_iota(jnp.int32, (share, LANES), 0)
-
-    def spread(ids, weights):
-        return jnp.where(row_of == ids - place[0] * share, weights, 0.0)
+def controls_kernel(place, rims, point_map, point_weight, out, values, hot, halves):
+    peers = rims.shape[0]
+    wide = 40
+    lane = lanes_of((1, LANES))
+
+    def target_of(ids):
+        column = lax.shift_right_logical(lax.shift_right_logical(ids, 6) * 13108, 16)
+        local = ids - 320 * column
+        row = lax.shift_right_logical(local * 6554, 16)
+        return (column >> 2) * 1280 + row * 40 + (column & 3) * 10 + local - 10 * row
 
     def window(ref, start):
         first = start // LANES
@@ -310,56 +454,113 @@
         pair = pltpu.roll(pair, lax.rem(2 * LANES - lax.rem(start, LANES), 2 * LANES), 1)
         return pair[:, :LANES]
 
-    lane = lanes_of((1, LANES))
-    west_at = 2048 + place[1] * wide
-    east_at = 3328 + place[1] * wide
-
     def joined(ref, fill):
-        west, east = window(ref, west_at), window(ref, east_at)
-        east = pltpu.roll(east, wide, 1)
+        west = window(ref, 2048 + place[1] * wide)
+        east = pltpu.roll(window(ref, 3328 + place[1] * wide), wide, 1)
         return jnp.where(lane < wide, west, jnp.where(lane < 2 * wide, east, fill))
 
-    beside[...] = jnp.zeros_like(beside)
-    beside[0:wide, :] = rims[0, depth:, :]
-    beside[wide : 2 * wide, :] = rims[peers - 1, depth:, :]
-    out[...] = lax.dot_general(
-        spread(joined(point_map, -1), joined(point_weight, 0.0)),
-        beside[...],
-        (((1,), (0,)), ((), ())),
-        precision=lax.Precision.HIGHEST,
-        preferred_element_type=jnp.float32,
+    def split(value, at):
+        for piece in range(3):
+            part = value.astype(jnp.bfloat16)
+            values[64 * piece : 64 * piece + 64, at : at + LANES] = part
+            value = value - part.astype(jnp.float32)
+
+    def unfolded(peer):
+        both = rims[peer, 64:96, :]
+        return jnp.concatenate([both, moved(both, 64, 0)], axis=0)
+
+    beside = jnp.where(
+        lane < wide, unfolded(0), jnp.where(lane < 2 * wide, moved(unfolded(peers - 1), 0, wide), 0.0)
     )
-    first = jnp.where(place[1] == 0, 0, peers)
-
-    @pl.when((place[1] == 0) | (place[1] == 31))
-    def _():
-        total = jnp.zeros((share, depth), jnp.float32)
-        for peer in range(peers):
-            ids = point_map[pl.ds(first + peer, 1), :]
-            weights = point_weight[pl.ds(first + peer, 1), :]
-            total = total + lax.dot_general(
-                spread(ids, weights),
-                rims[peer, 0:depth, :],
+    split(beside * joined(point_weight, 0.0), 0)
+    beside_target = target_of(joined(point_map, 0))
+
+    def spread(targets, length):
+        block = 512
+        height = lax.broadcasted_iota(jnp.int32, (block, LANES), 0)
+        for at in range(0, 2560, block):
+            here = slice(at, at + block)
+            for n, target in enumerate(targets):
+                hit = jnp.where(height == target - at, 1.0, 0.0)
+                hot[here, n * LANES : (n + 1) * LANES] = hit.astype(jnp.bfloat16)
+            got = lax.dot_general(
+                hot[here, :length],
+                values[:, :length],
                 (((1,), (1,)), ((), ())),
-                precision=lax.Precision.HIGHEST,
                 preferred_element_type=jnp.float32,
             )
-        out[:, 0:depth] = out[:, 0:depth] + total
+            low = got[:, :LANES]
+            high = jnp.concatenate([got[:, LANES:], got[:, LANES:]], axis=1)
+            halves[here, :] = low + pltpu.roll(low, 64, 1) + high
+
+    rim = (place[1] == 0) | (place[1] == place[3] - 1)
+
+    @pl.when(jnp.logical_not(rim))
+    def _():
+        spread([beside_target], LANES)
+
+    @pl.when(rim)
+    def _():
+        first = jnp.where(place[1] == 0, 0, peers)
+        targets = [beside_target]
+        for peer in range(peers):
+            split(rims[peer, 0:64, :] * point_weight[pl.ds(first + peer, 1), :], (peer + 1) * LANES)
+            targets.append(target_of(point_map[pl.ds(first + peer, 1), :]))
+        spread(targets, (peers + 1) * LANES)
+
+    sums = rims[0, 96:97, :]
+    for peer in range(1, peers):
+        sums = sums + rims[peer, 96:97, :]
+    for row in range(32):
+        at = slice(40 * row, 40 * row + 40)
+        above = slice(1280 + 40 * row, 1320 + 40 * row)
+        out[41 * row : 41 * row + 40, :] = jnp.where(lane < 64, halves[at, :], halves[above, :])
+        out[41 * row + 40 : 41 * row + 41, :] = sums
+
+
+def join_kernel(parts, sums_out, out):
+    total = parts[0:41, :]
+    for at in range(41, parts.shape[0], 41):
+        total = total + parts[at : at + 41, :]
+    sums_out[...] = total[40:41]
+    weights = krylov_weights(total[40:41])
+    value = total[0:40]
+    value = (
+        value
+        + weights[0] * pltpu.roll(value, LANES - 2, 1)
+        + weights[1] * pltpu.roll(value, LANES - 34, 1)
+        + weights[2] * pltpu.roll(value, LANES - 32, 1)
+    )
+    out[0:40, :] = value
+    out[40:80, :] = pltpu.roll(value, 64, 1)
 
 
 def gather_kernel(parts, out):
-    total = parts[0:SLOTS, :]
-    for at in range(SLOTS, parts.shape[0], SLOTS):
-        total = total + parts[at : at + SLOTS, :]
     levels = out.shape[2]
-    out[:, 0, :] = total[0:SLOTS, 0:levels]
-    out[:, 1, :] = total[0:SLOTS, levels : 2 * levels]
+    source = lax.broadcasted_iota(jnp.int32, (LANES, LANES), 0)
+    target = lanes_of((LANES, LANES))
+    total = jnp.zeros((SLOTS, LANES), jnp.float32)
+    for group in range(-(-levels // 8)):
+        wanted = 64 * (source & 3) + 8 * group + (source >> 2)
+        pick = (target == wanted) & ((source & 3) < 2) & (source < 32)
+        total = total + jnp.dot(
+            parts[SLOTS * group : SLOTS * group + SLOTS, :],
+            jnp.where(pick, 1.0, 0.0),
+            precision=lax.Precision.HIGHEST,
+            preferred_element_type=jnp.float32,
+        )
+    out[:, 0, :] = total[:, 0:levels]
+    out[:, 1, :] = total[:, 64 : 64 + levels]
 
 
 def shifted(value, axis, step):
     count = lax.axis_size(axis)
     pairs = [(i, i + step) for i in range(count) if 0 <= i + step < count]
     return lax.ppermute(value, axis, pairs)
+
+
+def in_hbm(value):
+    return pltpu.with_memory_space_constraint(value, pltpu.HBM)
 
 
 def shape_of(*shape):
@@ -383,21 +584,24 @@
 ):
     levels, rows, cols = flow_east.shape
     across, along = lax.axis_size("gx"), lax.axis_size("gy")
-    place = jnp.stack([lax.axis_index("gx"), lax.axis_index("gy")]).astype(jnp.int32)
+    place = jnp.stack([lax.axis_index("gx"), lax.axis_index("gy"), across, along]).astype(jnp.int32)
     point_map = control_map.reshape(-1, LANES)
     point_weight = control_weight.reshape(-1, LANES)
 
     tile = shape_of(rows, cols)
     field = shape_of(2, levels, rows, cols)
-    pack = shape_of(rows, 3 * LANES)
-    kept = pltpu.VMEM(field.shape, jnp.float32)
+    pack, inner = shape_of(rows, 3 * LANES), shape_of(rows, 2 * LANES)
+    count = 4 * levels
+    lines = shape_of(count, cols)
     south_shape, north_shape = shape_of(240, cols), shape_of(296, cols)
-    b, u, v, west_pack, east_pack, south_rows, north_rows = pl.pallas_call(
+    b, u, v, west_pack, east_pack, west_inner, east_inner, south_rows, north_rows, inner_rows = pl.pallas_call(
         columns_kernel,
-        out_shape=(tile, kept, kept, pack, pack, south_shape, north_shape),
-        in_specs=[HBM] * 11,
-        out_specs=(VMEM,) * 7,
+        out_shape=(tile, field, field, pack, pack, inner, inner, south_shape, north_shape, lines),
+        in_specs=[SMEM] + [HBM] * 11,
+        out_specs=(VMEM, HBM, HBM) + (VMEM,) * 7,
         scratch_shapes=[
+            pltpu.VMEM(field.shape, jnp.float32),
+            pltpu.VMEM(field.shape, jnp.float32),
             pltpu.VMEM((levels, rows, cols), jnp.float32),
             pltpu.SMEM((2, levels), jnp.float32),
             pltpu.SMEM((2, levels), jnp.float32),
@@ -415,15 +619,15 @@
         compiler_params=BIG,
         name="columns",
     )(
+        place,
         *(
-            pltpu.with_memory_space_constraint(value, pltpu.HBM)
+            in_hbm(value)
             for value in (
                 surface_forcing, pressure_load, tracer_adjoint, surface_adjoint, flow_east, flow_north,
                 vertical_mix, land_mask, conduct_east, conduct_north, surface_diagonal,
             )
-        )
+        ),
     )
-    stay = [pltpu.with_memory_space_constraint(value, pltpu.VMEM) for value in (u, v)]
     west_pack, place = lax.optimization_barrier((west_pack, place))
     west_in = shifted(east_pack, "gx", 1)
     east_in = shifted(west_pack, "gx", -1)
@@ -441,47 +645,62 @@
     south_in = shifted(north_rows, "gy", 1)
     north_in = shifted(south_rows, "gy", -1)
     full = shape_of(rows + 2 * BLOCK, 2 * LANES)
-    v0, v1, v2, sums = pl.pallas_call(
+    v0, v1, v2, rims = pl.pallas_call(
         krylov_kernel,
-        out_shape=(full, full, full, shape_of(1, LANES)),
-        in_specs=[VMEM] * 7,
+        out_shape=(full, full, full, shape_of(across, 104, LANES)),
+        in_specs=[SMEM] + [VMEM] * 18,
         out_specs=(VMEM,) * 4,
+        scratch_shapes=[pltpu.VMEM((count, cols), jnp.float32)] * 3
+        + [pltpu.VMEM((2 * LANES, LANES), jnp.float32)],
+        compiler_params=MIDDLE,
+        name="krylov",
+    )(
+        place, b, conduct_east, conduct_north, surface_diagonal, side, south_in, north_in, west_in, east_in,
+        flow_east, flow_north, west_pack, east_pack, west_inner, east_inner, south_rows, north_rows, inner_rows,
+    )
+    rims = lax.all_to_all(rims, "gx", 0, 0)
+    parts = pl.pallas_call(
+        controls_kernel,
+        out_shape=shape_of(along * 41, LANES),
+        in_specs=[SMEM] + [VMEM] * 3,
+        out_specs=VMEM,
+        scratch_shapes=[
+            pltpu.VMEM((192, (across + 1) * LANES), jnp.bfloat16),
+            pltpu.VMEM((2560, (across + 1) * LANES), jnp.bfloat16),
+            pltpu.VMEM((2560, LANES), jnp.float32),
+        ],
+        compiler_params=MIDDLE,
+        name="controls",
+    )(place, rims, point_map, point_weight)
+    parts = lax.all_to_all(parts.reshape(along, 1, 41 * LANES), "gy", 0, 0)
+    sums, joined = pl.pallas_call(
+        join_kernel,
+        out_shape=(shape_of(1, LANES), shape_of(across * SLOTS, LANES)),
+        in_specs=[VMEM],
+        out_specs=(VMEM,) * 2,
         compiler_params=SMALL,
-        name="krylov",
-    )(b, conduct_east, conduct_north, surface_diagonal, side, south_in, north_in)
-    everyone = across * along
-    sums = jnp.broadcast_to(sums[None], (everyone, 1, LANES))
-    sums = lax.all_to_all(sums, ("gx", "gy"), 0, 0).reshape(everyone, LANES)
-    rim_rows = 104 + rows
-    tracer_grad, x, rim = pl.pallas_call(
+        name="join",
+    )(parts.reshape(along * 41, LANES))
+    joined = lax.all_to_all(joined.reshape(across, 1, SLOTS * LANES), "gx", 0, 0)
+    tracer_grad, x = pl.pallas_call(
         fields_kernel,
-        out_shape=(field, tile, shape_of(rim_rows, LANES)),
-        in_specs=[SMEM] + [VMEM] * 12,
-        out_specs=(HBM, VMEM, VMEM),
+        out_shape=(field, tile),
+        in_specs=[VMEM] * 4 + [HBM] * 2 + [VMEM] * 6,
+        out_specs=(HBM, VMEM),
         scratch_shapes=[
+            pltpu.VMEM(field.shape, jnp.float32),
+            pltpu.VMEM(field.shape, jnp.float32),
             pltpu.VMEM((2, levels, rows, cols), jnp.float32),
             pltpu.VMEM(full.shape, jnp.float32),
-            pltpu.VMEM((2 * levels, cols), jnp.float32),
-            pltpu.VMEM((2 * levels, cols), jnp.float32),
+            pltpu.VMEM((count, cols), jnp.float32),
+            pltpu.VMEM((count, cols), jnp.float32),
             pltpu.VMEM((10, rows + BLOCK, cols), jnp.float32),
             pltpu.VMEM((10, rows + BLOCK, cols), jnp.float32),
-            pltpu.SemaphoreType.DMA((levels // 10,)),
+            pltpu.SemaphoreType.DMA((15,)),
         ],
         compiler_params=MIDDLE,
         name="fields",
-    )(place, sums, v0, v1, v2, *stay, flow_east, flow_north, west_in, east_in, south_in, north_in)
-    rims = lax.all_to_all(jnp.broadcast_to(rim[None], (across, rim_rows, LANES)), "gx", 0, 0)
-    parts = pl.pallas_call(
-        controls_kernel,
-        out_shape=shape_of(along * SLOTS, LANES),
-        in_specs=[SMEM] + [VMEM] * 3,
-        out_specs=VMEM,
-        scratch_shapes=[pltpu.VMEM((LANES, LANES), jnp.float32)],
-        compiler_params=SMALL,
-        name="controls",
-    )(place, rims, point_map, point_weight)
-    parts = lax.all_to_all(parts.reshape(along, 1, SLOTS * LANES), "gy", 0, 0)
-    parts = parts.reshape(along * SLOTS, LANES)
+    )(sums, v0, v1, v2, in_hbm(u), in_hbm(v), flow_east, flow_north, west_in, east_in, south_in, north_in)
     control_grad = pl.pallas_call(
         gather_kernel,
         out_shape=shape_of(SLOTS, 2, levels),
@@ -489,7 +708,7 @@
         out_specs=VMEM,
         compiler_params=SMALL,
         name="gather",
-    )(parts)
+    )(joined.reshape(across * SLOTS, LANES))
     return tracer_grad, x, jnp.transpose(control_grad, (1, 2, 0))
 
 

time: 90.7 us -> 88.4 us (0.975)
  blocking collectives: 56.6 us -> 44.4 us
  starting transfers between devices: 10.9 us -> 16.8 us
  Pallas kernels: 15.3 us -> 19.5 us
    all_to_all x3 -> x2, blocking collectives: 56.6 us -> 44.4 us  [the longest x1 30.1 us: per_device(): parts = lax.all_to_all(parts.reshape(along, 1, 41 * LANES), 'gy', 0, 0)]
    all_to_all x0 -> x1, starting transfers between devices: none -> 5.72 us  [per_device(): lax.all_to_all(joined.reshape(across, 1, SLOTS * LANES), 'gx', 0, 0)]
    pallas_call x4 -> x5, Pallas kernels: 14.5 us -> 18.4 us  [the longest x1 7.38 us: per_device(): pl.pallas_call(columns_kernel, out_shape=(tile, field, field, pack, pack,...]
  transfers between devices with their start and end apart: 4 -> 5, of which waited for: 2 -> 2; matrix products, arithmetic and copies ran while one was open for 0% -> 0% of each run, Pallas kernels for 0% -> 6%
where the time goes in v2:
time: 88.4 us; the launch traced here: 88.1 us
  blocking collectives  44.4 us (50%)
  Pallas kernels  19.5 us (22%)
  starting transfers between devices  16.8 us (19%)
  waiting for transfers between devices  6.57 us (7%)
    all_to_all x1, blocking collectives, per_device(): parts = lax.all_to_all(parts.reshape(along, 1, 41 * LANES), 'gy', 0, 0)  30.1 us
    all_to_all x1, blocking collectives, per_device(): rims = lax.all_to_all(rims, 'gx', 0, 0)  14.3 us
    ppermute x4, starting transfers between devices, shifted(): return lax.ppermute(value, axis, pairs)  11.1 us
    pallas_call x1, Pallas kernels, per_device(): pl.pallas_call(columns_kernel, out_shape=(tile, field, field, pack, pack,...  7.38 us
    ppermute x4, waiting for transfers between devices, shifted(): return lax.ppermute(value, axis, pairs)  6.57 us
    all_to_all x1, starting transfers between devices, per_device(): lax.all_to_all(joined.reshape(across, 1, SLOTS * LANES), 'gx', 0, 0)  5.72 us
    pallas_call x1, Pallas kernels, per_device(): pl.pallas_call(fields_kernel, out_shape=(field, tile), in_specs=[VMEM] *...  5.55 us
    pallas_call x1, Pallas kernels, per_device(): pl.pallas_call(controls_kernel, out_shape=shape_of(along * 41, LANES), in...  3.13 us
  transfers between devices with their start and end apart: 5, of which 2 were waited for; matrix products, arithmetic and copies ran while one was open for 0% of the time, Pallas kernels for 6%

profile of v2, /device:TPU:1, one launch (start us, length us, event | category | flops | bytes accessed | tf_op | source)
XLA Modules:
  0.0 88.1 jit_solution(13628791302906186067)
XLA Ops:
  0.6 0.1 pad_add_fusion.place
  0.7 0.0 copy-start.4
  0.7 0.0 copy-start.5
  0.7 0.0 copy-start.6
  0.7 0.0 copy-start
  0.7 0.0 copy-start.1
  0.7 7.4 %columns.1 = (f32[40,128]{1,0:T(8,128)S(1)}, f32[2,50,40,128]{3,2,1,0:T(8,128)S(1)}, f32[2,50,40,128]{3,2,1,0:T(8,128)S(1)}, f32[40,384]{1,0:T(8,128)S(1)}, f32[...) custom-call(s32[4]{0:T(128)S(1)} %pad_add_fusion.place, ...), custom_call_target="tpu_custom_call" | custom-call | tf_op jit(solution)/shard_map/columns/pallas_call | solution.py:597
  8.1 0.0 copy-start.2
  8.1 0.0 copy-start.3
  8.1 5.1 %collective-permute-start.1 = (f32[40,384]{1,0:T(8,128)S(1)}, f32[40,384]{1,0:T(8,128)S(1)}, u32[]{:S(2)}, u32[]{:S(2)}) collective-permute-start(f32[40,384]{1,0:T(8,128)S(1)} %get-tuple-element.30.west_pack), channel_id=1, source_target_pairs={{32,0},{64,32},{96,64},{128,96},{160,128},{192,160},{224,192},{33,... | collective-permute-start | bytes 184328 | tf_op jit(solution)/shard_map/ppermute | solution.py:559
  13.3 1.9 %collective-permute-start = (f32[40,384]{1,0:T(8,128)S(1)}, f32[40,384]{1,0:T(8,128)S(1)}, u32[]{:S(2)}, u32[]{:S(2)}) collective-permute-start(f32[40,384]{1,0:T(8,128)S(1)} %get-tuple-element.29.east_pack), channel_id=1, source_target_pairs={{0,32},{32,64},{64,96},{96,128},{128,160},{160,192},{192,224},{1,3... | collective-permute-start | bytes 184328 | tf_op jit(solution)/shard_map/ppermute | solution.py:559
  15.2 0.0 collective-permute-done.1.east_in
  15.2 1.3 %collective-permute-done.west_in = f32[40,384]{1,0:T(8,128)S(1)} collective-permute-done((f32[40,384]{1,0:T(8,128)S(1)}, f32[40,384]{1,0:T(8,128)S(1)}, u32[]{:S(2)}, u32[]{:S(2)}) %collective-permute-start) | collective-permute-done | bytes 61472 | tf_op jit(solution)/shard_map/ppermute | solution.py:559
  16.5 0.0 copy-done.4
  16.5 0.0 copy-done.5
  16.5 0.0 copy-done.6
  16.5 0.1 rows.1
  16.6 0.0 copy-start.7
  16.6 0.0 copy-start.8
  16.6 2.7 %collective-permute-start.2 = (f32[296,128]{1,0:T(8,128)S(1)}, f32[296,128]{1,0:T(8,128)S(1)}, u32[]{:S(2)}, u32[]{:S(2)}) collective-permute-start(f32[296,128]{1,0:T(8,128)S(1)} %get-tuple-element.34.north_rows), channel_id=1, source_target_pairs={{0,1},{1,2},{2,3},{3,4},{4,5},{5,6},{6,7},{7,8},{8,9},{9,10},{10,1... | collective-permute-start | bytes 454664 | tf_op jit(solution)/shard_map/ppermute | solution.py:559
  19.3 1.3 %collective-permute-start.3 = (f32[240,128]{1,0:T(8,128)S(1)}, f32[240,128]{1,0:T(8,128)S(1)}, u32[]{:S(2)}, u32[]{:S(2)}) collective-permute-start(f32[240,128]{1,0:T(8,128)S(1)} %get-tuple-element.35.south_rows), channel_id=1, source_target_pairs={{1,0},{2,1},{3,2},{4,3},{5,4},{6,5},{7,6},{8,7},{9,8},{10,9},{11,1... | collective-permute-start | bytes 368648 | tf_op jit(solution)/shard_map/ppermute | solution.py:559
  20.6 5.3 %collective-permute-done.3.north_in = f32[240,128]{1,0:T(8,128)S(1)} collective-permute-done((f32[240,128]{1,0:T(8,128)S(1)}, f32[240,128]{1,0:T(8,128)S(1)}, u32[]{:S(2)}, u32[]{:S(2)}) %collective-permute-start.3) | collective-permute-done | bytes 122912 | tf_op jit(solution)/shard_map/ppermute | solution.py:559
  25.9 0.0 collective-permute-done.2.south_in
  25.9 0.0 copy-done
  25.9 0.0 copy-done.1
  25.9 1.5 %krylov.1 = (f32[56,256]{1,0:T(8,128)S(1)}, f32[56,256]{1,0:T(8,128)S(1)}, f32[56,256]{1,0:T(8,128)S(1)}, f32[8,104,128]{2,1,0:T(8,128)S(1)}) custom-call(s32[4]{0:T(128)S(1)} %pad_add_fusion.place, f32[40,128]{1,0:T(8,128)S(1)} %get-tuple-element.28.b, f32[40,128]{1,0:T(8,128)S(1)} %copy-done.4, f32[40,128]{1,0:T(8,128)S(1)} %copy-done.5, ...), custom_call_target="tpu_custom_call" | custom-call | tf_op jit(solution)/shard_map/krylov/pallas_call | solution.py:648
  27.4 14.3 %all_to_all.15.rims = f32[8,104,128]{2,1,0:T(8,128)S(1)} all-to-all(f32[8,104,128]{2,1,0:T(8,128)S(1)} %get-tuple-element.39), channel_id=1, replica_groups=mesh['gx'=8,'gy'=32] {'gx'}, dimensions={0} | all-to-all | bytes 851968 | tf_op jit(solution)/shard_map/all_to_all | solution.py:661
  41.7 0.0 copy-done.2
  41.7 0.0 copy-done.3
  41.7 0.0 copy-done.7
  41.7 0.0 copy-done.8
  41.7 3.1 %controls.1 = f32[1312,128]{1,0:T(8,128)S(1)} custom-call(s32[4]{0:T(128)S(1)} %pad_add_fusion.place, f32[8,104,128]{2,1,0:T(8,128)S(1)} %all_to_all.15.rims, s32[36,128]{1,0:T(8,128)S(1)} %bitcast.12, f32[36,128]{1,0:T(8,128)S(1)} %bitcast.13), custom_call_target="tpu_custom_call" | custom-call | tf_op jit(solution)/shard_map/controls/pallas_call | solution.py:662
  44.9 30.1 %all_to_all.16 = f32[32,1,5248]{2,1,0:T(1,128)S(1)} all-to-all(f32[32,1,5248]{2,1,0:T(1,128)S(1)} %bitcast.10), channel_id=1, replica_groups=mesh['gx'=8,'gy'=32] {'gy'}, dimensions={0} | all-to-all | bytes 1343488 | tf_op jit(solution)/shard_map/all_to_all | solution.py:675
  74.9 0.9 %join.1 = (f32[1,128]{1,0:T(1,128)S(1)}, f32[80,128]{1,0:T(8,128)}) custom-call(f32[1312,128]{1,0:T(8,128)S(1)} %bitcast.9), custom_call_target="tpu_custom_call" | custom-call | tf_op jit(solution)/shard_map/join/pallas_call | solution.py:676
  75.8 5.7 %all-to-all-start.2 = ((f32[8,1,1280]{2,1,0:T(1,128)}), f32[8,1,1280]{2,1,0:T(1,128)S(1)}, u32[]{:S(2)}, u32[]{:S(2)}) async-start(f32[8,1,1280]{2,1,0:T(1,128)} %bitcast.6), calls=%async_computation.2 | async-start | bytes 81920 | tf_op jit(solution)/shard_map/all_to_all | solution.py:684
  81.5 5.6 %fields.1 = (f32[2,50,40,128]{3,2,1,0:T(8,128)}, f32[40,128]{1,0:T(8,128)}) custom-call(f32[1,128]{1,0:T(1,128)S(1)} %get-tuple-element.40.sums_in, f32[56,256]{1,0:T(8,128)S(1)} %get-tuple-element.41.v0, f32[56,256]{1,0:T(8,128)S(1)} %get-tuple-element.42.v1, f32[56,256]{1,0:T(8,128)S(1)} %get-tuple-element.43.v2, f32[2,50,40,128]{3,2,1,0:T(8,128)} %copy-done.2, ...), custom_call_target="tpu_custom_call" | custom-call | tf_op jit(solution)/shard_map/fields/pallas_call | solution.py:685
  87.1 0.0 all-to-all-done.2
  87.1 0.9 %gather.1 = f32[10,2,50]{2,1,0:T(2,128)} custom-call(f32[80,128]{1,0:T(8,128)S(1)} %bitcast.11), custom_call_target="tpu_custom_call" | custom-call | tf_op jit(solution)/shard_map/gather/pallas_call | solution.py:704
Async XLA Ops:
  0.7 15.8 %copy-start.4 = (f32[40,128]{1,0:T(8,128)S(1)}, f32[40,128]{1,0:T(8,128)}, u32[]{:S(2)}) copy-start(f32[40,128]{1,0:T(8,128)} %c_east.3) | copy-start | bytes 61444
  0.7 15.8 %copy-start.5 = (f32[40,128]{1,0:T(8,128)S(1)}, f32[40,128]{1,0:T(8,128)}, u32[]{:S(2)}) copy-start(f32[40,128]{1,0:T(8,128)} %c_north.3) | copy-start | bytes 61444
  0.7 15.8 %copy-start.6 = (f32[40,128]{1,0:T(8,128)S(1)}, f32[40,128]{1,0:T(8,128)}, u32[]{:S(2)}) copy-start(f32[40,128]{1,0:T(8,128)} %diag.3) | copy-start | bytes 61444
  0.7 25.2 %copy-start = (f32[50,40,128]{2,1,0:T(8,128)S(1)}, f32[50,40,128]{2,1,0:T(8,128)}, u32[]{:S(2)}) copy-start(f32[50,40,128]{2,1,0:T(8,128)} %flow_east.3) | copy-start | bytes 3072004
  0.7 25.2 %copy-start.1 = (f32[50,40,128]{2,1,0:T(8,128)S(1)}, f32[50,40,128]{2,1,0:T(8,128)}, u32[]{:S(2)}) copy-start(f32[50,40,128]{2,1,0:T(8,128)} %flow_north.3) | copy-start | bytes 3072004
  8.1 33.6 %copy-start.2 = (f32[2,50,40,128]{3,2,1,0:T(8,128)}, f32[2,50,40,128]{3,2,1,0:T(8,128)S(1)}, u32[]{:S(2)}) copy-start(f32[2,50,40,128]{3,2,1,0:T(8,128)S(1)} %get-tuple-element.44.u_hbm) | copy-start | bytes 6144004
  8.1 33.6 %copy-start.3 = (f32[2,50,40,128]{3,2,1,0:T(8,128)}, f32[2,50,40,128]{3,2,1,0:T(8,128)S(1)}, u32[]{:S(2)}) copy-start(f32[2,50,40,128]{3,2,1,0:T(8,128)S(1)} %get-tuple-element.45.v_hbm) | copy-start | bytes 6144004
  8.1 7.1 %collective-permute-start.1 = (f32[40,384]{1,0:T(8,128)S(1)}, f32[40,384]{1,0:T(8,128)S(1)}, u32[]{:S(2)}, u32[]{:S(2)}) collective-permute-start(f32[40,384]{1,0:T(8,128)S(1)} %get-tuple-element.30.west_pack), channel_id=1, source_target_pairs={{32,0},{64,32},{96,64},{128,96},{160,128},{192,160},{224,192},{33,... | collective-permute-start | bytes 184328 | tf_op jit(solution)/shard_map/ppermute | solution.py:559
  13.3 3.2 %collective-permute-start = (f32[40,384]{1,0:T(8,128)S(1)}, f32[40,384]{1,0:T(8,128)S(1)}, u32[]{:S(2)}, u32[]{:S(2)}) collective-permute-start(f32[40,384]{1,0:T(8,128)S(1)} %get-tuple-element.29.east_pack), channel_id=1, source_target_pairs={{0,32},{32,64},{64,96},{96,128},{128,160},{160,192},{192,224},{1,3... | collective-permute-start | bytes 184328 | tf_op jit(solution)/shard_map/ppermute | solution.py:559
  16.6 25.1 %copy-start.7 = (s32[4608]{0:T(1024)S(1)}, s32[4608]{0:T(1024)}, u32[]{:S(2)}) copy-start(s32[4608]{0:T(1024)} %param.24) | copy-start | bytes 55300
  16.6 25.1 %copy-start.8 = (f32[4608]{0:T(1024)S(1)}, f32[4608]{0:T(1024)}, u32[]{:S(2)}) copy-start(f32[4608]{0:T(1024)} %param.25) | copy-start | bytes 55300
  16.6 9.3 %collective-permute-start.2 = (f32[296,128]{1,0:T(8,128)S(1)}, f32[296,128]{1,0:T(8,128)S(1)}, u32[]{:S(2)}, u32[]{:S(2)}) collective-permute-start(f32[296,128]{1,0:T(8,128)S(1)} %get-tuple-element.34.north_rows), channel_id=1, source_target_pairs={{0,1},{1,2},{2,3},{3,4},{4,5},{5,6},{6,7},{7,8},{8,9},{9,10},{10,1... | collective-permute-start | bytes 454664 | tf_op jit(solution)/shard_map/ppermute | solution.py:559
  19.3 6.6 %collective-permute-start.3 = (f32[240,128]{1,0:T(8,128)S(1)}, f32[240,128]{1,0:T(8,128)S(1)}, u32[]{:S(2)}, u32[]{:S(2)}) collective-permute-start(f32[240,128]{1,0:T(8,128)S(1)} %get-tuple-element.35.south_rows), channel_id=1, source_target_pairs={{1,0},{2,1},{3,2},{4,3},{5,4},{6,5},{7,6},{8,7},{9,8},{10,9},{11,1... | collective-permute-start | bytes 368648 | tf_op jit(solution)/shard_map/ppermute | solution.py:559
  75.8 11.3 %all-to-all-start.2 = ((f32[8,1,1280]{2,1,0:T(1,128)}), f32[8,1,1280]{2,1,0:T(1,128)S(1)}, u32[]{:S(2)}, u32[]{:S(2)}) async-start(f32[8,1,1280]{2,1,0:T(1,128)} %bitcast.6), calls=%async_computation.2 | async-start | bytes 81920 | tf_op jit(solution)/shard_map/all_to_all | solution.py:684

commit v3 on v2

--- a/solution.py
+++ b/solution.py
@@ -10,6 +10,7 @@
 SLOTS = 10
 LANES = 128
 BLOCK = 8
+GROUP = 25
 GRAM = ((0, 0), (0, 1), (0, 2), (0, 3), (1, 1), (1, 2), (1, 3), (2, 2), (2, 3))
 VMEM = pl.BlockSpec(memory_space=pltpu.VMEM)
 SMEM = pl.BlockSpec(memory_space=pltpu.SMEM)
@@ -237,20 +238,16 @@
     for n, (i, j) in enumerate(GRAM):
         part = jnp.sum(tiles[i] * tiles[j], axis=0, keepdims=True)
         row = jnp.where(spot == n, jnp.sum(part, axis=1, keepdims=True), row)
-    groups = out.shape[0]
     out[...] = jnp.zeros_like(out)
-    for group in range(groups):
-        out[group, 96:97, :] = row
+    for at in range(0, out.shape[0], GROUP):
+        out[at + GROUP - 1 : at + GROUP, :] = row
     count = 4 * levels
-    used = -(-count // 32)
-
-    def emit(parts, first, step):
-        for group in range(used):
-            length = min(32, count - 32 * group)
+
+    def emit(parts, first):
+        for group in range(count // BLOCK):
             for n, part in enumerate(parts):
-                out[group, first + n * step : first + n * step + length, :] = part[
-                    32 * group : 32 * group + length
-                ]
+                at = GROUP * group + first + n * BLOCK
+                out[at : at + BLOCK, :] = part[BLOCK * group : BLOCK * group + BLOCK]
 
     @pl.when((place[1] == 0) | (place[1] == place[3] - 1))
     def _():
@@ -284,7 +281,7 @@
             inner_rows[...], west_turned[0:count], high[0:count],
             high_buf[...], low_buf[...], face_buf[...], cols - 1, factors,
         )
-        emit(parts, 0, 32)
+        emit(parts, 0)
 
     @pl.when((place[0] == 0) | (place[0] == place[2] - 1))
     def _():
@@ -328,7 +325,7 @@
             high_buf[...], line_up(low_buf[...], 0), face_buf[...], rows - 1, factors,
         )
         half = lanes_of(first.shape) < 64
-        emit((jnp.where(half, first, moved(second, 0, 64)),), 64, 0)
+        emit((jnp.where(half, first, moved(second, 0, 64)),), 2 * BLOCK)
 
 
 def krylov_weights(sums):
@@ -436,119 +433,102 @@
         copy.wait()
 
 
-def controls_kernel(place, rims, point_map, point_weight, out, values, hot, halves):
-    peers = rims.shape[0]
-    wide = 40
+def controls_kernel(place, rims, point_map, point_weight, out, values, hot, total):
+    peers, high, wide = out.shape
     lane = lanes_of((1, LANES))
-
-    def target_of(ids):
+    rows = 40
+    tiles = rows * (rims.shape[0] // GROUP) // LANES
+
+    def point_tile(n, value, row):
+        value = value * point_weight[pl.ds(row, 1), :]
+        ids = point_map[pl.ds(row, 1), :]
         column = lax.shift_right_logical(lax.shift_right_logical(ids, 6) * 13108, 16)
-        local = ids - 320 * column
-        row = lax.shift_right_logical(local * 6554, 16)
-        return (column >> 2) * 1280 + row * 40 + (column & 3) * 10 + local - 10 * row
-
-    def window(ref, start):
-        first = start // LANES
-        second = jnp.minimum(first + 1, ref.shape[0] - 1)
-        pair = jnp.concatenate([ref[pl.ds(first, 1), :], ref[pl.ds(second, 1), :]], axis=1)
-        pair = pltpu.roll(pair, lax.rem(2 * LANES - lax.rem(start, LANES), 2 * LANES), 1)
-        return pair[:, :LANES]
-
-    def joined(ref, fill):
-        west = window(ref, 2048 + place[1] * wide)
-        east = pltpu.roll(window(ref, 3328 + place[1] * wide), wide, 1)
-        return jnp.where(lane < wide, west, jnp.where(lane < 2 * wide, east, fill))
-
-    def split(value, at):
+        here = slice(n * LANES, (n + 1) * LANES)
         for piece in range(3):
-            part = value.astype(jnp.bfloat16)
-            values[64 * piece : 64 * piece + 64, at : at + LANES] = part
-            value = value - part.astype(jnp.float32)
-
-    def unfolded(peer):
-        both = rims[peer, 64:96, :]
-        return jnp.concatenate([both, moved(both, 64, 0)], axis=0)
-
-    beside = jnp.where(
-        lane < wide, unfolded(0), jnp.where(lane < 2 * wide, moved(unfolded(peers - 1), 0, wide), 0.0)
+            part = value.astype(jnp.bfloat16).astype(jnp.float32)
+            for peer in range(peers):
+                at = high * (3 * peer + piece)
+                mine = jnp.where(column == peer, part, 0.0)
+                values[at : at + high, here] = mine.astype(jnp.bfloat16)
+            value = value - part
+        target = ids - 32 * SLOTS * column
+        target = jnp.transpose(jnp.broadcast_to(target, (LANES, LANES)))
+        across = lanes_of((LANES, LANES))
+        for at in range(0, wide, LANES):
+            hit = jnp.where(across == target - at, 1.0, 0.0)
+            hot[here, at : at + LANES] = hit.astype(jnp.bfloat16)
+
+    def product(depth):
+        total[...] = jnp.dot(
+            values[:, :depth], hot[:depth, :], preferred_element_type=jnp.float32
+        )
+
+    last = rims.shape[0] - GROUP
+    point_tile(0, rims[0:high, :], place[0])
+    point_tile(1, rims[last : last + high, :], peers + place[0])
+    beside = (place[0] == 0) | (place[0] == place[2] - 1)
+
+    @pl.when(jnp.logical_not(beside))
+    def _():
+        product(2 * LANES)
+
+    @pl.when(beside)
+    def _():
+        first = jnp.where(place[0] == 0, 2 * peers, 2 * peers + tiles)
+        for tile in range(tiles):
+            parts = []
+            for source in (0, 64):
+                value = jnp.zeros((BLOCK, LANES), jnp.float32)
+                for row in range(tile * LANES // rows, -(-(tile + 1) * LANES // rows)):
+                    at = rows * row - tile * LANES
+                    piece = rims[GROUP * row + 2 * BLOCK : GROUP * row + 3 * BLOCK, :]
+                    value = jnp.where(
+                        (lane >= at) & (lane < at + rows), moved(piece, source, at % LANES), value
+                    )
+                parts.append(value)
+            point_tile(2 + tile, jnp.concatenate(parts, axis=0), first + tile)
+        product((2 + tiles) * LANES)
+
+    sums = rims[GROUP - 1 : GROUP, :]
+    for at in range(GROUP, rims.shape[0], GROUP):
+        sums = sums + rims[at + GROUP - 1 : at + GROUP, :]
+    sums = pltpu.roll(sums, 64, 1)
+    for peer in range(peers):
+        at = 3 * high * peer
+        out[peer] = (
+            total[at : at + high] + total[at + high : at + 2 * high] + total[at + 2 * high : at + 3 * high]
+        )
+        at = slice(wide - LANES, wide)
+        out[peer, 0:1, at] = jnp.where(lane < 64, out[peer, 0:1, at], sums)
+
+
+def join_kernel(parts, sums_out, out, spread):
+    total = jnp.sum(parts[...], axis=0)
+    sums = pltpu.roll(total[0:1, 2 * LANES :], 64, 1)
+    sums_out[...] = sums
+    weights = krylov_weights(sums)
+    first, second = total[0:BLOCK], total[BLOCK:]
+    value = (
+        first
+        + weights[0] * pltpu.roll(first, BLOCK - 2, 0)
+        + weights[1] * pltpu.roll(second, BLOCK - 2, 0)
+        + weights[2] * second
     )
-    split(beside * joined(point_weight, 0.0), 0)
-    beside_target = target_of(joined(point_map, 0))
-
-    def spread(targets, length):
-        block = 512
-        height = lax.broadcasted_iota(jnp.int32, (block, LANES), 0)
-        for at in range(0, 2560, block):
-            here = slice(at, at + block)
-            for n, target in enumerate(targets):
-                hit = jnp.where(height == target - at, 1.0, 0.0)
-                hot[here, n * LANES : (n + 1) * LANES] = hit.astype(jnp.bfloat16)
-            got = lax.dot_general(
-                hot[here, :length],
-                values[:, :length],
-                (((1,), (1,)), ((), ())),
-                preferred_element_type=jnp.float32,
-            )
-            low = got[:, :LANES]
-            high = jnp.concatenate([got[:, LANES:], got[:, LANES:]], axis=1)
-            halves[here, :] = low + pltpu.roll(low, 64, 1) + high
-
-    rim = (place[1] == 0) | (place[1] == place[3] - 1)
-
-    @pl.when(jnp.logical_not(rim))
-    def _():
-        spread([beside_target], LANES)
-
-    @pl.when(rim)
-    def _():
-        first = jnp.where(place[1] == 0, 0, peers)
-        targets = [beside_target]
-        for peer in range(peers):
-            split(rims[peer, 0:64, :] * point_weight[pl.ds(first + peer, 1), :], (peer + 1) * LANES)
-            targets.append(target_of(point_map[pl.ds(first + peer, 1), :]))
-        spread(targets, (peers + 1) * LANES)
-
-    sums = rims[0, 96:97, :]
-    for peer in range(1, peers):
-        sums = sums + rims[peer, 96:97, :]
-    for row in range(32):
-        at = slice(40 * row, 40 * row + 40)
-        above = slice(1280 + 40 * row, 1320 + 40 * row)
-        out[41 * row : 41 * row + 40, :] = jnp.where(lane < 64, halves[at, :], halves[above, :])
-        out[41 * row + 40 : 41 * row + 41, :] = sums
-
-
-def join_kernel(parts, sums_out, out):
-    total = parts[0:41, :]
-    for at in range(41, parts.shape[0], 41):
-        total = total + parts[at : at + 41, :]
-    sums_out[...] = total[40:41]
-    weights = krylov_weights(total[40:41])
-    value = total[0:40]
-    value = (
-        value
-        + weights[0] * pltpu.roll(value, LANES - 2, 1)
-        + weights[1] * pltpu.roll(value, LANES - 34, 1)
-        + weights[2] * pltpu.roll(value, LANES - 32, 1)
-    )
-    out[0:40, :] = value
-    out[40:80, :] = pltpu.roll(value, 64, 1)
+    spread[...] = jnp.zeros_like(spread)
+    for source, target in ((0, 0), (4, 1), (1, 64), (5, 65)):
+        spread[target : target + 1, :] = value[source : source + 1]
+    for tile in range(3):
+        at = slice(tile * LANES, min((tile + 1) * LANES, out.shape[0]))
+        out[at, :] = jnp.transpose(spread[:, tile * LANES : (tile + 1) * LANES])[: at.stop - at.start]
 
 
 def gather_kernel(parts, out):
     levels = out.shape[2]
-    source = lax.broadcasted_iota(jnp.int32, (LANES, LANES), 0)
-    target = lanes_of((LANES, LANES))
+    lane = lanes_of((1, LANES))
     total = jnp.zeros((SLOTS, LANES), jnp.float32)
-    for group in range(-(-levels // 8)):
-        wanted = 64 * (source & 3) + 8 * group + (source >> 2)
-        pick = (target == wanted) & ((source & 3) < 2) & (source < 32)
-        total = total + jnp.dot(
-            parts[SLOTS * group : SLOTS * group + SLOTS, :],
-            jnp.where(pick, 1.0, 0.0),
-            precision=lax.Precision.HIGHEST,
-            preferred_element_type=jnp.float32,
-        )
+    for pair in range(levels // 2):
+        value = parts[SLOTS * pair : SLOTS * pair + SLOTS, :]
+        total = jnp.where((lane & 63) >> 1 == pair, moved(value, 0, 2 * pair), total)
     out[:, 0, :] = total[:, 0:levels]
     out[:, 1, :] = total[:, 64 : 64 + levels]
 
@@ -647,7 +627,7 @@
     full = shape_of(rows + 2 * BLOCK, 2 * LANES)
     v0, v1, v2, rims = pl.pallas_call(
         krylov_kernel,
-        out_shape=(full, full, full, shape_of(across, 104, LANES)),
+        out_shape=(full, full, full, shape_of(along * GROUP, LANES)),
         in_specs=[SMEM] + [VMEM] * 18,
         out_specs=(VMEM,) * 4,
         scratch_shapes=[pltpu.VMEM((count, cols), jnp.float32)] * 3
@@ -658,30 +638,32 @@
         place, b, conduct_east, conduct_north, surface_diagonal, side, south_in, north_in, west_in, east_in,
         flow_east, flow_north, west_pack, east_pack, west_inner, east_inner, south_rows, north_rows, inner_rows,
     )
-    rims = lax.all_to_all(rims, "gx", 0, 0)
+    rims = lax.all_to_all(rims.reshape(along, 1, GROUP * LANES), "gy", 0, 0)
+    points = (2 + rows * along // LANES) * LANES
     parts = pl.pallas_call(
         controls_kernel,
-        out_shape=shape_of(along * 41, LANES),
+        out_shape=shape_of(across, 16, 3 * LANES),
         in_specs=[SMEM] + [VMEM] * 3,
         out_specs=VMEM,
         scratch_shapes=[
-            pltpu.VMEM((192, (across + 1) * LANES), jnp.bfloat16),
-            pltpu.VMEM((2560, (across + 1) * LANES), jnp.bfloat16),
-            pltpu.VMEM((2560, LANES), jnp.float32),
+            pltpu.VMEM((across * 48, points), jnp.bfloat16),
+            pltpu.VMEM((points, 3 * LANES), jnp.bfloat16),
+            pltpu.VMEM((across * 48, 3 * LANES), jnp.float32),
         ],
         compiler_params=MIDDLE,
         name="controls",
-    )(place, rims, point_map, point_weight)
-    parts = lax.all_to_all(parts.reshape(along, 1, 41 * LANES), "gy", 0, 0)
+    )(place, rims.reshape(along * GROUP, LANES), point_map, point_weight)
+    parts = lax.all_to_all(parts, "gx", 0, 0)
     sums, joined = pl.pallas_call(
         join_kernel,
-        out_shape=(shape_of(1, LANES), shape_of(across * SLOTS, LANES)),
+        out_shape=(shape_of(1, LANES), shape_of(along * SLOTS, LANES)),
         in_specs=[VMEM],
         out_specs=(VMEM,) * 2,
+        scratch_shapes=[pltpu.VMEM((LANES, 3 * LANES), jnp.float32)],
         compiler_params=SMALL,
         name="join",
-    )(parts.reshape(along * 41, LANES))
-    joined = lax.all_to_all(joined.reshape(across, 1, SLOTS * LANES), "gx", 0, 0)
+    )(parts)
+    joined = lax.all_to_all(joined.reshape(along, 1, SLOTS * LANES), "gy", 0, 0)
     tracer_grad, x = pl.pallas_call(
         fields_kernel,
         out_shape=(field, tile),
@@ -708,7 +690,7 @@
         out_specs=VMEM,
         compiler_params=SMALL,
         name="gather",
-    )(joined.reshape(across * SLOTS, LANES))
+    )(joined.reshape(along * SLOTS, LANES))
     return tracer_grad, x, jnp.transpose(control_grad, (1, 2, 0))
 
 

time: 88.4 us -> 82.8 us (0.937)
  blocking collectives: 44.4 us -> 38.5 us
  waiting for transfers between devices: 6.57 us -> 10.7 us
  Pallas kernels: 19.5 us -> 17.4 us
  starting transfers between devices: 16.8 us -> 14.9 us
    all_to_all x2, blocking collectives: 44.4 us -> 38.5 us  [the longest x1 25.5 us: per_device(): rims = lax.all_to_all(rims.reshape(along, 1, GROUP * LANES), 'gy', 0, 0)]
    all_to_all x1, waiting for transfers between devices: 0.01 us -> 4.12 us  [per_device(): joined = lax.all_to_all(joined.reshape(along, 1, SLOTS * LANES), 'gy', 0, 0)]
    pallas_call x3, Pallas kernels: 5.5 us -> 3.56 us  [the longest x1 1.5 us: per_device(): pl.pallas_call(krylov_kernel, out_shape=(full, full, full, shape_of(along...]
    all_to_all x1, starting transfers between devices: 5.72 us -> 3.86 us  [per_device(): joined = lax.all_to_all(joined.reshape(along, 1, SLOTS * LANES), 'gy', 0, 0)]
  transfers between devices with their start and end apart: 5 -> 5, of which waited for: 2 -> 3; matrix products, arithmetic and copies ran while one was open for 0% -> 0% of each run, Pallas kernels for 6% -> 7%
where the time goes in v3:
time: 82.8 us; the launch traced here: 82.4 us
  blocking collectives  38.5 us (46%)
  Pallas kernels  17.4 us (21%)
  starting transfers between devices  14.9 us (18%)
  waiting for transfers between devices  10.7 us (13%)
    all_to_all x1, blocking collectives, per_device(): rims = lax.all_to_all(rims.reshape(along, 1, GROUP * LANES), 'gy', 0, 0)  25.5 us
    all_to_all x1, blocking collectives, per_device(): parts = lax.all_to_all(parts, 'gx', 0, 0)  13.1 us
    ppermute x4, starting transfers between devices, shifted(): return lax.ppermute(value, axis, pairs)  11.1 us
    pallas_call x1, Pallas kernels, per_device(): pl.pallas_call(columns_kernel, out_shape=(tile, field, field, pack, pack,...  7.38 us
    ppermute x4, waiting for transfers between devices, shifted(): return lax.ppermute(value, axis, pairs)  6.57 us
    pallas_call x1, Pallas kernels, per_device(): pl.pallas_call(fields_kernel, out_shape=(field, tile), in_specs=[VMEM] *...  5.56 us
    all_to_all x1, waiting for transfers between devices, per_device(): joined = lax.all_to_all(joined.reshape(along, 1, SLOTS * LANES), 'gy', 0, 0)  4.12 us
    all_to_all x1, starting transfers between devices, per_device(): joined = lax.all_to_all(joined.reshape(along, 1, SLOTS * LANES), 'gy', 0, 0)  3.86 us
  transfers between devices with their start and end apart: 5, of which 3 were waited for; matrix products, arithmetic and copies ran while one was open for 0% of the time, Pallas kernels for 7%

profile of v3, /device:TPU:1, one launch (start us, length us, event | category | flops | bytes accessed | tf_op | source)
XLA Modules:
  0.0 82.4 jit_solution(11043827132265454033)
XLA Ops:
  0.6 0.1 pad_add_fusion.place
  0.7 0.0 copy-start.4
  0.7 0.0 copy-start.5
  0.7 0.0 copy-start.6
  0.7 0.0 copy-start
  0.7 0.0 copy-start.1
  0.7 7.4 %columns.1 = (f32[40,128]{1,0:T(8,128)S(1)}, f32[2,50,40,128]{3,2,1,0:T(8,128)S(1)}, f32[2,50,40,128]{3,2,1,0:T(8,128)S(1)}, f32[40,384]{1,0:T(8,128)S(1)}, f32[...) custom-call(s32[4]{0:T(128)S(1)} %pad_add_fusion.place, ...), custom_call_target="tpu_custom_call" | custom-call | tf_op jit(solution)/shard_map/columns/pallas_call | solution.py:577
  8.1 0.0 copy-start.2
  8.1 0.0 copy-start.3
  8.1 5.1 %collective-permute-start.1 = (f32[40,384]{1,0:T(8,128)S(1)}, f32[40,384]{1,0:T(8,128)S(1)}, u32[]{:S(2)}, u32[]{:S(2)}) collective-permute-start(f32[40,384]{1,0:T(8,128)S(1)} %get-tuple-element.30.west_pack), channel_id=1, source_target_pairs={{32,0},{64,32},{96,64},{128,96},{160,128},{192,160},{224,192},{33,... | collective-permute-start | bytes 184328 | tf_op jit(solution)/shard_map/ppermute | solution.py:539
  13.3 1.9 %collective-permute-start = (f32[40,384]{1,0:T(8,128)S(1)}, f32[40,384]{1,0:T(8,128)S(1)}, u32[]{:S(2)}, u32[]{:S(2)}) collective-permute-start(f32[40,384]{1,0:T(8,128)S(1)} %get-tuple-element.29.east_pack), channel_id=1, source_target_pairs={{0,32},{32,64},{64,96},{96,128},{128,160},{160,192},{192,224},{1,3... | collective-permute-start | bytes 184328 | tf_op jit(solution)/shard_map/ppermute | solution.py:539
  15.2 0.0 collective-permute-done.1.east_in
  15.2 1.3 %collective-permute-done.west_in = f32[40,384]{1,0:T(8,128)S(1)} collective-permute-done((f32[40,384]{1,0:T(8,128)S(1)}, f32[40,384]{1,0:T(8,128)S(1)}, u32[]{:S(2)}, u32[]{:S(2)}) %collective-permute-start) | collective-permute-done | bytes 61472 | tf_op jit(solution)/shard_map/ppermute | solution.py:539
  16.5 0.0 copy-done.4
  16.5 0.0 copy-done.5
  16.5 0.0 copy-done.6
  16.5 0.1 rows.1
  16.6 0.0 copy-start.7
  16.6 0.0 copy-start.8
  16.6 2.7 %collective-permute-start.2 = (f32[296,128]{1,0:T(8,128)S(1)}, f32[296,128]{1,0:T(8,128)S(1)}, u32[]{:S(2)}, u32[]{:S(2)}) collective-permute-start(f32[296,128]{1,0:T(8,128)S(1)} %get-tuple-element.34.north_rows), channel_id=1, source_target_pairs={{0,1},{1,2},{2,3},{3,4},{4,5},{5,6},{6,7},{7,8},{8,9},{9,10},{10,1... | collective-permute-start | bytes 454664 | tf_op jit(solution)/shard_map/ppermute | solution.py:539
  19.3 1.3 %collective-permute-start.3 = (f32[240,128]{1,0:T(8,128)S(1)}, f32[240,128]{1,0:T(8,128)S(1)}, u32[]{:S(2)}, u32[]{:S(2)}) collective-permute-start(f32[240,128]{1,0:T(8,128)S(1)} %get-tuple-element.35.south_rows), channel_id=1, source_target_pairs={{1,0},{2,1},{3,2},{4,3},{5,4},{6,5},{7,6},{8,7},{9,8},{10,9},{11,1... | collective-permute-start | bytes 368648 | tf_op jit(solution)/shard_map/ppermute | solution.py:539
  20.6 5.3 %collective-permute-done.3.north_in = f32[240,128]{1,0:T(8,128)S(1)} collective-permute-done((f32[240,128]{1,0:T(8,128)S(1)}, f32[240,128]{1,0:T(8,128)S(1)}, u32[]{:S(2)}, u32[]{:S(2)}) %collective-permute-start.3) | collective-permute-done | bytes 122912 | tf_op jit(solution)/shard_map/ppermute | solution.py:539
  25.9 0.0 collective-permute-done.2.south_in
  25.9 0.0 copy-done
  25.9 0.0 copy-done.1
  25.9 1.5 %krylov.1 = (f32[56,256]{1,0:T(8,128)S(1)}, f32[56,256]{1,0:T(8,128)S(1)}, f32[56,256]{1,0:T(8,128)S(1)}, f32[800,128]{1,0:T(8,128)S(1)}) custom-call(s32[4]{0:T(128)S(1)} %pad_add_fusion.place, f32[40,128]{1,0:T(8,128)S(1)} %get-tuple-element.28.b, f32[40,128]{1,0:T(8,128)S(1)} %copy-done.4, f32[40,128]{1,0:T(8,128)S(1)} %copy-done.5, ...), custom_call_target="tpu_custom_call" | custom-call | tf_op jit(solution)/shard_map/krylov/pallas_call | solution.py:628
  27.4 25.5 %all_to_all.15 = f32[32,1,3200]{2,1,0:T(1,128)S(1)} all-to-all(f32[32,1,3200]{2,1,0:T(1,128)S(1)} %bitcast.11), channel_id=1, replica_groups=mesh['gx'=8,'gy'=32] {'gy'}, dimensions={0} | all-to-all | bytes 819200 | tf_op jit(solution)/shard_map/all_to_all | solution.py:641
  52.9 0.0 copy-done.2
  52.9 0.0 copy-done.3
  52.9 0.0 copy-done.7
  52.9 0.0 copy-done.8
  52.9 1.0 %controls.1 = f32[8,16,384]{2,1,0:T(8,128)S(1)} custom-call(s32[4]{0:T(128)S(1)} %pad_add_fusion.place, f32[800,128]{1,0:T(8,128)S(1)} %bitcast.9, s32[36,128]{1,0:T(8,128)S(1)} %bitcast.12, f32[36,128]{1,0:T(8,128)S(1)} %bitcast.13), custom_call_target="tpu_custom_call" | custom-call | tf_op jit(solution)/shard_map/controls/pallas_call | solution.py:643
  54.0 13.1 %all_to_all.16.parts = f32[8,16,384]{2,1,0:T(8,128)S(1)} all-to-all(f32[8,16,384]{2,1,0:T(8,128)S(1)} %controls.1), channel_id=1, replica_groups=mesh['gx'=8,'gy'=32] {'gx'}, dimensions={0} | all-to-all | bytes 393216 | tf_op jit(solution)/shard_map/all_to_all | solution.py:656
  67.0 1.0 %join.1 = (f32[1,128]{1,0:T(1,128)S(1)}, f32[320,128]{1,0:T(8,128)}) custom-call(f32[8,16,384]{2,1,0:T(8,128)S(1)} %all_to_all.16.parts), custom_call_target="tpu_custom_call" | custom-call | tf_op jit(solution)/shard_map/join/pallas_call | solution.py:657
  68.0 3.9 %all-to-all-start.2 = ((f32[32,1,1280]{2,1,0:T(1,128)}), f32[32,1,1280]{2,1,0:T(1,128)S(1)}, u32[]{:S(2)}, u32[]{:S(2)}) async-start(f32[32,1,1280]{2,1,0:T(1,128)} %bitcast.6), calls=%async_computation.2 | async-start | bytes 327680 | tf_op jit(solution)/shard_map/all_to_all | solution.py:666
  71.9 5.6 %fields.1 = (f32[2,50,40,128]{3,2,1,0:T(8,128)}, f32[40,128]{1,0:T(8,128)}) custom-call(f32[1,128]{1,0:T(1,128)S(1)} %get-tuple-element.40.sums_in, f32[56,256]{1,0:T(8,128)S(1)} %get-tuple-element.41.v0, f32[56,256]{1,0:T(8,128)S(1)} %get-tuple-element.42.v1, f32[56,256]{1,0:T(8,128)S(1)} %get-tuple-element.43.v2, f32[2,50,40,128]{3,2,1,0:T(8,128)} %copy-done.2, ...), custom_call_target="tpu_custom_call" | custom-call | tf_op jit(solution)/shard_map/fields/pallas_call | solution.py:667
  77.5 4.1 %all-to-all-done.2 = f32[32,1,1280]{2,1,0:T(1,128)S(1)} async-done(((f32[32,1,1280]{2,1,0:T(1,128)}), f32[32,1,1280]{2,1,0:T(1,128)S(1)}, u32[]{:S(2)}, u32[]{:S(2)}) %all-to-all-start.2) | async-done | bytes 163872 | tf_op jit(solution)/shard_map/all_to_all | solution.py:666
  81.6 0.8 gather.1
Async XLA Ops:
  0.7 15.8 %copy-start.4 = (f32[40,128]{1,0:T(8,128)S(1)}, f32[40,128]{1,0:T(8,128)}, u32[]{:S(2)}) copy-start(f32[40,128]{1,0:T(8,128)} %c_east.3) | copy-start | bytes 61444
  0.7 15.8 %copy-start.5 = (f32[40,128]{1,0:T(8,128)S(1)}, f32[40,128]{1,0:T(8,128)}, u32[]{:S(2)}) copy-start(f32[40,128]{1,0:T(8,128)} %c_north.3) | copy-start | bytes 61444
  0.7 15.8 %copy-start.6 = (f32[40,128]{1,0:T(8,128)S(1)}, f32[40,128]{1,0:T(8,128)}, u32[]{:S(2)}) copy-start(f32[40,128]{1,0:T(8,128)} %diag.3) | copy-start | bytes 61444
  0.7 25.2 %copy-start = (f32[50,40,128]{2,1,0:T(8,128)S(1)}, f32[50,40,128]{2,1,0:T(8,128)}, u32[]{:S(2)}) copy-start(f32[50,40,128]{2,1,0:T(8,128)} %flow_east.3) | copy-start | bytes 3072004
  0.7 25.2 %copy-start.1 = (f32[50,40,128]{2,1,0:T(8,128)S(1)}, f32[50,40,128]{2,1,0:T(8,128)}, u32[]{:S(2)}) copy-start(f32[50,40,128]{2,1,0:T(8,128)} %flow_north.3) | copy-start | bytes 3072004
  8.1 44.8 %copy-start.2 = (f32[2,50,40,128]{3,2,1,0:T(8,128)}, f32[2,50,40,128]{3,2,1,0:T(8,128)S(1)}, u32[]{:S(2)}) copy-start(f32[2,50,40,128]{3,2,1,0:T(8,128)S(1)} %get-tuple-element.44.u_hbm) | copy-start | bytes 6144004
  8.1 44.8 %copy-start.3 = (f32[2,50,40,128]{3,2,1,0:T(8,128)}, f32[2,50,40,128]{3,2,1,0:T(8,128)S(1)}, u32[]{:S(2)}) copy-start(f32[2,50,40,128]{3,2,1,0:T(8,128)S(1)} %get-tuple-element.45.v_hbm) | copy-start | bytes 6144004
  8.1 7.1 %collective-permute-start.1 = (f32[40,384]{1,0:T(8,128)S(1)}, f32[40,384]{1,0:T(8,128)S(1)}, u32[]{:S(2)}, u32[]{:S(2)}) collective-permute-start(f32[40,384]{1,0:T(8,128)S(1)} %get-tuple-element.30.west_pack), channel_id=1, source_target_pairs={{32,0},{64,32},{96,64},{128,96},{160,128},{192,160},{224,192},{33,... | collective-permute-start | bytes 184328 | tf_op jit(solution)/shard_map/ppermute | solution.py:539
  13.3 3.2 %collective-permute-start = (f32[40,384]{1,0:T(8,128)S(1)}, f32[40,384]{1,0:T(8,128)S(1)}, u32[]{:S(2)}, u32[]{:S(2)}) collective-permute-start(f32[40,384]{1,0:T(8,128)S(1)} %get-tuple-element.29.east_pack), channel_id=1, source_target_pairs={{0,32},{32,64},{64,96},{96,128},{128,160},{160,192},{192,224},{1,3... | collective-permute-start | bytes 184328 | tf_op jit(solution)/shard_map/ppermute | solution.py:539
  16.6 36.3 %copy-start.7 = (s32[4608]{0:T(1024)S(1)}, s32[4608]{0:T(1024)}, u32[]{:S(2)}) copy-start(s32[4608]{0:T(1024)} %param.24) | copy-start | bytes 55300
  16.6 36.3 %copy-start.8 = (f32[4608]{0:T(1024)S(1)}, f32[4608]{0:T(1024)}, u32[]{:S(2)}) copy-start(f32[4608]{0:T(1024)} %param.25) | copy-start | bytes 55300
  16.6 9.3 %collective-permute-start.2 = (f32[296,128]{1,0:T(8,128)S(1)}, f32[296,128]{1,0:T(8,128)S(1)}, u32[]{:S(2)}, u32[]{:S(2)}) collective-permute-start(f32[296,128]{1,0:T(8,128)S(1)} %get-tuple-element.34.north_rows), channel_id=1, source_target_pairs={{0,1},{1,2},{2,3},{3,4},{4,5},{5,6},{6,7},{7,8},{8,9},{9,10},{10,1... | collective-permute-start | bytes 454664 | tf_op jit(solution)/shard_map/ppermute | solution.py:539
  19.3 6.6 %collective-permute-start.3 = (f32[240,128]{1,0:T(8,128)S(1)}, f32[240,128]{1,0:T(8,128)S(1)}, u32[]{:S(2)}, u32[]{:S(2)}) collective-permute-start(f32[240,128]{1,0:T(8,128)S(1)} %get-tuple-element.35.south_rows), channel_id=1, source_target_pairs={{1,0},{2,1},{3,2},{4,3},{5,4},{6,5},{7,6},{8,7},{9,8},{10,9},{11,1... | collective-permute-start | bytes 368648 | tf_op jit(solution)/shard_map/ppermute | solution.py:539
  68.0 13.5 %all-to-all-start.2 = ((f32[32,1,1280]{2,1,0:T(1,128)}), f32[32,1,1280]{2,1,0:T(1,128)S(1)}, u32[]{:S(2)}, u32[]{:S(2)}) async-start(f32[32,1,1280]{2,1,0:T(1,128)} %bitcast.6), calls=%async_computation.2 | async-start | bytes 327680 | tf_op jit(solution)/shard_map/all_to_all | solution.py:666

commit v4 on v3

--- a/solution.py
+++ b/solution.py
@@ -34,8 +34,8 @@
 def columns_kernel(
     place, forcing_in, loads_in, tracer_in, surface_in, east_flow, north_flow, mix_in, mask_in, c_east_in,
     c_north_in, diag_in,
-    b_out, u_hbm, v_hbm, west_pack, east_pack, west_inner, east_inner, south_rows, north_rows, inner_rows,
-    u_out, v_out, ratios, forcing, loads, tracer, surface, flow_east, flow_north, mix, mask, c_east, c_north, diag,
+    b_out, u_out, v_out, first_pack, second_pack, west_inner, east_inner, edge_flow,
+    ratios, forcing, loads, tracer, surface, flow_east, flow_north, mix, mask, c_east, c_north, diag,
     sems,
 ):
     levels, rows, cols = mask.shape
@@ -99,8 +99,6 @@
     total = total + surface[...]
     b_out[...] = total
 
-    southern = place[1] == 0
-    leaving = []
     for k in range(last, -1, -1):
         if k < last:
             ratio = ratios[k]
@@ -109,21 +107,13 @@
         wet = mask[k].astype(jnp.float32)
         fields = [wet * sol for sol in sols]
         u_out[0, k], u_out[1, k], v_out[0, k], v_out[1, k] = fields
-        for q, field in enumerate(fields):
-            line = slice(4 * k + q, 4 * k + q + 1)
-            south_rows[line, :] = field[0:1]
-            north_rows[line, :] = field[rows - 1 : rows]
-            inner_rows[line, :] = jnp.where(southern, field[1:2], field[rows - 2 : rows - 1])
-        if k % 10 == 0:
-            at = pl.ds(k, 10)
-            leaving += [
-                fetch(buffer.at[:, at], target.at[:, at])
-                for buffer, target in ((u_out, u_hbm), (v_out, v_hbm))
-            ]
     lane = lanes_of((1, cols))
-    side = slice(LANES, 2 * LANES)
-    west_pack[:, side] = zero
-    east_pack[:, side] = zero
+    even = (place[0] & 1) == 0
+
+    def pack(at, west, east):
+        first_pack[:, at] = jnp.where(even, east, west)
+        second_pack[:, at] = jnp.where(even, west, east)
+
     for tile in range(2):
         west, east, west_in, east_in = zero, zero, zero, zero
         for spot in range(4 * min(32, levels - 32 * tile)):
@@ -135,34 +125,64 @@
             east = jnp.where(lane == (spot - 1) % LANES, turned, east)
             east_in = jnp.where(lane == (spot - 2) % LANES, turned, east_in)
         at = slice(tile * LANES, (tile + 1) * LANES)
-        west_pack[:, at], east_pack[:, at] = west, moved(east, 0, 1)
+        east = moved(east, 0, 1)
+        if tile == 1:
+            for k in range(levels):
+                east = jnp.where(lane == 72 + k, moved(flow_east[k], cols - 1, 72 + k), east)
+        pack(at, west, east)
         west_inner[:, at], east_inner[:, at] = moved(west_in, 1, 0), moved(east_in, 0, 2)
-    value = east_pack[:, side]
     for k in range(levels):
-        value = jnp.where(lane == 72 + k, moved(flow_east[k], cols - 1, 72 + k), value)
-        north_rows[240 + k : 241 + k, :] = flow_north[k, BLOCK - 1 : BLOCK, :]
-    east_pack[:, side] = value
+        edge_flow[k : k + 1, :] = flow_north[k, BLOCK - 1 : BLOCK, :]
     west, east = zero, zero
     for a, field in enumerate((total, c_east[...], c_north[...], diag[...])):
         here = (lane >= 4 * a) & (lane < 4 * a + 3)
         west = jnp.where(here, moved(field, 0, 4 * a), west)
         east = jnp.where(here, moved(field, cols - 3, 4 * a), east)
-    west_pack[:, 2 * LANES :], east_pack[:, 2 * LANES :] = west, east
-    for copy in leaving:
+    pack(slice(2 * LANES, 3 * LANES), west, east)
+
+def store_kernel(place, u, v, edge_flow, u_hbm, v_hbm, first_rows, second_rows, inner_rows, sems):
+    _, levels, rows, _ = u.shape
+    copies = [
+        pltpu.make_async_copy(source, target, sems.at[n])
+        for n, (source, target) in enumerate(((u, u_hbm), (v, v_hbm)))
+    ]
+    for copy in copies:
+        copy.start()
+    even = (place[1] & 1) == 0
+    picks = (
+        (first_rows, jnp.where(even, rows - 1, 0)),
+        (second_rows, jnp.where(even, 0, rows - 1)),
+        (inner_rows, jnp.where(place[1] == 0, 1, rows - 2)),
+    )
+    for k in range(levels):
+        for q in range(4):
+            for target, row in picks:
+                line = slice(4 * k + q, 4 * k + q + 1)
+                target[line, :] = (u, v)[q // 2][q % 2, k, pl.ds(row, 1), :]
+    for target in (first_rows, second_rows):
+        target[240 : 240 + levels, :] = edge_flow[0:levels, :]
+    for copy in copies:
         copy.wait()
 
 
-def rows_kernel(b, c_east, c_north, diag, west_in, east_in, _s, _n, south_rows, north_rows, side):
+def rows_kernel(
+    place, b, c_east, c_north, diag, first_in, second_in, _f, _s,
+    first_rows, second_rows, side, west_in, east_in,
+):
     shape = b.shape
     rows = shape[0]
     lane = lanes_of(shape)
-    both = jnp.where(
+    even = (place[0] & 1) == 0
+    west_in[...] = jnp.where(even, second_in[...], first_in[...])
+    east_in[...] = jnp.where(even, first_in[...], second_in[...])
+    side[...] = jnp.where(
         lane < 64, west_in[:, 2 * LANES :], moved(east_in[:, 2 * LANES :], 0, 64)
     )
-    side[...] = both
+    even = (place[1] & 1) == 0
     for a, field in enumerate((b, c_east, c_north, diag, side)):
-        south_rows[8 * a : 8 * a + 8, :] = field[0:BLOCK, :]
-        north_rows[8 * a : 8 * a + 8, :] = field[rows - BLOCK :, :]
+        south, north = field[0:BLOCK, :], field[rows - BLOCK :, :]
+        first_rows[BLOCK * a : BLOCK * a + BLOCK, :] = jnp.where(even, north, south)
+        second_rows[BLOCK * a : BLOCK * a + BLOCK, :] = jnp.where(even, south, north)
 
 
 def tall_transpose(value):
@@ -173,87 +193,43 @@
     return jnp.concatenate(tiles, axis=0)
 
 
-def rim_parts(center, inner, low, high, face_high, face_low, face_inner, last, factors):
+def rim_weights(center, inner, low, high, face_high, face_low, face_inner, last):
     lane = lanes_of(center.shape)
-    which = lax.broadcasted_iota(jnp.int32, center.shape, 0) & 3
     low = jnp.where(lane == 0, low, pltpu.roll(center, 1, 1))
     high = jnp.where(lane == last, high, pltpu.roll(center, LANES - 1, 1))
     face_low = jnp.where(lane == 0, face_low, pltpu.roll(face_high, 1, 1))
+    return (
+        center * (1.0 - 0.5 * face_high + 0.5 * face_low - 0.5 * face_inner),
+        0.5 * face_inner * inner,
+        -0.5 * face_low * low,
+        0.5 * face_high * high,
+    )
+
+
+def rim_parts(weights, factors):
+    rows = weights[0].shape[0]
+    which = lax.broadcasted_iota(jnp.int32, weights[0].shape, 0) & 3
     parts = []
-    for n, (f_center, f_inner, f_low, f_high) in enumerate(factors):
+    for n, values in enumerate(factors):
         if n == 0:
-            f_center, f_inner, f_low, f_high = (
-                jnp.where(which < 2, 1.0, f) for f in (f_center, f_inner, f_low, f_high)
-            )
-        here = center * f_center
-        parts.append(
-            here
-            + 0.5 * face_high * (high * f_high - here)
-            + 0.5 * face_low * (here - low * f_low)
-            + 0.5 * face_inner * (inner * f_inner - here)
-        )
-    rows = center.shape[0]
+            values = [jnp.where(which < 2, 1.0, value) for value in values]
+        parts.append(sum(weight * value for weight, value in zip(weights, values)))
     return parts[0], jnp.where(which >= 2, parts[1], pltpu.roll(parts[2], rows - 2, 0))
 
 
-def krylov_kernel(
-    place, b, c_east, c_north, diag, side, south_in, north_in, west_in, east_in,
-    flow_east, flow_north, west_pack, east_pack, west_inner, east_inner, south_rows, north_rows, inner_rows,
-    v0_out, v1_out, v2_out, out,
+def prepare_kernel(
+    place, flow_east, flow_north, west_in, east_in, first_pack, second_pack, west_inner, east_inner,
+    first_rows, second_rows, inner_rows,
+    line_out, side_out,
     high_buf, low_buf, face_buf, turned,
 ):
     levels, rows, cols = flow_east.shape
-    sides = jnp.concatenate([south_in[232:240, :], side[...], north_in[232:240, :]], axis=0)
-    lane = lanes_of(sides.shape)
-    full = []
-    for a, field in enumerate((b, c_east, c_north, diag)):
-        at = slice(200 + 8 * a, 208 + 8 * a)
-        main = jnp.concatenate([south_in[at, :], field[...], north_in[at, :]], axis=0)
-        beside = jnp.where(
-            lane >= LANES - 3,
-            moved(sides, 4 * a, LANES - 3),
-            jnp.where(lane < 3, moved(sides, 64 + 4 * a, 0), 0.0),
-        )
-        full.append(jnp.concatenate([main, beside], axis=1))
-    vec, ce, cn, dg = full
-    tall, wide = vec.shape
-    cw = pltpu.roll(ce, 1, 1)
-    cs = pltpu.roll(cn, 1, 0)
-    vecs = [vec]
-    for _ in range(3):
-        vec = (
-            dg * vec
-            + ce * (vec - pltpu.roll(vec, wide - 1, 1))
-            + cw * (vec - pltpu.roll(vec, 1, 1))
-            + cn * (vec - pltpu.roll(vec, tall - 1, 0))
-            + cs * (vec - pltpu.roll(vec, 1, 0))
-        )
-        vecs.append(vec)
-    outs = (v0_out, v1_out, v2_out)
-    for target, value in zip(outs, vecs):
-        target[...] = value
-    tiles = [value[BLOCK : BLOCK + rows, :LANES] for value in vecs]
-    spot = lanes_of((1, LANES))
-    row = jnp.zeros((1, LANES), jnp.float32)
-    for n, (i, j) in enumerate(GRAM):
-        part = jnp.sum(tiles[i] * tiles[j], axis=0, keepdims=True)
-        row = jnp.where(spot == n, jnp.sum(part, axis=1, keepdims=True), row)
-    out[...] = jnp.zeros_like(out)
-    for at in range(0, out.shape[0], GROUP):
-        out[at + GROUP - 1 : at + GROUP, :] = row
     count = 4 * levels
-
-    def emit(parts, first):
-        for group in range(count // BLOCK):
-            for n, part in enumerate(parts):
-                at = GROUP * group + first + n * BLOCK
-                out[at : at + BLOCK, :] = part[BLOCK * group : BLOCK * group + BLOCK]
 
     @pl.when((place[1] == 0) | (place[1] == place[3] - 1))
     def _():
         south = place[1] == 0
         at = jnp.where(south, 0, rows - 1)
-        at_in = jnp.where(south, 1, rows - 2)
         sign = jnp.where(south, 1.0, -1.0)
         west_turned = tall_transpose(west_in[:, : 2 * LANES])
         west_turned = jnp.where(south, west_turned, moved(west_turned, rows - 1, 0))
@@ -269,25 +245,18 @@
             face_buf[four, :] = jnp.broadcast_to(
                 sign * flow_north[k, pl.ds(jnp.where(south, 0, rows - 2), 1), :], (4, cols)
             )
-        factors = []
-        for value in outs:
-            line = value[pl.ds(BLOCK + at, 1), :]
-            factors.append((
-                line[:, :cols], value[pl.ds(BLOCK + at_in, 1), :][:, :cols],
-                pltpu.roll(line, 1, 1)[:, :cols], pltpu.roll(line, wide - 1, 1)[:, :cols],
-            ))
-        parts = rim_parts(
-            jnp.where(south, south_rows[0:count, :], north_rows[0:count, :]),
+        second = south == ((place[1] & 1) == 0)
+        weights = rim_weights(
+            jnp.where(second, second_rows[0:count, :], first_rows[0:count, :]),
             inner_rows[...], west_turned[0:count], high[0:count],
-            high_buf[...], low_buf[...], face_buf[...], cols - 1, factors,
-        )
-        emit(parts, 0)
+            high_buf[...], low_buf[...], face_buf[...], cols - 1,
+        )
+        for n, weight in enumerate(weights):
+            line_out[n] = weight
 
     @pl.when((place[0] == 0) | (place[0] == place[2] - 1))
     def _():
         western = place[0] == 0
-        at = jnp.where(western, 0, cols - 1)
-        at_in = jnp.where(western, 1, cols - 2)
         sign = jnp.where(western, 1.0, -1.0)
         flat = lanes_of((rows, cols))
         norths = jnp.zeros((rows, cols), jnp.float32)
@@ -304,26 +273,116 @@
             four = slice(4 * k, 4 * k + 4)
             high_buf[four, :] = jnp.broadcast_to(turned[k : k + 1, :], (4, cols))
             face_buf[four, :] = jnp.broadcast_to(sign * turned[64 + k : 65 + k, :], (4, cols))
-            low_buf[four, :] = jnp.broadcast_to(south_in[240 + k : 241 + k, :], (4, cols))
+
+        second = western == ((place[0] & 1) == 0)
+        center = jnp.where(second, second_pack[:, : 2 * LANES], first_pack[:, : 2 * LANES])
+        inside = jnp.where(western, west_inner[...], east_inner[...])
+        center = tall_transpose(center)[0:count]
+        weights = rim_weights(
+            center, tall_transpose(inside)[0:count], 0.0, 0.0, high_buf[...], 0.0, face_buf[...], rows - 1
+        )
+        for n, weight in enumerate((*weights, 0.5 * center, 0.5 * high_buf[...])):
+            side_out[n] = weight
+
+
+def krylov_kernel(
+    place, b, c_east, c_north, diag, side, first_in, second_in, line_in, side_in,
+    v0_out, v1_out, v2_out, out, south_in, north_in,
+    low_buf, turned,
+):
+    rows, cols = b.shape
+    count = line_in.shape[1]
+    levels = count // 4
+    even = (place[1] & 1) == 0
+    south_in[...] = jnp.where(even, second_in[...], first_in[...])
+    north_in[...] = jnp.where(even, first_in[...], second_in[...])
+    sides = jnp.concatenate([south_in[232:240, :], side[...], north_in[232:240, :]], axis=0)
+    lane = lanes_of(sides.shape)
+    full = []
+    for a, field in enumerate((b, c_east, c_north, diag)):
+        at = slice(200 + 8 * a, 208 + 8 * a)
+        main = jnp.concatenate([south_in[at, :], field[...], north_in[at, :]], axis=0)
+        beside = jnp.where(
+            lane >= LANES - 3,
+            moved(sides, 4 * a, LANES - 3),
+            jnp.where(lane < 3, moved(sides, 64 + 4 * a, 0), 0.0),
+        )
+        full.append(jnp.concatenate([main, beside], axis=1))
+    vec, ce, cn, dg = full
+    tall, wide = vec.shape
+    cw = pltpu.roll(ce, 1, 1)
+    cs = pltpu.roll(cn, 1, 0)
+    vecs = [vec]
+    for _ in range(3):
+        vec = (
+            dg * vec
+            + ce * (vec - pltpu.roll(vec, wide - 1, 1))
+            + cw * (vec - pltpu.roll(vec, 1, 1))
+            + cn * (vec - pltpu.roll(vec, tall - 1, 0))
+            + cs * (vec - pltpu.roll(vec, 1, 0))
+        )
+        vecs.append(vec)
+    outs = (v0_out, v1_out, v2_out)
+    for target, value in zip(outs, vecs):
+        target[...] = value
+    tiles = [value[BLOCK : BLOCK + rows, :LANES] for value in vecs]
+    spot = lanes_of((1, LANES))
+    row = jnp.zeros((1, LANES), jnp.float32)
+    for n, (i, j) in enumerate(GRAM):
+        part = jnp.sum(tiles[i] * tiles[j], axis=0, keepdims=True)
+        row = jnp.where(spot == n, jnp.sum(part, axis=1, keepdims=True), row)
+    out[...] = jnp.zeros_like(out)
+    for at in range(0, out.shape[0], GROUP):
+        out[at + GROUP - 1 : at + GROUP, :] = row
+
+    def emit(parts, first):
+        for group in range(count // BLOCK):
+            for n, part in enumerate(parts):
+                at = GROUP * group + first + n * BLOCK
+                out[at : at + BLOCK, :] = part[BLOCK * group : BLOCK * group + BLOCK]
+
+    @pl.when((place[1] == 0) | (place[1] == place[3] - 1))
+    def _():
+        south = place[1] == 0
+        at = jnp.where(south, 0, rows - 1)
+        at_in = jnp.where(south, 1, rows - 2)
+        factors = []
+        for value in outs:
+            line = value[pl.ds(BLOCK + at, 1), :]
+            factors.append((
+                line[:, :cols], value[pl.ds(BLOCK + at_in, 1), :][:, :cols],
+                pltpu.roll(line, 1, 1)[:, :cols], pltpu.roll(line, wide - 1, 1)[:, :cols],
+            ))
+        emit(rim_parts([line_in[n] for n in range(4)], factors), 0)
+
+    @pl.when((place[0] == 0) | (place[0] == place[2] - 1))
+    def _():
+        western = place[0] == 0
+        at = jnp.where(western, 0, cols - 1)
+        at_in = jnp.where(western, 1, cols - 2)
+        for k in range(levels):
+            low_buf[4 * k : 4 * k + 4, :] = jnp.broadcast_to(south_in[240 + k : 241 + k, :], (4, cols))
 
         def line_up(value, target):
             return jnp.where(western, moved(value, 0, target), moved(value, cols - 1, target))
 
         factors = []
         for value in outs:
-            turned[0:LANES, :] = tall_transpose(value[:, :cols])
+            turned[...] = tall_transpose(value[:, :cols])
             line = pltpu.roll(turned[pl.ds(at, 1), :], LANES - BLOCK, 1)
             factors.append((
                 line, pltpu.roll(turned[pl.ds(at_in, 1), :], LANES - BLOCK, 1),
                 pltpu.roll(line, 1, 1), pltpu.roll(line, LANES - 1, 1),
             ))
-        center = jnp.where(western, west_pack[:, : 2 * LANES], east_pack[:, : 2 * LANES])
-        inside = jnp.where(western, west_inner[...], east_inner[...])
-        first, second = rim_parts(
-            tall_transpose(center)[0:count], tall_transpose(inside)[0:count],
-            line_up(south_in[0:count, :], 0), line_up(north_in[0:count, :], rows - 1),
-            high_buf[...], line_up(low_buf[...], 0), face_buf[...], rows - 1, factors,
-        )
+        here, inside, before, behind, center, face = (side_in[n] for n in range(6))
+        spots = lanes_of(here.shape)
+        low = line_up(low_buf[...], 0)
+        here = here + jnp.where(spots == 0, low * center, 0.0)
+        before = jnp.where(spots == 0, -0.5 * low * line_up(south_in[0:count, :], 0), before)
+        behind = jnp.where(
+            spots == rows - 1, face * line_up(north_in[0:count, :], rows - 1), behind
+        )
+        first, second = rim_parts((here, inside, before, behind), factors)
         half = lanes_of(first.shape) < 64
         emit((jnp.where(half, first, moved(second, 0, 64)),), 2 * BLOCK)
 
@@ -533,10 +592,16 @@
     out[:, 1, :] = total[:, 64 : 64 + levels]
 
 
-def shifted(value, axis, step):
+def swapped(value, axis, first):
     count = lax.axis_size(axis)
-    pairs = [(i, i + step) for i in range(count) if 0 <= i + step < count]
+    pairs = []
+    for low in range(0 if first else 1, count - 1, 2):
+        pairs += [(low, low + 1), (low + 1, low)]
     return lax.ppermute(value, axis, pairs)
+
+
+def in_vmem(value):
+    return pltpu.with_memory_space_constraint(value, pltpu.VMEM)
 
 
 def in_hbm(value):
@@ -573,15 +638,14 @@
     pack, inner = shape_of(rows, 3 * LANES), shape_of(rows, 2 * LANES)
     count = 4 * levels
     lines = shape_of(count, cols)
-    south_shape, north_shape = shape_of(240, cols), shape_of(296, cols)
-    b, u, v, west_pack, east_pack, west_inner, east_inner, south_rows, north_rows, inner_rows = pl.pallas_call(
+    rows_shape = shape_of(296, cols)
+    kept, away = pltpu.VMEM(field.shape, jnp.float32), pltpu.HBM(field.shape, jnp.float32)
+    b, u, v, first_pack, second_pack, west_inner, east_inner, edge_flow = pl.pallas_call(
         columns_kernel,
-        out_shape=(tile, field, field, pack, pack, inner, inner, south_shape, north_shape, lines),
+        out_shape=(tile, kept, kept, pack, pack, inner, inner, shape_of(56, cols)),
         in_specs=[SMEM] + [HBM] * 11,
-        out_specs=(VMEM, HBM, HBM) + (VMEM,) * 7,
+        out_specs=(VMEM,) * 8,
         scratch_shapes=[
-            pltpu.VMEM(field.shape, jnp.float32),
-            pltpu.VMEM(field.shape, jnp.float32),
             pltpu.VMEM((levels, rows, cols), jnp.float32),
             pltpu.SMEM((2, levels), jnp.float32),
             pltpu.SMEM((2, levels), jnp.float32),
@@ -608,35 +672,63 @@
             )
         ),
     )
-    west_pack, place = lax.optimization_barrier((west_pack, place))
-    west_in = shifted(east_pack, "gx", 1)
-    east_in = shifted(west_pack, "gx", -1)
+    first_in = swapped(first_pack, "gx", True)
+    second_in = swapped(second_pack, "gx", False)
+    u, v, first_rows, second_rows, inner_rows = pl.pallas_call(
+        store_kernel,
+        out_shape=(away, away, rows_shape, rows_shape, lines),
+        in_specs=[SMEM] + [VMEM] * 3,
+        out_specs=(HBM, HBM, VMEM, VMEM, VMEM),
+        scratch_shapes=[pltpu.SemaphoreType.DMA((2,))],
+        cost_estimate=pl.CostEstimate(flops=10**6, bytes_accessed=8 * 10**6, transcendentals=0),
+        compiler_params=SMALL,
+        name="store",
+    )(place, in_vmem(u), in_vmem(v), edge_flow)
     outer = pl.BlockSpec((5 * BLOCK, cols), lambda i: (5, 0))
-    south_rows, north_rows, side = pl.pallas_call(
+    first_rows, second_rows, side, west_in, east_in = pl.pallas_call(
         rows_kernel,
-        out_shape=(south_shape, north_shape, tile),
+        out_shape=(rows_shape, rows_shape, tile, pack, pack),
         grid=(1,),
-        in_specs=[VMEM] * 6 + [pl.BlockSpec(memory_space=pl.ANY)] * 2,
-        out_specs=(outer, outer, VMEM),
-        input_output_aliases={6: 0, 7: 1},
+        in_specs=[SMEM] + [VMEM] * 6 + [pl.BlockSpec(memory_space=pl.ANY)] * 2,
+        out_specs=(outer, outer) + (VMEM,) * 3,
+        input_output_aliases={7: 0, 8: 1},
         compiler_params=SMALL,
         name="rows",
-    )(b, conduct_east, conduct_north, surface_diagonal, west_in, east_in, south_rows, north_rows)
-    south_in = shifted(north_rows, "gy", 1)
-    north_in = shifted(south_rows, "gy", -1)
+    )(
+        place, b, conduct_east, conduct_north, surface_diagonal, first_in, second_in,
+        first_rows, second_rows,
+    )
+    first_in = swapped(first_rows, "gy", True)
+    second_in = swapped(second_rows, "gy", False)
     full = shape_of(rows + 2 * BLOCK, 2 * LANES)
-    v0, v1, v2, rims = pl.pallas_call(
-        krylov_kernel,
-        out_shape=(full, full, full, shape_of(along * GROUP, LANES)),
-        in_specs=[SMEM] + [VMEM] * 18,
-        out_specs=(VMEM,) * 4,
+    line_weights, side_weights = pl.pallas_call(
+        prepare_kernel,
+        out_shape=(shape_of(4, count, cols), shape_of(6, count, cols)),
+        in_specs=[SMEM] + [VMEM] * 11,
+        out_specs=(VMEM,) * 2,
         scratch_shapes=[pltpu.VMEM((count, cols), jnp.float32)] * 3
         + [pltpu.VMEM((2 * LANES, LANES), jnp.float32)],
+        cost_estimate=pl.CostEstimate(flops=10**6, bytes_accessed=4 * 10**6, transcendentals=0),
+        compiler_params=MIDDLE,
+        name="prepare",
+    )(
+        place, flow_east, flow_north, west_in, east_in, first_pack, second_pack, west_inner, east_inner,
+        first_rows, second_rows, inner_rows,
+    )
+    v0, v1, v2, rims, south_in, north_in = pl.pallas_call(
+        krylov_kernel,
+        out_shape=(full, full, full, shape_of(along * GROUP, LANES), rows_shape, rows_shape),
+        in_specs=[SMEM] + [VMEM] * 9,
+        out_specs=(VMEM,) * 6,
+        scratch_shapes=[
+            pltpu.VMEM((count, cols), jnp.float32),
+            pltpu.VMEM((LANES, LANES), jnp.float32),
+        ],
         compiler_params=MIDDLE,
         name="krylov",
     )(
-        place, b, conduct_east, conduct_north, surface_diagonal, side, south_in, north_in, west_in, east_in,
-        flow_east, flow_north, west_pack, east_pack, west_inner, east_inner, south_rows, north_rows, inner_rows,
+        place, b, conduct_east, conduct_north, surface_diagonal, side, first_in, second_in,
+        line_weights, side_weights,
     )
     rims = lax.all_to_all(rims.reshape(along, 1, GROUP * LANES), "gy", 0, 0)
     points = (2 + rows * along // LANES) * LANES

time: 82.8 us -> 79.5 us (0.960)
  starting transfers between devices: 14.9 us -> 9.91 us
  waiting for transfers between devices: 10.7 us -> 7.5 us
  blocking collectives: 38.5 us -> 41.2 us
  Pallas kernels: 17.4 us -> 19.7 us
    ppermute x4, starting transfers between devices: 11.1 us -> 5.95 us  [swapped(): return lax.ppermute(value, axis, pairs)]
    all_to_all x1, blocking collectives: 25.5 us -> 28.8 us  [per_device(): rims = lax.all_to_all(rims.reshape(along, 1, GROUP * LANES), 'gy', 0, 0)]
    ppermute x4, waiting for transfers between devices: 6.57 us -> 3.45 us  [swapped(): return lax.ppermute(value, axis, pairs)]
    pallas_call x2 -> x4, Pallas kernels: 7.46 us -> 10.1 us  [the longest x1 6.14 us: per_device(): pl.pallas_call(columns_kernel, out_shape=(tile, kept, kept, pack, pack, i...]
  transfers between devices with their start and end apart: 5 -> 5, of which waited for: 3 -> 3; matrix products, arithmetic and copies ran while one was open for 0% -> 0% of each run, Pallas kernels for 7% -> 11%
where the time goes in v4:
time: 79.5 us; the launch traced here: 79.2 us
  blocking collectives  41.2 us (52%)
  Pallas kernels  19.7 us (25%)
  starting transfers between devices  9.91 us (12%)
  waiting for transfers between devices  7.5 us (9%)
  between operations  0.8 us (1%)
    all_to_all x1, blocking collectives, per_device(): rims = lax.all_to_all(rims.reshape(along, 1, GROUP * LANES), 'gy', 0, 0)  28.8 us
    all_to_all x1, blocking collectives, per_device(): parts = lax.all_to_all(parts, 'gx', 0, 0)  12.4 us
    pallas_call x1, Pallas kernels, per_device(): pl.pallas_call(columns_kernel, out_shape=(tile, kept, kept, pack, pack, i...  6.14 us
    ppermute x4, starting transfers between devices, swapped(): return lax.ppermute(value, axis, pairs)  5.95 us
    pallas_call x1, Pallas kernels, per_device(): pl.pallas_call(fields_kernel, out_shape=(field, tile), in_specs=[VMEM] *...  5.55 us
    all_to_all x1, waiting for transfers between devices, per_device(): joined = lax.all_to_all(joined.reshape(along, 1, SLOTS * LANES), 'gy', 0, 0)  4.05 us
    all_to_all x1, starting transfers between devices, per_device(): joined = lax.all_to_all(joined.reshape(along, 1, SLOTS * LANES), 'gy', 0, 0)  3.96 us
    ppermute x4, waiting for transfers between devices, swapped(): return lax.ppermute(value, axis, pairs)  3.45 us
  transfers between devices with their start and end apart: 5, of which 3 were waited for; matrix products, arithmetic and copies ran while one was open for 0% of the time, Pallas kernels for 11%

profile of v4, /device:TPU:1, one launch (start us, length us, event | category | flops | bytes accessed | tf_op | source)
XLA Modules:
  0.0 79.2 jit_solution(3387006854666791414)
XLA Ops:
  0.6 0.1 pad_add_fusion.place
  0.7 6.1 %columns.1 = (f32[40,128]{1,0:T(8,128)S(1)}, f32[2,50,40,128]{3,2,1,0:T(8,128)S(1)}, f32[2,50,40,128]{3,2,1,0:T(8,128)S(1)}, f32[40,384]{1,0:T(8,128)S(1)}, f32[...) custom-call(s32[4]{0:T(128)S(1)} %pad_add_fusion.place, ...), custom_call_target="tpu_custom_call" | custom-call | tf_op jit(solution)/shard_map/columns/pallas_call | solution.py:643
  6.9 3.3 %collective-permute-start = (f32[40,384]{1,0:T(8,128)S(1)}, f32[40,384]{1,0:T(8,128)S(1)}, u32[]{:S(2)}, u32[]{:S(2)}) collective-permute-start(f32[40,384]{1,0:T(8,128)S(1)} %get-tuple-element.34.first_pack), channel_id=1, source_target_pairs={{0,32},{32,0},{64,96},{96,64},{128,160},{160,128},{192,224},{224,1... | collective-permute-start | bytes 184328 | tf_op jit(solution)/shard_map/ppermute | solution.py:600
  10.2 1.9 %collective-permute-start.1 = (f32[40,384]{1,0:T(8,128)S(1)}, f32[40,384]{1,0:T(8,128)S(1)}, u32[]{:S(2)}, u32[]{:S(2)}) collective-permute-start(f32[40,384]{1,0:T(8,128)S(1)} %get-tuple-element.35.second_pack), channel_id=1, source_target_pairs={{32,64},{64,32},{96,128},{128,96},{160,192},{192,160},{33,65},{65,... | collective-permute-start | bytes 184328 | tf_op jit(solution)/shard_map/ppermute | solution.py:600
  12.1 0.0 copy-start.2
  12.1 0.0 copy-start.3
  12.1 0.0 copy-start.4
  12.1 0.0 copy-start
  12.2 0.0 copy-start.1
  12.2 2.5 %store.1 = (f32[2,50,40,128]{3,2,1,0:T(8,128)}, f32[2,50,40,128]{3,2,1,0:T(8,128)}, f32[296,128]{1,0:T(8,128)S(1)}, f32[296,128]{1,0:T(8,128)S(1)}, f32[200,128]{1,0:T(8,128)S(1)}) custom-call(s32[4]{0:T(128)S(1)} %pad_add_fusion.place, f32[2,50,40,128]{3,2,1,0:T(8,128)S(1)} %get-tuple-element.36.u, f32[2,50,40,128]{3,2,1,0:T(8,128)S(1)} %get-tuple-element.37.v, ...), custom_call_target="tpu_custom_call" | custom-call | flops 1000000 | bytes 8000000 | tf_op jit(solution)/shard_map/store/pallas_call | solution.py:677
  14.6 0.0 collective-permute-done.first_in
  14.7 1.1 %collective-permute-done.1.second_in = f32[40,384]{1,0:T(8,128)S(1)} collective-permute-done((f32[40,384]{1,0:T(8,128)S(1)}, f32[40,384]{1,0:T(8,128)S(1)}, u32[]{:S(2)}, u32[]{:S(2)}) %collective-permute-start.1) | collective-permute-done | bytes 61472 | tf_op jit(solution)/shard_map/ppermute | solution.py:600
  15.7 0.0 copy-done.2
  15.7 0.0 copy-done.3
  15.7 0.0 copy-done.4
  15.7 0.6 rows.1
  16.4 0.0 collective-permute-start.2
  16.4 0.7 collective-permute-start.3
  17.1 0.0 copy-done
  17.1 0.0 copy-done.1
  17.1 0.0 copy-start.5
  17.1 0.0 copy-start.6
  17.1 0.9 %prepare.1 = (f32[4,200,128]{2,1,0:T(8,128)S(1)}, f32[6,200,128]{2,1,0:T(8,128)S(1)}) custom-call(s32[4]{0:T(128)S(1)} %pad_add_fusion.place, f32[50,40,128]{2,1,0:T(8,128)S(1)} %copy-done, f32[50,40,128]{2,1,0:T(8,128)S(1)} %copy-done.1, f32[40,384]{1,0:T(8,128)S(1)} %get-tuple-element.44.west_in, f32[40,384]{1,0:T(8,128)S(1)} %get-tuple-element.45.east_in, ...), custom_call_target="tpu_custom_call" | custom-call | flops 1000000 | bytes 4000000 | tf_op jit(solution)/shard_map/prepare/pallas_call | solution.py:704
  18.0 2.4 %collective-permute-done.2.first_in = f32[296,128]{1,0:T(8,128)S(1)} collective-permute-done((f32[296,128]{1,0:T(8,128)S(1)}, f32[296,128]{1,0:T(8,128)S(1)}, u32[]{:S(2)}, u32[]{:S(2)}) %collective-permute-start.2) | collective-permute-done | bytes 151584 | tf_op jit(solution)/shard_map/ppermute | solution.py:600
  20.4 0.0 collective-permute-done.3.second_in
  20.4 1.2 %krylov.1 = (f32[56,256]{1,0:T(8,128)S(1)}, f32[56,256]{1,0:T(8,128)S(1)}, f32[56,256]{1,0:T(8,128)S(1)}, f32[800,128]{1,0:T(8,128)S(1)}, f32[296,128]{1,0:T(8,128)S(1)}, /*index=5*/f32[296,128]{1,0:T(8,128)S(1)}) custom-call(s32[4]{0:T(128)S(1)} %pad_add_fusion.place, f32[40,128]{1,0:T(8,128)S(1)} %get-tuple-element.33.b, f32[40,128]{1,0:T(8,128)S(1)} %copy-done.2, ...), custom_call_target="tpu_custom_call" | custom-call | tf_op jit(solution)/shard_map/krylov/pallas_call | solution.py:718
  21.6 28.8 %all_to_all.15 = f32[32,1,3200]{2,1,0:T(1,128)S(1)} all-to-all(f32[32,1,3200]{2,1,0:T(1,128)S(1)} %bitcast.11), channel_id=1, replica_groups=mesh['gx'=8,'gy'=32] {'gy'}, dimensions={0} | all-to-all | bytes 819200 | tf_op jit(solution)/shard_map/all_to_all | solution.py:733
  50.4 0.0 copy-done.5
  50.4 0.0 copy-done.6
  50.4 1.0 %controls.1 = f32[8,16,384]{2,1,0:T(8,128)S(1)} custom-call(s32[4]{0:T(128)S(1)} %pad_add_fusion.place, f32[800,128]{1,0:T(8,128)S(1)} %bitcast.9, s32[36,128]{1,0:T(8,128)S(1)} %bitcast.12, f32[36,128]{1,0:T(8,128)S(1)} %bitcast.13), custom_call_target="tpu_custom_call" | custom-call | tf_op jit(solution)/shard_map/controls/pallas_call | solution.py:735
  51.5 12.4 %all_to_all.16.parts = f32[8,16,384]{2,1,0:T(8,128)S(1)} all-to-all(f32[8,16,384]{2,1,0:T(8,128)S(1)} %controls.1), channel_id=1, replica_groups=mesh['gx'=8,'gy'=32] {'gx'}, dimensions={0} | all-to-all | bytes 393216 | tf_op jit(solution)/shard_map/all_to_all | solution.py:748
  63.8 1.0 %join.1 = (f32[1,128]{1,0:T(1,128)S(1)}, f32[320,128]{1,0:T(8,128)}) custom-call(f32[8,16,384]{2,1,0:T(8,128)S(1)} %all_to_all.16.parts), custom_call_target="tpu_custom_call" | custom-call | tf_op jit(solution)/shard_map/join/pallas_call | solution.py:749
  64.9 4.0 %all-to-all-start.2 = ((f32[32,1,1280]{2,1,0:T(1,128)}), f32[32,1,1280]{2,1,0:T(1,128)S(1)}, u32[]{:S(2)}, u32[]{:S(2)}) async-start(f32[32,1,1280]{2,1,0:T(1,128)} %bitcast.6), calls=%async_computation.2 | async-start | bytes 327680 | tf_op jit(solution)/shard_map/all_to_all | solution.py:758
  68.8 5.6 %fields.1 = (f32[2,50,40,128]{3,2,1,0:T(8,128)}, f32[40,128]{1,0:T(8,128)}) custom-call(f32[1,128]{1,0:T(1,128)S(1)} %get-tuple-element.52.sums_in, f32[56,256]{1,0:T(8,128)S(1)} %get-tuple-element.53.v0, f32[56,256]{1,0:T(8,128)S(1)} %get-tuple-element.54.v1, f32[56,256]{1,0:T(8,128)S(1)} %get-tuple-element.55.v2, ...), custom_call_target="tpu_custom_call" | custom-call | tf_op jit(solution)/shard_map/fields/pallas_call | solution.py:759
  74.4 4.0 %all-to-all-done.2 = f32[32,1,1280]{2,1,0:T(1,128)S(1)} async-done(((f32[32,1,1280]{2,1,0:T(1,128)}), f32[32,1,1280]{2,1,0:T(1,128)S(1)}, u32[]{:S(2)}, u32[]{:S(2)}) %all-to-all-start.2) | async-done | bytes 163872 | tf_op jit(solution)/shard_map/all_to_all | solution.py:758
  78.4 0.8 gather.1
Async XLA Ops:
  6.9 7.8 %collective-permute-start = (f32[40,384]{1,0:T(8,128)S(1)}, f32[40,384]{1,0:T(8,128)S(1)}, u32[]{:S(2)}, u32[]{:S(2)}) collective-permute-start(f32[40,384]{1,0:T(8,128)S(1)} %get-tuple-element.34.first_pack), channel_id=1, source_target_pairs={{0,32},{32,0},{64,96},{96,64},{128,160},{160,128},{192,224},{224,1... | collective-permute-start | bytes 184328 | tf_op jit(solution)/shard_map/ppermute | solution.py:600
  10.2 5.5 %collective-permute-start.1 = (f32[40,384]{1,0:T(8,128)S(1)}, f32[40,384]{1,0:T(8,128)S(1)}, u32[]{:S(2)}, u32[]{:S(2)}) collective-permute-start(f32[40,384]{1,0:T(8,128)S(1)} %get-tuple-element.35.second_pack), channel_id=1, source_target_pairs={{32,64},{64,32},{96,128},{128,96},{160,192},{192,160},{33,65},{65,... | collective-permute-start | bytes 184328 | tf_op jit(solution)/shard_map/ppermute | solution.py:600
  12.1 3.6 %copy-start.2 = (f32[40,128]{1,0:T(8,128)S(1)}, f32[40,128]{1,0:T(8,128)}, u32[]{:S(2)}) copy-start(f32[40,128]{1,0:T(8,128)} %c_east.3) | copy-start | bytes 61444
  12.1 3.6 %copy-start.3 = (f32[40,128]{1,0:T(8,128)S(1)}, f32[40,128]{1,0:T(8,128)}, u32[]{:S(2)}) copy-start(f32[40,128]{1,0:T(8,128)} %c_north.3) | copy-start | bytes 61444
  12.1 3.6 %copy-start.4 = (f32[40,128]{1,0:T(8,128)S(1)}, f32[40,128]{1,0:T(8,128)}, u32[]{:S(2)}) copy-start(f32[40,128]{1,0:T(8,128)} %diag.3) | copy-start | bytes 61444
  12.1 4.9 %copy-start = (f32[50,40,128]{2,1,0:T(8,128)S(1)}, f32[50,40,128]{2,1,0:T(8,128)}, u32[]{:S(2)}) copy-start(f32[50,40,128]{2,1,0:T(8,128)} %flow_east.3) | copy-start | bytes 3072004
  12.2 4.9 %copy-start.1 = (f32[50,40,128]{2,1,0:T(8,128)S(1)}, f32[50,40,128]{2,1,0:T(8,128)}, u32[]{:S(2)}) copy-start(f32[50,40,128]{2,1,0:T(8,128)} %flow_north.3) | copy-start | bytes 3072004
  16.4 4.1 %collective-permute-start.2 = (f32[296,128]{1,0:T(8,128)S(1)}, f32[296,128]{1,0:T(8,128)S(1)}, u32[]{:S(2)}, u32[]{:S(2)}) collective-permute-start(f32[296,128]{1,0:T(8,128)S(1)} %get-tuple-element.42.first_rows), channel_id=1, source_target_pairs={{0,1},{1,0},{2,3},{3,2},{4,5},{5,4},{6,7},{7,6},{8,9},{9,8},{10,11... | collective-permute-start | bytes 454664 | tf_op jit(solution)/shard_map/ppermute | solution.py:600
  16.4 4.0 %collective-permute-start.3 = (f32[296,128]{1,0:T(8,128)S(1)}, f32[296,128]{1,0:T(8,128)S(1)}, u32[]{:S(2)}, u32[]{:S(2)}) collective-permute-start(f32[296,128]{1,0:T(8,128)S(1)} %get-tuple-element.43.second_rows), channel_id=1, source_target_pairs={{1,2},{2,1},{3,4},{4,3},{5,6},{6,5},{7,8},{8,7},{9,10},{10,9},{11,... | collective-permute-start | bytes 454664 | tf_op jit(solution)/shard_map/ppermute | solution.py:600
  17.1 33.3 %copy-start.5 = (s32[4608]{0:T(1024)S(1)}, s32[4608]{0:T(1024)}, u32[]{:S(2)}) copy-start(s32[4608]{0:T(1024)} %param.24) | copy-start | bytes 55300
  17.1 33.3 %copy-start.6 = (f32[4608]{0:T(1024)S(1)}, f32[4608]{0:T(1024)}, u32[]{:S(2)}) copy-start(f32[4608]{0:T(1024)} %param.25) | copy-start | bytes 55300
  64.9 13.6 %all-to-all-start.2 = ((f32[32,1,1280]{2,1,0:T(1,128)}), f32[32,1,1280]{2,1,0:T(1,128)S(1)}, u32[]{:S(2)}, u32[]{:S(2)}) async-start(f32[32,1,1280]{2,1,0:T(1,128)} %bitcast.6), calls=%async_computation.2 | async-start | bytes 327680 | tf_op jit(solution)/shard_map/all_to_all | solution.py:758

commit v5 on v4

--- a/solution.py
+++ b/solution.py
@@ -13,7 +13,6 @@
 GROUP = 25
 GRAM = ((0, 0), (0, 1), (0, 2), (0, 3), (1, 1), (1, 2), (1, 3), (2, 2), (2, 3))
 VMEM = pl.BlockSpec(memory_space=pltpu.VMEM)
-SMEM = pl.BlockSpec(memory_space=pltpu.SMEM)
 HBM = pl.BlockSpec(memory_space=pltpu.HBM)
 MIB = 1024 * 1024
 BIG = pltpu.CompilerParams(vmem_limit_bytes=16 * MIB)
@@ -25,6 +24,11 @@
     return lax.broadcasted_iota(jnp.int32, shape, len(shape) - 1)
 
 
+def own_place():
+    axes = ("gx", "gy")
+    return tuple(map(lax.axis_index, axes)) + tuple(map(lax.axis_size, axes))
+
+
 def moved(value, source, target):
     shift = target - source
     shift = shift % LANES if isinstance(shift, int) else lax.rem(shift + 4 * LANES, LANES)
@@ -32,7 +36,7 @@
 
 
 def columns_kernel(
-    place, forcing_in, loads_in, tracer_in, surface_in, east_flow, north_flow, mix_in, mask_in, c_east_in,
+    forcing_in, loads_in, tracer_in, surface_in, east_flow, north_flow, mix_in, mask_in, c_east_in,
     c_north_in, diag_in,
     b_out, u_out, v_out, first_pack, second_pack, west_inner, east_inner, edge_flow,
     ratios, forcing, loads, tracer, surface, flow_east, flow_north, mix, mask, c_east, c_north, diag,
@@ -40,6 +44,7 @@
 ):
     levels, rows, cols = mask.shape
     shape = (rows, cols)
+    place = own_place()
     zero = jnp.zeros(shape, jnp.float32)
     last = levels - 1
     chunk = 7
@@ -140,8 +145,9 @@
         east = jnp.where(here, moved(field, cols - 3, 4 * a), east)
     pack(slice(2 * LANES, 3 * LANES), west, east)
 
-def store_kernel(place, u, v, edge_flow, u_hbm, v_hbm, first_rows, second_rows, inner_rows, sems):
+def store_kernel(u, v, edge_flow, u_hbm, v_hbm, first_rows, second_rows, inner_rows, sems):
     _, levels, rows, _ = u.shape
+    place = own_place()
     copies = [
         pltpu.make_async_copy(source, target, sems.at[n])
         for n, (source, target) in enumerate(((u, u_hbm), (v, v_hbm)))
@@ -166,11 +172,12 @@
 
 
 def rows_kernel(
-    place, b, c_east, c_north, diag, first_in, second_in, _f, _s,
+    b, c_east, c_north, diag, first_in, second_in, _f, _s,
     first_rows, second_rows, side, west_in, east_in,
 ):
     shape = b.shape
     rows = shape[0]
+    place = own_place()
     lane = lanes_of(shape)
     even = (place[0] & 1) == 0
     west_in[...] = jnp.where(even, second_in[...], first_in[...])
@@ -218,13 +225,14 @@
 
 
 def prepare_kernel(
-    place, flow_east, flow_north, west_in, east_in, first_pack, second_pack, west_inner, east_inner,
+    flow_east, flow_north, west_in, east_in, first_pack, second_pack, west_inner, east_inner,
     first_rows, second_rows, inner_rows,
     line_out, side_out,
     high_buf, low_buf, face_buf, turned,
 ):
     levels, rows, cols = flow_east.shape
     count = 4 * levels
+    place = own_place()
 
     @pl.when((place[1] == 0) | (place[1] == place[3] - 1))
     def _():
@@ -286,13 +294,14 @@
 
 
 def krylov_kernel(
-    place, b, c_east, c_north, diag, side, first_in, second_in, line_in, side_in,
+    b, c_east, c_north, diag, side, first_in, second_in, line_in, side_in,
     v0_out, v1_out, v2_out, out, south_in, north_in,
     low_buf, turned,
 ):
     rows, cols = b.shape
     count = line_in.shape[1]
     levels = count // 4
+    place = own_place()
     even = (place[1] & 1) == 0
     south_in[...] = jnp.where(even, second_in[...], first_in[...])
     north_in[...] = jnp.where(even, first_in[...], second_in[...])
@@ -492,8 +501,9 @@
         copy.wait()
 
 
-def controls_kernel(place, rims, point_map, point_weight, out, values, hot, total):
+def controls_kernel(rims, point_map, point_weight, out, values, hot, total):
     peers, high, wide = out.shape
+    place = own_place()
     lane = lanes_of((1, LANES))
     rows = 40
     tiles = rows * (rims.shape[0] // GROUP) // LANES
@@ -548,10 +558,10 @@
             point_tile(2 + tile, jnp.concatenate(parts, axis=0), first + tile)
         product((2 + tiles) * LANES)
 
-    sums = rims[GROUP - 1 : GROUP, :]
-    for at in range(GROUP, rims.shape[0], GROUP):
-        sums = sums + rims[at + GROUP - 1 : at + GROUP, :]
-    sums = pltpu.roll(sums, 64, 1)
+    sums = [rims[at - 1 : at, :] for at in range(GROUP, rims.shape[0] + 1, GROUP)]
+    while len(sums) > 1:
+        sums = [a + b for a, b in zip(sums[0::2], sums[1::2])]
+    sums = pltpu.roll(sums[0], 64, 1)
     for peer in range(peers):
         at = 3 * high * peer
         out[peer] = (
@@ -629,7 +639,6 @@
 ):
     levels, rows, cols = flow_east.shape
     across, along = lax.axis_size("gx"), lax.axis_size("gy")
-    place = jnp.stack([lax.axis_index("gx"), lax.axis_index("gy"), across, along]).astype(jnp.int32)
     point_map = control_map.reshape(-1, LANES)
     point_weight = control_weight.reshape(-1, LANES)
 
@@ -643,7 +652,7 @@
     b, u, v, first_pack, second_pack, west_inner, east_inner, edge_flow = pl.pallas_call(
         columns_kernel,
         out_shape=(tile, kept, kept, pack, pack, inner, inner, shape_of(56, cols)),
-        in_specs=[SMEM] + [HBM] * 11,
+        in_specs=[HBM] * 11,
         out_specs=(VMEM,) * 8,
         scratch_shapes=[
             pltpu.VMEM((levels, rows, cols), jnp.float32),
@@ -663,7 +672,6 @@
         compiler_params=BIG,
         name="columns",
     )(
-        place,
         *(
             in_hbm(value)
             for value in (
@@ -677,25 +685,25 @@
     u, v, first_rows, second_rows, inner_rows = pl.pallas_call(
         store_kernel,
         out_shape=(away, away, rows_shape, rows_shape, lines),
-        in_specs=[SMEM] + [VMEM] * 3,
+        in_specs=[VMEM] * 3,
         out_specs=(HBM, HBM, VMEM, VMEM, VMEM),
         scratch_shapes=[pltpu.SemaphoreType.DMA((2,))],
         cost_estimate=pl.CostEstimate(flops=10**6, bytes_accessed=8 * 10**6, transcendentals=0),
         compiler_params=SMALL,
         name="store",
-    )(place, in_vmem(u), in_vmem(v), edge_flow)
+    )(in_vmem(u), in_vmem(v), edge_flow)
     outer = pl.BlockSpec((5 * BLOCK, cols), lambda i: (5, 0))
     first_rows, second_rows, side, west_in, east_in = pl.pallas_call(
         rows_kernel,
         out_shape=(rows_shape, rows_shape, tile, pack, pack),
         grid=(1,),
-        in_specs=[SMEM] + [VMEM] * 6 + [pl.BlockSpec(memory_space=pl.ANY)] * 2,
+        in_specs=[VMEM] * 6 + [pl.BlockSpec(memory_space=pl.ANY)] * 2,
         out_specs=(outer, outer) + (VMEM,) * 3,
-        input_output_aliases={7: 0, 8: 1},
+        input_output_aliases={6: 0, 7: 1},
         compiler_params=SMALL,
         name="rows",
     )(
-        place, b, conduct_east, conduct_north, surface_diagonal, first_in, second_in,
+        b, conduct_east, conduct_north, surface_diagonal, first_in, second_in,
         first_rows, second_rows,
     )
     first_in = swapped(first_rows, "gy", True)
@@ -704,7 +712,7 @@
     line_weights, side_weights = pl.pallas_call(
         prepare_kernel,
         out_shape=(shape_of(4, count, cols), shape_of(6, count, cols)),
-        in_specs=[SMEM] + [VMEM] * 11,
+        in_specs=[VMEM] * 11,
         out_specs=(VMEM,) * 2,
         scratch_shapes=[pltpu.VMEM((count, cols), jnp.float32)] * 3
         + [pltpu.VMEM((2 * LANES, LANES), jnp.float32)],
@@ -712,13 +720,13 @@
         compiler_params=MIDDLE,
         name="prepare",
     )(
-        place, flow_east, flow_north, west_in, east_in, first_pack, second_pack, west_inner, east_inner,
+        flow_east, flow_north, west_in, east_in, first_pack, second_pack, west_inner, east_inner,
         first_rows, second_rows, inner_rows,
     )
     v0, v1, v2, rims, south_in, north_in = pl.pallas_call(
         krylov_kernel,
         out_shape=(full, full, full, shape_of(along * GROUP, LANES), rows_shape, rows_shape),
-        in_specs=[SMEM] + [VMEM] * 9,
+        in_specs=[VMEM] * 9,
         out_specs=(VMEM,) * 6,
         scratch_shapes=[
             pltpu.VMEM((count, cols), jnp.float32),
@@ -727,7 +735,7 @@
         compiler_params=MIDDLE,
         name="krylov",
     )(
-        place, b, conduct_east, conduct_north, surface_diagonal, side, first_in, second_in,
+        b, conduct_east, conduct_north, surface_diagonal, side, first_in, second_in,
         line_weights, side_weights,
     )
     rims = lax.all_to_all(rims.reshape(along, 1, GROUP * LANES), "gy", 0, 0)
@@ -735,7 +743,7 @@
     parts = pl.pallas_call(
         controls_kernel,
         out_shape=shape_of(across, 16, 3 * LANES),
-        in_specs=[SMEM] + [VMEM] * 3,
+        in_specs=[VMEM] * 3,
         out_specs=VMEM,
         scratch_shapes=[
             pltpu.VMEM((across * 48, points), jnp.bfloat16),
@@ -744,7 +752,7 @@
         ],
         compiler_params=MIDDLE,
         name="controls",
-    )(place, rims.reshape(along * GROUP, LANES), point_map, point_weight)
+    )(rims.reshape(along * GROUP, LANES), point_map, point_weight)
     parts = lax.all_to_all(parts, "gx", 0, 0)
     sums, joined = pl.pallas_call(
         join_kernel,

time: 79.5 us -> 77.3 us (0.972)
  Pallas kernels: 19.7 us -> 16.6 us
  waiting for transfers between devices: 7.5 us -> 8.42 us
    ppermute x4, waiting for transfers between devices: 3.45 us -> 4.37 us  [swapped(): return lax.ppermute(value, axis, pairs)]
  transfers between devices with their start and end apart: 5 -> 5, of which waited for: 3 -> 3; matrix products, arithmetic and copies ran while one was open for 0% -> 0% of each run, Pallas kernels for 11% -> 10%
where the time goes in v5:
time: 77.3 us; the launch traced here: 77 us
  blocking collectives  41.2 us (53%)
  Pallas kernels  16.6 us (21%)
  starting transfers between devices  9.89 us (13%)
  waiting for transfers between devices  8.42 us (11%)
  between operations  0.79 us (1%)
    all_to_all x1, blocking collectives, per_device(): rims = lax.all_to_all(rims.reshape(along, 1, GROUP * LANES), 'gy', 0, 0)  28.6 us
    all_to_all x1, blocking collectives, per_device(): parts = lax.all_to_all(parts, 'gx', 0, 0)  12.6 us
    ppermute x4, starting transfers between devices, swapped(): return lax.ppermute(value, axis, pairs)  5.95 us
    pallas_call x1, Pallas kernels, per_device(): pl.pallas_call(columns_kernel, out_shape=(tile, kept, kept, pack, pack, i...  5.63 us
    pallas_call x1, Pallas kernels, per_device(): pl.pallas_call(fields_kernel, out_shape=(field, tile), in_specs=[VMEM] *...  5.55 us
    ppermute x4, waiting for transfers between devices, swapped(): return lax.ppermute(value, axis, pairs)  4.37 us
    all_to_all x1, waiting for transfers between devices, per_device(): joined = lax.all_to_all(joined.reshape(along, 1, SLOTS * LANES), 'gy', 0, 0)  4.05 us
    all_to_all x1, starting transfers between devices, per_device(): joined = lax.all_to_all(joined.reshape(along, 1, SLOTS * LANES), 'gy', 0, 0)  3.94 us
  transfers between devices with their start and end apart: 5, of which 3 were waited for; matrix products, arithmetic and copies ran while one was open for 0% of the time, Pallas kernels for 10%

profile of v5, /device:TPU:1, one launch (start us, length us, event | category | flops | bytes accessed | tf_op | source)
XLA Modules:
  0.0 77.0 jit_solution(1770847489642424684)
XLA Ops:
  0.6 5.6 %columns.1 = (f32[40,128]{1,0:T(8,128)S(1)}, f32[2,50,40,128]{3,2,1,0:T(8,128)S(1)}, f32[2,50,40,128]{3,2,1,0:T(8,128)S(1)}, f32[40,384]{1,0:T(8,128)S(1)}, f32[...) custom-call(f32[2,50]{1,0:T(2,128)} %forcing_in.1, ...), custom_call_target="tpu_custom_call" | custom-call | tf_op jit(solution)/shard_map/columns/pallas_call | solution.py:652
  6.3 3.3 %collective-permute-start = (f32[40,384]{1,0:T(8,128)S(1)}, f32[40,384]{1,0:T(8,128)S(1)}, u32[]{:S(2)}, u32[]{:S(2)}) collective-permute-start(f32[40,384]{1,0:T(8,128)S(1)} %get-tuple-element.34.first_pack), channel_id=1, source_target_pairs={{0,32},{32,0},{64,96},{96,64},{128,160},{160,128},{192,224},{224,1... | collective-permute-start | bytes 184328 | tf_op jit(solution)/shard_map/ppermute | solution.py:610
  9.6 1.9 %collective-permute-start.1 = (f32[40,384]{1,0:T(8,128)S(1)}, f32[40,384]{1,0:T(8,128)S(1)}, u32[]{:S(2)}, u32[]{:S(2)}) collective-permute-start(f32[40,384]{1,0:T(8,128)S(1)} %get-tuple-element.35.second_pack), channel_id=1, source_target_pairs={{32,64},{64,32},{96,128},{128,96},{160,192},{192,160},{33,65},{65,... | collective-permute-start | bytes 184328 | tf_op jit(solution)/shard_map/ppermute | solution.py:610
  11.5 0.0 copy-start.2
  11.5 0.0 copy-start.3
  11.5 0.0 copy-start.4
  11.6 0.0 copy-start
  11.6 0.0 copy-start.1
  11.6 2.1 %store.1 = (f32[2,50,40,128]{3,2,1,0:T(8,128)}, f32[2,50,40,128]{3,2,1,0:T(8,128)}, f32[296,128]{1,0:T(8,128)S(1)}, f32[296,128]{1,0:T(8,128)S(1)}, f32[200,128]{1,0:T(8,128)S(1)}) custom-call(f32[2,50,40,128]{3,2,1,0:T(8,128)S(1)} %get-tuple-element.36.u, f32[2,50,40,128]{3,2,1,0:T(8,128)S(1)} %get-tuple-element.37.v, f32[56,128]{1,0:T(8,128)S(1)} %get-tuple-element.38.edge_flow), custom_call_target="tpu_custom_call" | custom-call | flops 1000000 | bytes 8000000 | tf_op jit(solution)/shard_map/store/pallas_call | solution.py:685
  13.7 0.0 collective-permute-done.first_in
  13.7 1.4 %collective-permute-done.1.second_in = f32[40,384]{1,0:T(8,128)S(1)} collective-permute-done((f32[40,384]{1,0:T(8,128)S(1)}, f32[40,384]{1,0:T(8,128)S(1)}, u32[]{:S(2)}, u32[]{:S(2)}) %collective-permute-start.1) | collective-permute-done | bytes 61472 | tf_op jit(solution)/shard_map/ppermute | solution.py:610
  15.1 0.0 copy-done.2
  15.1 0.0 copy-done.3
  15.1 0.0 copy-done.4
  15.1 0.1 rows.1
  15.2 0.0 collective-permute-start.2
  15.3 0.7 collective-permute-start.3
  16.0 0.0 copy-done
  16.0 0.0 copy-done.1
  16.0 0.0 copy-start.5
  16.0 0.0 copy-start.6
  16.0 0.4 prepare.1
  16.4 2.9 %collective-permute-done.2.first_in = f32[296,128]{1,0:T(8,128)S(1)} collective-permute-done((f32[296,128]{1,0:T(8,128)S(1)}, f32[296,128]{1,0:T(8,128)S(1)}, u32[]{:S(2)}, u32[]{:S(2)}) %collective-permute-start.2) | collective-permute-done | bytes 151584 | tf_op jit(solution)/shard_map/ppermute | solution.py:610
  19.3 0.0 collective-permute-done.3.second_in
  19.3 0.6 krylov.1
  19.9 28.6 %all_to_all.15 = f32[32,1,3200]{2,1,0:T(1,128)S(1)} all-to-all(f32[32,1,3200]{2,1,0:T(1,128)S(1)} %bitcast.9), channel_id=1, replica_groups=mesh['gx'=8,'gy'=32] {'gy'}, dimensions={0} | all-to-all | bytes 819200 | tf_op jit(solution)/shard_map/all_to_all | solution.py:741
  48.6 0.0 copy-done.5
  48.6 0.0 copy-done.6
  48.6 0.5 controls.1
  49.0 12.6 %all_to_all.16.parts = f32[8,16,384]{2,1,0:T(8,128)S(1)} all-to-all(f32[8,16,384]{2,1,0:T(8,128)S(1)} %controls.1), channel_id=1, replica_groups=mesh['gx'=8,'gy'=32] {'gx'}, dimensions={0} | all-to-all | bytes 393216 | tf_op jit(solution)/shard_map/all_to_all | solution.py:756
  61.6 1.0 %join.1 = (f32[1,128]{1,0:T(1,128)S(1)}, f32[320,128]{1,0:T(8,128)}) custom-call(f32[8,16,384]{2,1,0:T(8,128)S(1)} %all_to_all.16.parts), custom_call_target="tpu_custom_call" | custom-call | tf_op jit(solution)/shard_map/join/pallas_call | solution.py:757
  62.6 3.9 %all-to-all-start.2 = ((f32[32,1,1280]{2,1,0:T(1,128)}), f32[32,1,1280]{2,1,0:T(1,128)S(1)}, u32[]{:S(2)}, u32[]{:S(2)}) async-start(f32[32,1,1280]{2,1,0:T(1,128)} %bitcast.4), calls=%async_computation.2 | async-start | bytes 327680 | tf_op jit(solution)/shard_map/all_to_all | solution.py:766
  66.6 5.6 %fields.1 = (f32[2,50,40,128]{3,2,1,0:T(8,128)}, f32[40,128]{1,0:T(8,128)}) custom-call(f32[1,128]{1,0:T(1,128)S(1)} %get-tuple-element.52.sums_in, f32[56,256]{1,0:T(8,128)S(1)} %get-tuple-element.53.v0, f32[56,256]{1,0:T(8,128)S(1)} %get-tuple-element.54.v1, f32[56,256]{1,0:T(8,128)S(1)} %get-tuple-element.55.v2, ...), custom_call_target="tpu_custom_call" | custom-call | tf_op jit(solution)/shard_map/fields/pallas_call | solution.py:767
  72.1 4.0 %all-to-all-done.2 = f32[32,1,1280]{2,1,0:T(1,128)S(1)} async-done(((f32[32,1,1280]{2,1,0:T(1,128)}), f32[32,1,1280]{2,1,0:T(1,128)S(1)}, u32[]{:S(2)}, u32[]{:S(2)}) %all-to-all-start.2) | async-done | bytes 163872 | tf_op jit(solution)/shard_map/all_to_all | solution.py:766
  76.2 0.8 %gather.1 = f32[10,2,50]{2,1,0:T(2,128)} custom-call(f32[320,128]{1,0:T(8,128)S(1)} %bitcast.8), custom_call_target="tpu_custom_call" | custom-call | tf_op jit(solution)/shard_map/gather/pallas_call | solution.py:786
Async XLA Ops:
  6.3 7.4 %collective-permute-start = (f32[40,384]{1,0:T(8,128)S(1)}, f32[40,384]{1,0:T(8,128)S(1)}, u32[]{:S(2)}, u32[]{:S(2)}) collective-permute-start(f32[40,384]{1,0:T(8,128)S(1)} %get-tuple-element.34.first_pack), channel_id=1, source_target_pairs={{0,32},{32,0},{64,96},{96,64},{128,160},{160,128},{192,224},{224,1... | collective-permute-start | bytes 184328 | tf_op jit(solution)/shard_map/ppermute | solution.py:610
  9.6 5.5 %collective-permute-start.1 = (f32[40,384]{1,0:T(8,128)S(1)}, f32[40,384]{1,0:T(8,128)S(1)}, u32[]{:S(2)}, u32[]{:S(2)}) collective-permute-start(f32[40,384]{1,0:T(8,128)S(1)} %get-tuple-element.35.second_pack), channel_id=1, source_target_pairs={{32,64},{64,32},{96,128},{128,96},{160,192},{192,160},{33,65},{65,... | collective-permute-start | bytes 184328 | tf_op jit(solution)/shard_map/ppermute | solution.py:610
  11.5 3.6 %copy-start.2 = (f32[40,128]{1,0:T(8,128)S(1)}, f32[40,128]{1,0:T(8,128)}, u32[]{:S(2)}) copy-start(f32[40,128]{1,0:T(8,128)} %c_east.3) | copy-start | bytes 61444
  11.5 3.6 %copy-start.3 = (f32[40,128]{1,0:T(8,128)S(1)}, f32[40,128]{1,0:T(8,128)}, u32[]{:S(2)}) copy-start(f32[40,128]{1,0:T(8,128)} %c_north.3) | copy-start | bytes 61444
  11.5 3.6 %copy-start.4 = (f32[40,128]{1,0:T(8,128)S(1)}, f32[40,128]{1,0:T(8,128)}, u32[]{:S(2)}) copy-start(f32[40,128]{1,0:T(8,128)} %diag.3) | copy-start | bytes 61444
  11.6 4.4 %copy-start = (f32[50,40,128]{2,1,0:T(8,128)S(1)}, f32[50,40,128]{2,1,0:T(8,128)}, u32[]{:S(2)}) copy-start(f32[50,40,128]{2,1,0:T(8,128)} %flow_east.3) | copy-start | bytes 3072004
  11.6 4.4 %copy-start.1 = (f32[50,40,128]{2,1,0:T(8,128)S(1)}, f32[50,40,128]{2,1,0:T(8,128)}, u32[]{:S(2)}) copy-start(f32[50,40,128]{2,1,0:T(8,128)} %flow_north.3) | copy-start | bytes 3072004
  15.2 4.1 %collective-permute-start.2 = (f32[296,128]{1,0:T(8,128)S(1)}, f32[296,128]{1,0:T(8,128)S(1)}, u32[]{:S(2)}, u32[]{:S(2)}) collective-permute-start(f32[296,128]{1,0:T(8,128)S(1)} %get-tuple-element.42.first_rows), channel_id=1, source_target_pairs={{0,1},{1,0},{2,3},{3,2},{4,5},{5,4},{6,7},{7,6},{8,9},{9,8},{10,11... | collective-permute-start | bytes 454664 | tf_op jit(solution)/shard_map/ppermute | solution.py:610
  15.3 4.0 %collective-permute-start.3 = (f32[296,128]{1,0:T(8,128)S(1)}, f32[296,128]{1,0:T(8,128)S(1)}, u32[]{:S(2)}, u32[]{:S(2)}) collective-permute-start(f32[296,128]{1,0:T(8,128)S(1)} %get-tuple-element.43.second_rows), channel_id=1, source_target_pairs={{1,2},{2,1},{3,4},{4,3},{5,6},{6,5},{7,8},{8,7},{9,10},{10,9},{11,... | collective-permute-start | bytes 454664 | tf_op jit(solution)/shard_map/ppermute | solution.py:610
  16.0 32.6 %copy-start.5 = (s32[4608]{0:T(1024)S(1)}, s32[4608]{0:T(1024)}, u32[]{:S(2)}) copy-start(s32[4608]{0:T(1024)} %param.24) | copy-start | bytes 55300
  16.0 32.6 %copy-start.6 = (f32[4608]{0:T(1024)S(1)}, f32[4608]{0:T(1024)}, u32[]{:S(2)}) copy-start(f32[4608]{0:T(1024)} %param.25) | copy-start | bytes 55300
  62.6 13.6 %all-to-all-start.2 = ((f32[32,1,1280]{2,1,0:T(1,128)}), f32[32,1,1280]{2,1,0:T(1,128)S(1)}, u32[]{:S(2)}, u32[]{:S(2)}) async-start(f32[32,1,1280]{2,1,0:T(1,128)} %bitcast.4), calls=%async_computation.2 | async-start | bytes 327680 | tf_op jit(solution)/shard_map/all_to_all | solution.py:766

commit v6 on v5

--- a/solution.py
+++ b/solution.py
@@ -99,11 +99,7 @@
         u_out[0, k], u_out[1, k], v_out[0, k], v_out[1, k] = reds
         carry = (kappa, ratio, *reds, total)
     _, *sols, total = level_step(last, carry, zero)
-    for copy in flats:
-        copy.wait()
-    total = total + surface[...]
     b_out[...] = total
-
     for k in range(last, -1, -1):
         if k < last:
             ratio = ratios[k]
@@ -112,6 +108,10 @@
         wet = mask[k].astype(jnp.float32)
         fields = [wet * sol for sol in sols]
         u_out[0, k], u_out[1, k], v_out[0, k], v_out[1, k] = fields
+    for copy in flats:
+        copy.wait()
+    total = b_out[...] + surface[...]
+    b_out[...] = total
     lane = lanes_of((1, cols))
     even = (place[0] & 1) == 0
 

time: 77.3 us -> 77 us (level)
  no operation moved by 1% of the time
where the time goes in v6:
time: 77 us; the launch traced here: 76.7 us
  blocking collectives  41.2 us (54%)
  Pallas kernels  16.3 us (21%)
  starting transfers between devices  9.91 us (13%)
  waiting for transfers between devices  8.42 us (11%)
  between operations  0.79 us (1%)
    all_to_all x1, blocking collectives, per_device(): rims = lax.all_to_all(rims.reshape(along, 1, GROUP * LANES), 'gy', 0, 0)  28.6 us
    all_to_all x1, blocking collectives, per_device(): parts = lax.all_to_all(parts, 'gx', 0, 0)  12.6 us
    ppermute x4, starting transfers between devices, swapped(): return lax.ppermute(value, axis, pairs)  5.95 us
    pallas_call x1, Pallas kernels, per_device(): pl.pallas_call(fields_kernel, out_shape=(field, tile), in_specs=[VMEM] *...  5.55 us
    pallas_call x1, Pallas kernels, per_device(): pl.pallas_call(columns_kernel, out_shape=(tile, kept, kept, pack, pack, i...  5.32 us
    ppermute x4, waiting for transfers between devices, swapped(): return lax.ppermute(value, axis, pairs)  4.37 us
    all_to_all x1, waiting for transfers between devices, per_device(): joined = lax.all_to_all(joined.reshape(along, 1, SLOTS * LANES), 'gy', 0, 0)  4.05 us
    all_to_all x1, starting transfers between devices, per_device(): joined = lax.all_to_all(joined.reshape(along, 1, SLOTS * LANES), 'gy', 0, 0)  3.96 us
  transfers between devices with their start and end apart: 5, of which 3 were waited for; matrix products, arithmetic and copies ran while one was open for 0% of the time, Pallas kernels for 10%

profile of v6, /device:TPU:1, one launch (start us, length us, event | category | flops | bytes accessed | tf_op | source)
XLA Modules:
  0.0 76.7 jit_solution(14509452392708245678)
XLA Ops:
  0.6 5.3 %columns.1 = (f32[40,128]{1,0:T(8,128)S(1)}, f32[2,50,40,128]{3,2,1,0:T(8,128)S(1)}, f32[2,50,40,128]{3,2,1,0:T(8,128)S(1)}, f32[40,384]{1,0:T(8,128)S(1)}, f32[...) custom-call(f32[2,50]{1,0:T(2,128)} %forcing_in.1, ...), custom_call_target="tpu_custom_call" | custom-call | tf_op jit(solution)/shard_map/columns/pallas_call | solution.py:652
  6.0 3.3 %collective-permute-start = (f32[40,384]{1,0:T(8,128)S(1)}, f32[40,384]{1,0:T(8,128)S(1)}, u32[]{:S(2)}, u32[]{:S(2)}) collective-permute-start(f32[40,384]{1,0:T(8,128)S(1)} %get-tuple-element.34.first_pack), channel_id=1, source_target_pairs={{0,32},{32,0},{64,96},{96,64},{128,160},{160,128},{192,224},{224,1... | collective-permute-start | bytes 184328 | tf_op jit(solution)/shard_map/ppermute | solution.py:610
  9.3 1.9 %collective-permute-start.1 = (f32[40,384]{1,0:T(8,128)S(1)}, f32[40,384]{1,0:T(8,128)S(1)}, u32[]{:S(2)}, u32[]{:S(2)}) collective-permute-start(f32[40,384]{1,0:T(8,128)S(1)} %get-tuple-element.35.second_pack), channel_id=1, source_target_pairs={{32,64},{64,32},{96,128},{128,96},{160,192},{192,160},{33,65},{65,... | collective-permute-start | bytes 184328 | tf_op jit(solution)/shard_map/ppermute | solution.py:610
  11.2 0.0 copy-start.2
  11.2 0.0 copy-start.3
  11.2 0.0 copy-start.4
  11.2 0.0 copy-start
  11.3 0.0 copy-start.1
  11.3 2.1 %store.1 = (f32[2,50,40,128]{3,2,1,0:T(8,128)}, f32[2,50,40,128]{3,2,1,0:T(8,128)}, f32[296,128]{1,0:T(8,128)S(1)}, f32[296,128]{1,0:T(8,128)S(1)}, f32[200,128]{1,0:T(8,128)S(1)}) custom-call(f32[2,50,40,128]{3,2,1,0:T(8,128)S(1)} %get-tuple-element.36.u, f32[2,50,40,128]{3,2,1,0:T(8,128)S(1)} %get-tuple-element.37.v, f32[56,128]{1,0:T(8,128)S(1)} %get-tuple-element.38.edge_flow), custom_call_target="tpu_custom_call" | custom-call | flops 1000000 | bytes 8000000 | tf_op jit(solution)/shard_map/store/pallas_call | solution.py:685
  13.4 0.0 collective-permute-done.first_in
  13.4 1.4 %collective-permute-done.1.second_in = f32[40,384]{1,0:T(8,128)S(1)} collective-permute-done((f32[40,384]{1,0:T(8,128)S(1)}, f32[40,384]{1,0:T(8,128)S(1)}, u32[]{:S(2)}, u32[]{:S(2)}) %collective-permute-start.1) | collective-permute-done | bytes 61472 | tf_op jit(solution)/shard_map/ppermute | solution.py:610
  14.8 0.0 copy-done.2
  14.8 0.0 copy-done.3
  14.8 0.0 copy-done.4
  14.8 0.1 rows.1
  14.9 0.0 collective-permute-start.2
  15.0 0.7 collective-permute-start.3
  15.7 0.0 copy-done
  15.7 0.0 copy-done.1
  15.7 0.0 copy-start.5
  15.7 0.0 copy-start.6
  15.7 0.4 prepare.1
  16.1 2.9 %collective-permute-done.2.first_in = f32[296,128]{1,0:T(8,128)S(1)} collective-permute-done((f32[296,128]{1,0:T(8,128)S(1)}, f32[296,128]{1,0:T(8,128)S(1)}, u32[]{:S(2)}, u32[]{:S(2)}) %collective-permute-start.2) | collective-permute-done | bytes 151584 | tf_op jit(solution)/shard_map/ppermute | solution.py:610
  19.0 0.0 collective-permute-done.3.second_in
  19.0 0.6 krylov.1
  19.6 28.6 %all_to_all.15 = f32[32,1,3200]{2,1,0:T(1,128)S(1)} all-to-all(f32[32,1,3200]{2,1,0:T(1,128)S(1)} %bitcast.9), channel_id=1, replica_groups=mesh['gx'=8,'gy'=32] {'gy'}, dimensions={0} | all-to-all | bytes 819200 | tf_op jit(solution)/shard_map/all_to_all | solution.py:741
  48.2 0.0 copy-done.5
  48.3 0.0 copy-done.6
  48.3 0.5 controls.1
  48.7 12.6 %all_to_all.16.parts = f32[8,16,384]{2,1,0:T(8,128)S(1)} all-to-all(f32[8,16,384]{2,1,0:T(8,128)S(1)} %controls.1), channel_id=1, replica_groups=mesh['gx'=8,'gy'=32] {'gx'}, dimensions={0} | all-to-all | bytes 393216 | tf_op jit(solution)/shard_map/all_to_all | solution.py:756
  61.3 1.0 %join.1 = (f32[1,128]{1,0:T(1,128)S(1)}, f32[320,128]{1,0:T(8,128)}) custom-call(f32[8,16,384]{2,1,0:T(8,128)S(1)} %all_to_all.16.parts), custom_call_target="tpu_custom_call" | custom-call | tf_op jit(solution)/shard_map/join/pallas_call | solution.py:757
  62.3 4.0 %all-to-all-start.2 = ((f32[32,1,1280]{2,1,0:T(1,128)}), f32[32,1,1280]{2,1,0:T(1,128)S(1)}, u32[]{:S(2)}, u32[]{:S(2)}) async-start(f32[32,1,1280]{2,1,0:T(1,128)} %bitcast.4), calls=%async_computation.2 | async-start | bytes 327680 | tf_op jit(solution)/shard_map/all_to_all | solution.py:766
  66.3 5.6 %fields.1 = (f32[2,50,40,128]{3,2,1,0:T(8,128)}, f32[40,128]{1,0:T(8,128)}) custom-call(f32[1,128]{1,0:T(1,128)S(1)} %get-tuple-element.52.sums_in, f32[56,256]{1,0:T(8,128)S(1)} %get-tuple-element.53.v0, f32[56,256]{1,0:T(8,128)S(1)} %get-tuple-element.54.v1, f32[56,256]{1,0:T(8,128)S(1)} %get-tuple-element.55.v2, ...), custom_call_target="tpu_custom_call" | custom-call | tf_op jit(solution)/shard_map/fields/pallas_call | solution.py:767
  71.9 4.0 %all-to-all-done.2 = f32[32,1,1280]{2,1,0:T(1,128)S(1)} async-done(((f32[32,1,1280]{2,1,0:T(1,128)}), f32[32,1,1280]{2,1,0:T(1,128)S(1)}, u32[]{:S(2)}, u32[]{:S(2)}) %all-to-all-start.2) | async-done | bytes 163872 | tf_op jit(solution)/shard_map/all_to_all | solution.py:766
  75.9 0.8 %gather.1 = f32[10,2,50]{2,1,0:T(2,128)} custom-call(f32[320,128]{1,0:T(8,128)S(1)} %bitcast.8), custom_call_target="tpu_custom_call" | custom-call | tf_op jit(solution)/shard_map/gather/pallas_call | solution.py:786
Async XLA Ops:
  6.0 7.4 %collective-permute-start = (f32[40,384]{1,0:T(8,128)S(1)}, f32[40,384]{1,0:T(8,128)S(1)}, u32[]{:S(2)}, u32[]{:S(2)}) collective-permute-start(f32[40,384]{1,0:T(8,128)S(1)} %get-tuple-element.34.first_pack), channel_id=1, source_target_pairs={{0,32},{32,0},{64,96},{96,64},{128,160},{160,128},{192,224},{224,1... | collective-permute-start | bytes 184328 | tf_op jit(solution)/shard_map/ppermute | solution.py:610
  9.3 5.5 %collective-permute-start.1 = (f32[40,384]{1,0:T(8,128)S(1)}, f32[40,384]{1,0:T(8,128)S(1)}, u32[]{:S(2)}, u32[]{:S(2)}) collective-permute-start(f32[40,384]{1,0:T(8,128)S(1)} %get-tuple-element.35.second_pack), channel_id=1, source_target_pairs={{32,64},{64,32},{96,128},{128,96},{160,192},{192,160},{33,65},{65,... | collective-permute-start | bytes 184328 | tf_op jit(solution)/shard_map/ppermute | solution.py:610
  11.2 3.6 %copy-start.2 = (f32[40,128]{1,0:T(8,128)S(1)}, f32[40,128]{1,0:T(8,128)}, u32[]{:S(2)}) copy-start(f32[40,128]{1,0:T(8,128)} %c_east.3) | copy-start | bytes 61444
  11.2 3.6 %copy-start.3 = (f32[40,128]{1,0:T(8,128)S(1)}, f32[40,128]{1,0:T(8,128)}, u32[]{:S(2)}) copy-start(f32[40,128]{1,0:T(8,128)} %c_north.3) | copy-start | bytes 61444
  11.2 3.6 %copy-start.4 = (f32[40,128]{1,0:T(8,128)S(1)}, f32[40,128]{1,0:T(8,128)}, u32[]{:S(2)}) copy-start(f32[40,128]{1,0:T(8,128)} %diag.3) | copy-start | bytes 61444
  11.2 4.4 %copy-start = (f32[50,40,128]{2,1,0:T(8,128)S(1)}, f32[50,40,128]{2,1,0:T(8,128)}, u32[]{:S(2)}) copy-start(f32[50,40,128]{2,1,0:T(8,128)} %flow_east.3) | copy-start | bytes 3072004
  11.3 4.4 %copy-start.1 = (f32[50,40,128]{2,1,0:T(8,128)S(1)}, f32[50,40,128]{2,1,0:T(8,128)}, u32[]{:S(2)}) copy-start(f32[50,40,128]{2,1,0:T(8,128)} %flow_north.3) | copy-start | bytes 3072004
  14.9 4.1 %collective-permute-start.2 = (f32[296,128]{1,0:T(8,128)S(1)}, f32[296,128]{1,0:T(8,128)S(1)}, u32[]{:S(2)}, u32[]{:S(2)}) collective-permute-start(f32[296,128]{1,0:T(8,128)S(1)} %get-tuple-element.42.first_rows), channel_id=1, source_target_pairs={{0,1},{1,0},{2,3},{3,2},{4,5},{5,4},{6,7},{7,6},{8,9},{9,8},{10,11... | collective-permute-start | bytes 454664 | tf_op jit(solution)/shard_map/ppermute | solution.py:610
  15.0 4.0 %collective-permute-start.3 = (f32[296,128]{1,0:T(8,128)S(1)}, f32[296,128]{1,0:T(8,128)S(1)}, u32[]{:S(2)}, u32[]{:S(2)}) collective-permute-start(f32[296,128]{1,0:T(8,128)S(1)} %get-tuple-element.43.second_rows), channel_id=1, source_target_pairs={{1,2},{2,1},{3,4},{4,3},{5,6},{6,5},{7,8},{8,7},{9,10},{10,9},{11,... | collective-permute-start | bytes 454664 | tf_op jit(solution)/shard_map/ppermute | solution.py:610
  15.7 32.6 %copy-start.5 = (s32[4608]{0:T(1024)S(1)}, s32[4608]{0:T(1024)}, u32[]{:S(2)}) copy-start(s32[4608]{0:T(1024)} %param.24) | copy-start | bytes 55300
  15.7 32.6 %copy-start.6 = (f32[4608]{0:T(1024)S(1)}, f32[4608]{0:T(1024)}, u32[]{:S(2)}) copy-start(f32[4608]{0:T(1024)} %param.25) | copy-start | bytes 55300
  62.3 13.6 %all-to-all-start.2 = ((f32[32,1,1280]{2,1,0:T(1,128)}), f32[32,1,1280]{2,1,0:T(1,128)S(1)}, u32[]{:S(2)}, u32[]{:S(2)}) async-start(f32[32,1,1280]{2,1,0:T(1,128)} %bitcast.4), calls=%async_computation.2 | async-start | bytes 327680 | tf_op jit(solution)/shard_map/all_to_all | solution.py:766
